TPU v7x, 32 devices: a whole 2x2x4 slice. The times are simulated.
32 devices in a mesh: gene: 8 (over z, x), cell: 4 (over y, core).
Axes of the slice: x: 2, y: 2, z: 4, core: 2. Of those that a mesh axis runs over, the one named last changes fastest.
Arguments:
- counts: int32 [16384, 20000], P('cell', 'gene'), may hold values from 0 to 63, as said below
- batch_index: int32 [16384], P('cell'), may hold values from 0 to 31
- valid_mask: int32 [16384], P('cell'), may hold values from 0 to 1, as said below
- noise_draw: float32 [16384, 10], P('cell'), may hold values from -5 to 5
- encoder_weight: float32 [20000, 128], P('gene'), may hold values from -0.0390625 to 0.0390625
- output_weight: float32 [2, 128, 20000], P(None, None, 'gene'), may hold values from -0.5 to 0.5
- gene_vectors: float32 [3, 20000], P(None, 'gene'), may hold values from -3 to 3
- batch_shift: float32 [32, 128], replicated, may hold values from -3 to 3
- layer_norm_params: float32 [4, 128], replicated, may hold values from 0.1 to 1.9
- head_weight: float32 [128, 20], replicated, may hold values from -0.5 to 0.5
- head_bias: float32 [20], replicated, may hold values from -1.5 to 1.5
- decoder_input: float32 [42, 128], replicated, may hold values from -2 to 2
- encoder_weight_momentum: float32 [20000, 128], P('gene'), may hold values from -0.00036621094 to 0.00036621094
- output_weight_momentum: float32 [2, 128, 20000], P(None, None, 'gene'), may hold values from -0.0029296875 to 0.0029296875
- gene_vectors_momentum: float32 [3, 20000], P(None, 'gene'), may hold values from -0.0014648438 to 0.0014648438
- batch_shift_momentum: float32 [32, 128], replicated, may hold values from -3.8146973e-05 to 3.8146973e-05
- norm_params_momentum: float32 [4, 128], replicated, may hold values from -0.00021362305 to 0.00021362305
- head_weight_momentum: float32 [128, 20], replicated, may hold values from -0.00012207031 to 0.00012207031
- head_bias_momentum: float32 [20], replicated, may hold values from -0.00021362305 to 0.00021362305
- decoder_input_momentum: float32 [42, 128], replicated, may hold values from -0.00021362305 to 0.00021362305
- encoder_weight_average: float32 [20000, 128], P('gene'), may hold values from -0.0390625 to 0.0390625
- output_weight_average: float32 [2, 128, 20000], P(None, None, 'gene'), may hold values from -0.5 to 0.5
- gene_vectors_average: float32 [3, 20000], P(None, 'gene'), may hold values from -3 to 3
- batch_shift_average: float32 [32, 128], replicated, may hold values from -3 to 3
- norm_params_average: float32 [4, 128], replicated, may hold values from 0.1 to 1.9
- head_weight_average: float32 [128, 20], replicated, may hold values from -0.5 to 0.5
- head_bias_average: float32 [20], replicated, may hold values from -1.5 to 1.5
- decoder_input_average: float32 [42, 128], replicated, may hold values from -2 to 2
Outputs:
- cell_loss: float32 [16384], P('cell')
- input_grad: float32 [16384, 20000], P('cell', 'gene')
- new_encoder_weight: float32 [20000, 128], P('gene')
- new_output_weight: float32 [2, 128, 20000], P(None, None, 'gene')
- new_gene_vectors: float32 [3, 20000], P(None, 'gene')
- new_batch_shift: float32 [32, 128], replicated
- new_norm_params: float32 [4, 128], replicated
- new_head_weight: float32 [128, 20], replicated
- new_head_bias: float32 [20], replicated
- new_decoder_input: float32 [42, 128], replicated
- new_encoder_weight_momentum: float32 [20000, 128], P('gene')
- new_output_weight_momentum: float32 [2, 128, 20000], P(None, None, 'gene')
- new_gene_vectors_momentum: float32 [3, 20000], P(None, 'gene')
- new_batch_shift_momentum: float32 [32, 128], replicated
- new_norm_params_momentum: float32 [4, 128], replicated
- new_head_weight_momentum: float32 [128, 20], replicated
- new_head_bias_momentum: float32 [20], replicated
- new_decoder_input_momentum: float32 [42, 128], replicated
- new_encoder_weight_average: float32 [20000, 128], P('gene')
- new_output_weight_average: float32 [2, 128, 20000], P(None, None, 'gene')
- new_gene_vectors_average: float32 [3, 20000], P(None, 'gene')
- new_batch_shift_average: float32 [32, 128], replicated
- new_norm_params_average: float32 [4, 128], replicated
- new_head_weight_average: float32 [128, 20], replicated
- new_head_bias_average: float32 [20], replicated
- new_decoder_input_average: float32 [42, 128], replicated
Inputs may be any that keep to these rules, and one draw needn't show every extreme that they name: `counts`: counts are whole numbers; about half of them are zero. `valid_mask`: each index of cell and each run of 4096 // 8 rows within it has its own share of real cells.
All inputs are finite; a program needn't handle non-finite values.
Results may differ from a plain program's by a relative error of at most 0.0022.
The roundings to bfloat16 on the way count: a program that leaves them out, or rounds other values in their place, can miss the bound.
Values may be sent and summed in bfloat16 or wider, within the bound.
A program may use at most 512 MiB of HBM per device.

v0:
```python
import jax
import jax.numpy as jnp
from jax import lax
from jax.sharding import PartitionSpec as P

momentum_decay = 0.9
average_decay = 0.99
norm_epsilon = 0.001
rate_epsilon = 1e-08
step_rates = (110.0, 46000.0, 300000.0, 70000.0, 13000.0, 3700.0, 7600.0, 8000.0)


def combined_all(part, axis, combine):
    gathered = jax.tree.map(lambda a: lax.all_gather(a, axis), part)

    def take(source):
        return jax.tree.map(lambda a: lax.dynamic_index_in_dim(a, source, 0, False), gathered)

    return lax.fori_loop(
        1, lax.axis_size(axis), lambda source, state: combine(state, take(source)), take(0)
    )


def negative_loglik(counted, rate, theta, dropout):
    softplus_pi = jax.nn.softplus(-dropout)
    log_theta = jnp.log(theta + rate_epsilon)
    log_both = jnp.log(theta + rate + rate_epsilon)
    pi_theta = -dropout + theta * (log_theta - log_both)
    zero_case = jax.nn.softplus(pi_theta) - softplus_pi
    other_case = (
        -softplus_pi
        + pi_theta
        + counted * (jnp.log(rate + rate_epsilon) - log_both)
        + lax.lgamma(counted + theta)
        - lax.lgamma(theta)
        - lax.lgamma(counted + 1.0)
    )
    return -jnp.where(counted < 0.5, zero_case, other_case)


def encode_hot(index, width):
    return (index[:, None] == jnp.arange(width)[None, :]).astype(jnp.float32)


def silu_slope(value):
    sigma = jax.nn.sigmoid(value)
    return sigma * (1.0 + value * (1.0 - sigma))


def nesterov(weight, momentum, average, grad, rate):
    moment = momentum_decay * momentum + grad
    fresh = weight - rate * (grad + momentum_decay * moment)
    return (fresh, moment, average_decay * average + (1.0 - average_decay) * fresh)


def local(
    counts,
    batch_index,
    valid_mask,
    noise_draw,
    encoder_weight,
    output_weight,
    gene_vectors,
    batch_shift,
    layer_norm_params,
    head_weight,
    head_bias,
    decoder_input,
    encoder_weight_momentum,
    output_weight_momentum,
    gene_vectors_momentum,
    batch_shift_momentum,
    norm_params_momentum,
    head_weight_momentum,
    head_bias_momentum,
    decoder_input_momentum,
    encoder_weight_average,
    output_weight_average,
    gene_vectors_average,
    batch_shift_average,
    norm_params_average,
    head_weight_average,
    head_bias_average,
    decoder_input_average,
):
    cells, genes_here = counts.shape
    groups = lax.axis_size("gene")
    genes_all = genes_here * groups
    slab = cells // groups
    first = lax.axis_index("gene") * slab
    latent_width = head_bias.shape[0] // 2
    batches = batch_shift.shape[0]
    highest = lax.Precision.HIGHEST
    counted = counts.astype(jnp.float32)
    inputs16 = jnp.log1p(counted).astype(jnp.bfloat16)
    weight16 = encoder_weight.astype(jnp.bfloat16)
    valid_all = valid_mask.astype(jnp.float32)
    encoded = lax.psum_scatter(
        jnp.dot(inputs16, weight16, preferred_element_type=jnp.float32),
        "gene",
        scatter_dimension=0,
        tiled=True,
    )
    rows_batch = lax.dynamic_slice_in_dim(batch_index, first, slab, 0)
    valid_row_mask = lax.dynamic_slice_in_dim(valid_all, first, slab, 0)
    rows_noise = lax.dynamic_slice_in_dim(noise_draw, first, slab, 0)
    row_weight_share = 1.0
    hot = encode_hot(rows_batch, batches)
    encoder_preactivation = encoded + jnp.dot(hot, batch_shift, precision=highest)
    sum1, square1, tally = lax.psum(
        (
            row_weight_share * jnp.sum(valid_row_mask[:, None] * encoder_preactivation, axis=0),
            row_weight_share
            * jnp.sum(
                valid_row_mask[:, None] * encoder_preactivation * encoder_preactivation, axis=0
            ),
            row_weight_share * jnp.sum(valid_row_mask),
        ),
        ("gene", "cell"),
    )
    valid_count = jnp.maximum(tally, 1.0)
    scale = 1.0 / (valid_count * genes_all)
    encoder_row_mean = sum1 / valid_count
    encoder_inverse_std = lax.rsqrt(
        square1 / valid_count - encoder_row_mean * encoder_row_mean + norm_epsilon
    )
    encoder_centered = (encoder_preactivation - encoder_row_mean) * encoder_inverse_std
    encoder_normed = encoder_centered * layer_norm_params[0] + layer_norm_params[1]
    hidden1 = jax.nn.silu(encoder_normed)

    def middle(hidden, weights, biases, mixing):
        heads = jnp.dot(hidden, weights, precision=highest) + biases
        mean_z = heads[:, :latent_width]
        log_var = heads[:, latent_width:]
        latent = mean_z + jnp.exp(0.5 * log_var) * rows_noise
        diverge = 0.5 * jnp.sum(mean_z * mean_z + jnp.exp(log_var) - log_var - 1.0, axis=1)
        pre = jnp.dot(jnp.concatenate([latent, hot], axis=1), mixing, precision=highest)
        return (pre, valid_row_mask * diverge)

    (decoder_preactivation, diverge_rows), middle_pull = jax.vjp(
        middle, hidden1, head_weight, head_bias, decoder_input
    )
    sum2, square2 = lax.psum(
        (
            row_weight_share * jnp.sum(valid_row_mask[:, None] * decoder_preactivation, axis=0),
            row_weight_share
            * jnp.sum(
                valid_row_mask[:, None] * decoder_preactivation * decoder_preactivation, axis=0
            ),
        ),
        ("gene", "cell"),
    )
    decoder_row_mean = sum2 / valid_count
    decoder_inverse_std = lax.rsqrt(
        square2 / valid_count - decoder_row_mean * decoder_row_mean + norm_epsilon
    )
    decoder_centered = (decoder_preactivation - decoder_row_mean) * decoder_inverse_std
    decoder_normed = decoder_centered * layer_norm_params[2] + layer_norm_params[3]
    hidden16 = jax.nn.silu(decoder_normed).astype(jnp.bfloat16)
    full16 = lax.all_gather(hidden16, "gene", axis=0, tiled=True)
    out16 = output_weight.astype(jnp.bfloat16)
    logits = (
        jnp.einsum("rh,khg->rkg", full16, out16, preferred_element_type=jnp.float32)
        + gene_vectors[None, :2, :]
    )
    local_top = jnp.max(logits[:, 0], axis=1)
    local_total = jnp.sum(jnp.exp(logits[:, 0] - local_top[:, None]), axis=1)

    def combine(left, right):
        upper = jnp.maximum(left[0], right[0])
        return (
            upper,
            left[1] * jnp.exp(left[0] - upper) + right[1] * jnp.exp(right[0] - upper),
            left[2] + right[2],
        )

    top, total, library = combined_all(
        (local_top, local_total, jnp.sum(counted, axis=1)), "gene", combine
    )

    def recon(values, log_theta, totals):
        fraction = jnp.exp(values[:, 0] - top[:, None]) / totals[:, None]
        rate = library[:, None] * fraction
        terms = negative_loglik(counted, rate, jnp.exp(log_theta)[None, :], values[:, 1])
        row_sums = jnp.sum(valid_all[:, None] * terms, axis=1)
        return (jnp.sum(row_sums), row_sums)

    recon_sum, recon_pull, row_sums = jax.vjp(recon, logits, gene_vectors[2], total, has_aux=True)
    grad_logits, grad_theta, grad_total = recon_pull(scale)
    row_share = row_sums + lax.dynamic_update_slice_in_dim(
        jnp.zeros((cells,), jnp.float32), diverge_rows, first, 0
    )
    total_back, row_loss = lax.psum((grad_total, row_share), "gene")
    cell_loss = row_loss / genes_all
    grad_logits = jnp.stack(
        [
            grad_logits[:, 0] + total_back[:, None] * jnp.exp(logits[:, 0] - top[:, None]),
            grad_logits[:, 1],
        ],
        axis=1,
    )
    grad16 = grad_logits.astype(jnp.bfloat16)
    grad_output = jnp.einsum("rh,rkg->khg", full16, grad16, preferred_element_type=jnp.float32)
    grad_genes = jnp.concatenate([jnp.sum(grad_logits, axis=0), grad_theta[None, :]], axis=0)
    grad_hidden2 = lax.psum_scatter(
        jnp.einsum(
            "rkg,khg->rh",
            lax.slice_in_dim(grad16, 0, slab * lax.axis_size("gene"), axis=0),
            out16,
            preferred_element_type=jnp.float32,
        ),
        "gene",
        scatter_dimension=0,
        tiled=True,
    )
    decoder_normed_gradient = grad_hidden2 * silu_slope(decoder_normed)
    decoder_gain_gradient, decoder_shift_gradient = lax.psum(
        (
            row_weight_share * jnp.sum(decoder_normed_gradient * decoder_centered, axis=0),
            row_weight_share * jnp.sum(decoder_normed_gradient, axis=0),
        ),
        ("gene", "cell"),
    )
    decoder_gain = layer_norm_params[2]
    grad_pre2 = decoder_inverse_std * (
        decoder_normed_gradient * decoder_gain
        - valid_row_mask[:, None]
        * (
            decoder_shift_gradient * decoder_gain
            + decoder_centered * decoder_gain_gradient * decoder_gain
        )
        / valid_count
    )
    grad_hidden1, grad_heads, grad_bias, grad_mixing = middle_pull(
        (grad_pre2, scale * jnp.ones_like(diverge_rows))
    )
    encoder_normed_gradient = grad_hidden1 * silu_slope(encoder_normed)
    encoder_gain_gradient, encoder_shift_gradient = lax.psum(
        (
            row_weight_share * jnp.sum(encoder_normed_gradient * encoder_centered, axis=0),
            row_weight_share * jnp.sum(encoder_normed_gradient, axis=0),
        ),
        ("gene", "cell"),
    )
    encoder_gain = layer_norm_params[0]
    grad_pre1 = encoder_inverse_std * (
        encoder_normed_gradient * encoder_gain
        - valid_row_mask[:, None]
        * (
            encoder_shift_gradient * encoder_gain
            + encoder_centered * encoder_gain_gradient * encoder_gain
        )
        / valid_count
    )
    grad_shift = lax.dot_general(hot, grad_pre1, (((0,), (0,)), ((), ())), precision=highest)
    grad_pre16 = grad_pre1.astype(jnp.bfloat16)
    grad_full = lax.all_gather(grad_pre16, "gene", axis=0, tiled=True)
    grad_encoder = lax.dot_general(
        inputs16, grad_full, (((0,), (0,)), ((), ())), preferred_element_type=jnp.float32
    )
    input_grad = lax.dot_general(
        grad_full, weight16, (((1,), (1,)), ((), ())), preferred_element_type=jnp.float32
    )
    grad_shift, grad_heads, grad_bias, grad_mixing = lax.psum(
        (
            row_weight_share * grad_shift,
            row_weight_share * grad_heads,
            row_weight_share * grad_bias,
            row_weight_share * grad_mixing,
        ),
        ("gene", "cell"),
    )
    grad_norms = jnp.stack(
        [
            encoder_gain_gradient,
            encoder_shift_gradient,
            decoder_gain_gradient,
            decoder_shift_gradient,
        ]
    )
    grad_encoder, grad_output, grad_genes = lax.psum(
        (grad_encoder, grad_output, grad_genes), "cell"
    )
    new_encoder_weight, new_encoder_weight_momentum, new_encoder_weight_average = nesterov(
        encoder_weight, encoder_weight_momentum, encoder_weight_average, grad_encoder, step_rates[0]
    )
    new_output_weight, new_output_weight_momentum, new_output_weight_average = nesterov(
        output_weight, output_weight_momentum, output_weight_average, grad_output, step_rates[1]
    )
    new_gene_vectors, new_gene_vectors_momentum, new_gene_vectors_average = nesterov(
        gene_vectors, gene_vectors_momentum, gene_vectors_average, grad_genes, step_rates[2]
    )
    new_batch_shift, new_batch_shift_momentum, new_batch_shift_average = nesterov(
        batch_shift, batch_shift_momentum, batch_shift_average, grad_shift, step_rates[3]
    )
    new_norm_params, new_norm_params_momentum, new_norm_params_average = nesterov(
        layer_norm_params, norm_params_momentum, norm_params_average, grad_norms, step_rates[4]
    )
    new_head_weight, new_head_weight_momentum, new_head_weight_average = nesterov(
        head_weight, head_weight_momentum, head_weight_average, grad_heads, step_rates[5]
    )
    new_head_bias, new_head_bias_momentum, new_head_bias_average = nesterov(
        head_bias, head_bias_momentum, head_bias_average, grad_bias, step_rates[6]
    )
    new_decoder_input, new_decoder_input_momentum, new_decoder_input_average = nesterov(
        decoder_input, decoder_input_momentum, decoder_input_average, grad_mixing, step_rates[7]
    )
    return (
        cell_loss,
        input_grad,
        new_encoder_weight,
        new_output_weight,
        new_gene_vectors,
        new_batch_shift,
        new_norm_params,
        new_head_weight,
        new_head_bias,
        new_decoder_input,
        new_encoder_weight_momentum,
        new_output_weight_momentum,
        new_gene_vectors_momentum,
        new_batch_shift_momentum,
        new_norm_params_momentum,
        new_head_weight_momentum,
        new_head_bias_momentum,
        new_decoder_input_momentum,
        new_encoder_weight_average,
        new_output_weight_average,
        new_gene_vectors_average,
        new_batch_shift_average,
        new_norm_params_average,
        new_head_weight_average,
        new_head_bias_average,
        new_decoder_input_average,
    )


def solution(mesh):
    return jax.shard_map(
        local,
        mesh=mesh,
        in_specs=(
            P("cell", "gene"),
            P("cell"),
            P("cell"),
            P("cell", None),
            P("gene", None),
            P(None, None, "gene"),
            P(None, "gene"),
            P(),
            P(),
            P(),
            P(),
            P(),
            P("gene", None),
            P(None, None, "gene"),
            P(None, "gene"),
            P(),
            P(),
            P(),
            P(),
            P(),
            P("gene", None),
            P(None, None, "gene"),
            P(None, "gene"),
            P(),
            P(),
            P(),
            P(),
            P(),
        ),
        out_specs=(
            P("cell"),
            P("cell", "gene"),
            P("gene", None),
            P(None, None, "gene"),
            P(None, "gene"),
            P(),
            P(),
            P(),
            P(),
            P(),
            P("gene", None),
            P(None, None, "gene"),
            P(None, "gene"),
            P(),
            P(),
            P(),
            P(),
            P(),
            P("gene", None),
            P(None, None, "gene"),
            P(None, "gene"),
            P(),
            P(),
            P(),
            P(),
            P(),
        ),
        check_vma=False,
    )
```

profile of v0, /device:TPU:0, one launch (start us, length us, event | category | flops | bytes accessed | tf_op | source)
XLA Modules:
  0.0 1859.9 jit_solution(12767536583246724004)
XLA Ops:
  7.4 23.4 %fusion.38 = f32[4096,128]{1,0:T(8,128)} fusion(s32[4096,2500]{0,1:T(8,128)} %param.31, f32[2500,128]{1,0:T(8,128)} %param.35), kind=kOutput, calls=%fused_computation.87 | convolution fusion | flops 2642240000 | bytes 44337152 | tf_op jit(solution)/shard_map/dot_general | solution.py:99
  30.8 0.0 all-gather.6.cloned.1.call-start
  30.9 0.8 dynamic_slice.49
  31.6 0.7 fusion.96
  32.4 69.0 %reduce-scatter.3.cloned.1.call-done = f32[512,128]{1,0:T(8,128)} async-done(((f32[4096,128]{1,0:T(8,128)}), f32[512,128]{1,0:T(8,128)}) %reduce-scatter.3.cloned.1.call-update) | async-done | bytes 262160 | tf_op jit(solution)/shard_map/reduce_scatter | solution.py:98
  101.4 1.4 fusion.60
  102.7 39.8 %all-reduce.8 = (f32[128]{0:T(128)S(1)}, f32[]{:T(128)}, f32[128]{0:T(128)S(1)}) all-reduce(f32[128]{0:T(128)S(1)} %get-tuple-element.277, f32[]{:T(128)} %get-tuple-element.355, f32[128]{0:T(128)S(1)} %get-tuple-element.276), channel_id=1, replica_groups=mesh['gene'=8,'cell'=4] {'gene','cell'}, use_global_device_ids=true, to_apply=%region_2.0 | all-reduce | flops 257 | bytes 2056 | tf_op jit(solution)/shard_map/psum | solution.py:110
  143.3 0.5 copy-done.54
  143.8 0.4 convolution_add_fusion.1
  144.2 1.4 add_reduce_fusion
  145.6 0.6 fusion.61
  146.3 39.7 %all-reduce.7 = (f32[128]{0:T(128)S(1)}, f32[128]{0:T(128)S(1)}) all-reduce(f32[128]{0:T(128)S(1)} %get-tuple-element.275, f32[128]{0:T(128)S(1)} %get-tuple-element.274), channel_id=1, replica_groups=mesh['gene'=8,'cell'=4] {'gene','cell'}, use_global_device_ids=true, to_apply=%region_8.9 | all-reduce | flops 256 | bytes 2048 | tf_op jit(solution)/shard_map/psum | solution.py:143
  186.0 0.8 multiply_convert_fusion
  186.8 0.0 reduce-scatter.5.cloned.1.call-start
  186.9 14.7 convert_reduce_fusion
  201.6 31.1 %all-gather.2 = f32[32768]{0:T(1024)S(1)} all-gather(f32[4096]{0:T(1024)S(1)} %convert_reduce_fusion), channel_id=4, replica_groups=mesh['gene'=8,'cell'=4] {'gene'}, dimensions={0}, use_global_device_ids=true | all-gather | bytes 147456 | tf_op jit(solution)/shard_map/all_gather | solution.py:14
  232.8 2.1 convert_element_type.33
  235.0 1.7 fusion.91
  236.8 31.0 %broadcast_add_fusion = f32[4096,2,2500]{0,2,1:T(8,128)} fusion(f32[2,2500]{1,0:T(2,128)S(1)} %slice-done.1, bf16[2,128,2500]{1,0,2:T(2,128)(2,1)} %convert_element_type.33, bf16[4096,128]{1,0:T(8,128)(2,1)} %all-gather.6.cloned.1.call-done), kind=kOutput, calls=%fused_computation.71 | convolution fusion | flops 5263360000 | bytes 84268576 | tf_op jit(solution)/shard_map/rh,khg->rkg/dot_general | solution.py:163
  267.7 14.2 slice_reduce_fusion
  281.9 16.0 fusion.24
  297.9 30.5 %all-gather = f32[32768]{0:T(1024)S(1)} all-gather(f32[4096]{0:T(1024)S(1)} %slice_reduce_fusion), channel_id=2, replica_groups=mesh['gene'=8,'cell'=4] {'gene'}, dimensions={0}, use_global_device_ids=true | all-gather | bytes 147456 | tf_op jit(solution)/shard_map/all_gather | solution.py:14
  328.5 30.5 %all-gather.1 = f32[32768]{0:T(1024)S(1)} all-gather(f32[4096]{0:T(1024)S(1)} %fusion.24), channel_id=3, replica_groups=mesh['gene'=8,'cell'=4] {'gene'}, dimensions={0}, use_global_device_ids=true | all-gather | bytes 147456 | tf_op jit(solution)/shard_map/all_gather | solution.py:14
  359.0 0.9 while.19
  359.9 103.0 %fusion.6 = (f32[4096,1,2500]{0,2,1:T(8,128)}, f32[4096,2500]{0,1:T(8,128)}) fusion(f32[4096,2,2500]{0,2,1:T(8,128)} %broadcast_add_fusion, f32[4096]{0:T(1024)S(1)} %multiply_negate_fusion, s32[4096,2500]{0,1:T(8,128)} %param.31, f32[4096]{0:T(1024)S(1)} %get-tuple-element.210, f32[4096]{0:T(1024)S(1)} %get-tuple-element.209, ...), kind=kLoop, calls=%fused_computation.32 | loop fusion | flops 450560000 | bytes 204885536 | tf_op jit(solution)/shard_map/transpose(jvp())/broadcast_in_dim | solution.py:184
  463.0 70.7 %multiply_bitcast_fusion = (f32[4096,1,2500]{0,2,1:T(8,128)}, f32[4096,2500]{0,1:T(8,128)}) fusion(f32[4096,2,2500]{0,2,1:T(8,128)} %broadcast_add_fusion, f32[4096]{0:T(1024)S(1)} %get-tuple-element.210, f32[4096]{0:T(1024)S(1)} %get-tuple-element.209, f32[4096,2500]{0,1:T(8,128)} %get-tuple-element.347, f32[2500]{0:T(1024)S(1)} %get-tuple-element.282, ...), kind=kLoop, calls=%fused_computation.62 | loop fusion | flops 204800000 | bytes 204875536 | tf_op jit(solution)/shard_map/transpose(jvp())/broadcast_in_dim | solution.py:182
  533.7 856.0 %multiply_reduce_fusion = (f32[2500]{0:T(1024)S(1)}, f32[2500]{0:T(1024)S(1)}, f32[4096]{0:T(1024)S(1)}, f32[4096]{0:T(1024)S(1)}, f32[2500]{0:T(1024)S(1)}, /*index=5*/f32[2500]{0:T(1024)S(1)}, f32[2500]{0:T(1024)S(1)}) fusion(f32[4096,2500]{0,1:T(8,128)} %get-tuple-element.347, f32[2500]{0:T(1024)S(1)} %get-tuple-element.283, ...), kind=kLoop, calls=%fused_computation.60 | loop fusion | flops 2078699136 | bytes 205011072 | tf_op jit(solution)/shard_map/transpose(jvp())/reduce_sum | solution.py:28
  1389.7 0.2 fusion.95
  1389.9 37.2 %all-reduce.9 = (f32[4096]{0:T(1024)S(1)}, f32[4096]{0:T(1024)S(1)}) all-reduce(f32[4096]{0:T(1024)S(1)} %get-tuple-element.366, f32[4096]{0:T(1024)S(1)} %neg.76), channel_id=1, replica_groups=mesh['gene'=8,'cell'=4] {'gene'}, use_global_device_ids=true, to_apply=%region_18.20 | all-reduce | flops 8192 | bytes 65536 | tf_op jit(solution)/shard_map/psum | solution.py:193
  1427.1 66.0 %fusion.10 = (f32[4096,1,2500]{0,2,1:T(8,128)}, f32[4096,1,2500]{0,2,1:T(8,128)}) fusion(f32[4096,1,2500]{0,2,1:T(8,128)} %get-tuple-element.346, f32[4096,1,2500]{0,2,1:T(8,128)} %get-tuple-element.348, f32[4096,2,2500]{0,2,1:T(8,128)} %broadcast_add_fusion, f32[4096]{0:T(1024)S(1)} %get-tuple-element.209, f32[4096]{0:T(1024)S(1)} %get-tuple-element.313), kind=kLoop, calls=%fused_computation.36 | loop fusion | flops 51200000 | bytes 204832768 | tf_op jit(solution)/shard_map/add | solution.py:197
  1493.1 29.0 %fusion.44 = f32[4096,128]{1,0:T(8,128)} fusion(f32[4096,1,2500]{0,2,1:T(8,128)} %get-tuple-element.360, f32[4096,1,2500]{0,2,1:T(8,128)} %get-tuple-element.359, bf16[2,128,2500]{1,0,2:T(2,128)(2,1)S(1)} %copy-done.3), kind=kOutput, calls=%fused_computation.91 | convolution fusion | flops 5263360000 | bytes 85297152 | tf_op jit(solution)/shard_map/rkg,khg->rh/dot_general | solution.py:206
  1522.2 0.0 all-gather.8.cloned.1.call-start
  1522.2 26.1 %fusion = f32[2,2500]{1,0:T(2,128)S(1)} fusion(f32[4096,1,2500]{0,2,1:T(8,128)} %get-tuple-element.360, f32[4096,1,2500]{0,2,1:T(8,128)} %get-tuple-element.359), kind=kLoop, calls=%fused_computation.20 | loop fusion | flops 40955000 | bytes 81940000 | tf_op jit(solution)/shard_map/reduce_sum | solution.py:204
  1548.3 0.5 add_multiply_fusion.1
  1548.9 10.7 psum.139
  1559.6 0.6 broadcast_multiply_fusion
  1560.5 29.6 %fusion.47 = f32[2,128,2500]{1,2,0:T(8,128)} fusion(f32[4096,1,2500]{0,2,1:T(8,128)} %get-tuple-element.360, f32[4096,1,2500]{0,2,1:T(8,128)} %get-tuple-element.359, bf16[4096,128]{1,0:T(8,128)(2,1)S(1)} %copy-done.6), kind=kOutput, calls=%fused_computation.92 | convolution fusion | flops 5263360000 | bytes 85528576 | tf_op jit(solution)/shard_map/rh,rkg->khg/dot_general | solution.py:203
  1590.1 1.1 fusion.93
  1591.3 36.9 %all-reduce.6 = (f32[128]{0:T(128)S(1)}, f32[128]{0:T(128)S(1)}) all-reduce(f32[128]{0:T(128)S(1)} %get-tuple-element.281, f32[128]{0:T(128)S(1)} %get-tuple-element.280), channel_id=1, replica_groups=mesh['gene'=8,'cell'=4] {'gene','cell'}, use_global_device_ids=true, to_apply=%region_25.27 | all-reduce | flops 256 | bytes 2048 | tf_op jit(solution)/shard_map/psum | solution.py:217
  1628.2 0.1 subtract_multiply_fusion.1
  1628.4 1.1 multiply_add_fusion.9
  1629.6 0.6 fusion.92
  1630.2 41.8 %all-reduce.5 = (f32[128]{0:T(128)S(1)}, f32[128]{0:T(128)S(1)}) all-reduce(f32[128]{0:T(128)S(1)} %get-tuple-element.279, f32[128]{0:T(128)S(1)} %get-tuple-element.278), channel_id=1, replica_groups=mesh['gene'=8,'cell'=4] {'gene','cell'}, use_global_device_ids=true, to_apply=%region_29.31 | all-reduce | flops 256 | bytes 2048 | tf_op jit(solution)/shard_map/psum | solution.py:238
  1672.0 0.8 fusion.94
  1672.9 0.0 all-reduce.13.cloned.1.call-start
  1672.9 0.7 multiply_add_fusion.6
  1673.6 0.1 fusion.69
  1673.7 0.3 fusion.70
  1674.1 0.2 fusion.65
  1674.3 0.3 fusion.63
  1674.6 40.4 %all-reduce.4 = (f32[32,128]{1,0:T(8,128)S(1)}, f32[128,20]{0,1:T(8,128)S(1)}, f32[20]{0:T(128)S(1)}, f32[42,128]{1,0:T(8,128)S(1)}) all-reduce(f32[32,128]{1,0:T(8,128)S(1)} %fusion.65, f32[128,20]{0,1:T(8,128)S(1)} %fusion.70, f32[20]{0:T(128)S(1)} %fusion.69, ...), channel_id=1, replica_groups=mesh['gene'=8,'cell'=4] {'gene','cell'}, use_global_device_ids=true, to_apply=%region_39.41 | all-reduce | flops 12052 | bytes 96416 | tf_op jit(solution)/shard_map/psum | solution.py:264
  1715.0 0.6 multiply_add_fusion.17
  1715.6 0.6 multiply_add_fusion.15
  1716.2 0.6 multiply_add_fusion.13
  1716.9 20.1 %fusion.50 = f32[2500,128]{1,0:T(8,128)} fusion(bf16[4096,128]{1,0:T(8,128)(2,1)} %all-gather.8.cloned.1.call-done, s32[4096,2500]{0,1:T(8,128)} %param.31), kind=kOutput, calls=%fused_computation.93 | convolution fusion | flops 2641920000 | bytes 43288576 | tf_op jit(solution)/shard_map/dot_general | solution.py:258
  1737.1 0.5 multiply_add_fusion.19
  1737.6 0.6 multiply_add_fusion.11
  1738.2 17.0 fusion.57
  1755.2 61.9 %all-reduce.13.cloned.1.call-done = (f32[2500,128]{1,0:T(8,128)}, f32[2,128,2500]{1,2,0:T(8,128)}) async-done(((f32[2500,128]{1,0:T(8,128)}, f32[2,128,2500]{1,2,0:T(8,128)}), (f32[2500,128]{1,0:T(8,128)}, f32[2,128,2500]{1,2,0:T(8,128)})) %all-reduce.13.cloned.1.call-update) | async-done | bytes 3840016 | tf_op jit(solution)/shard_map/psum | solution.py:281
  1817.1 5.0 fusion.51
  1822.2 9.0 copy.70
  1831.2 8.8 copy.68
  1840.0 8.8 copy.69
  1848.9 4.3 multiply_add_fusion.2
  (189 shorter events, 1.2 us)
Async XLA Ops:
  7.2 94.1 %copy-start.22 = (f32[32,128]{1,0:T(8,128)S(1)}, f32[32,128]{1,0:T(8,128)}, u32[]{:S(2)}) copy-start(f32[32,128]{1,0:T(8,128)} %param.38) | copy-start | bytes 49156
  7.2 136.5 %copy-start.37 = (f32[128,20]{0,1:T(8,128)S(1)}, f32[128,20]{0,1:T(8,128)}, u32[]{:S(2)}) copy-start(f32[128,20]{0,1:T(8,128)} %param.40) | copy-start | bytes 30724
  7.2 136.5 %copy-start.60 = (f32[20]{0:T(128)S(1)}, f32[20]{0:T(128)}, u32[]{:S(2)}) copy-start(f32[20]{0:T(128)} %param.41) | copy-start | bytes 244
  7.3 138.4 %copy-start.18 = (f32[42,128]{1,0:T(8,128)S(1)}, f32[42,128]{1,0:T(8,128)}, u32[]{:S(2)}) copy-start(f32[42,128]{1,0:T(8,128)} %param.42) | copy-start | bytes 64516
  7.3 227.7 %copy-start.10 = (f32[3,2500]{1,0:T(4,128)S(1)}, f32[3,2500]{1,0:T(4,128)}, u32[]{:S(2)}) copy-start(f32[3,2500]{1,0:T(4,128)} %param.37) | copy-start | bytes 90004
  7.3 229.5 %slice-start.1 = ((f32[3,2500]{1,0:T(4,128)}), f32[2,2500]{1,0:T(2,128)S(1)}, s32[]{:S(2)}) async-start(f32[3,2500]{1,0:T(4,128)} %param.37), calls=%async_computation.8 | async-start | bytes 40960 | tf_op jit(solution)/shard_map/slice | solution.py:164
  7.3 225.5 %copy-start.1 = (f32[2,128,2500]{1,0,2:T(2,128)S(1)}, f32[2,128,2500]{1,0,2:T(2,128)}, u32[]{:S(2)}) copy-start(f32[2,128,2500]{1,0,2:T(2,128)} %param.36) | copy-start | bytes 7680004
  7.3 94.1 %reduce-scatter.3.cloned.1.call-start = ((), (), s32[]{:S(2)}) async-start(), calls=%async_computation.2 | async-start | bytes 2359296 | tf_op jit(solution)/shard_map/reduce_scatter | solution.py:98
  30.8 206.0 %all-gather.6.cloned.1.call-start = ((), (), s32[]{:S(2)}) async-start(), calls=%async_computation.3 | async-start | bytes 1179648 | tf_op jit(solution)/shard_map/all_gather | solution.py:160
  30.8 112.4 %copy-start.32 = (f32[4096]{0:T(1024)}, f32[4096]{0:T(1024)S(1)}, u32[]{:S(2)}) copy-start(f32[4096]{0:T(1024)S(1)} %convert_element_type.27) | copy-start | bytes 49156
  31.6 155.2 %copy-start.28 = (s32[512]{0:T(512)}, s32[512]{0:T(512)S(1)}, u32[]{:S(2)}) copy-start(s32[512]{0:T(512)S(1)} %dynamic_slice.49) | copy-start | bytes 6148
  32.3 154.6 %copy-start.20 = (f32[512]{0:T(512)}, f32[512]{0:T(512)S(1)}, u32[]{:S(2)}) copy-start(f32[512]{0:T(512)S(1)} %get-tuple-element.356) | copy-start | bytes 6148
  32.3 200.5 %copy-start.45 = (f32[128]{0:T(128)}, f32[128]{0:T(128)S(1)}, u32[]{:S(2)}) copy-start(f32[128]{0:T(128)S(1)} %get-tuple-element.367) | copy-start | bytes 1540
  32.3 200.4 %copy-start.50 = (f32[128]{0:T(128)}, f32[128]{0:T(128)S(1)}, u32[]{:S(2)}) copy-start(f32[128]{0:T(128)S(1)} %get-tuple-element.370) | copy-start | bytes 1540
  32.3 200.4 %copy-start.56 = (f32[128]{0:T(128)}, f32[128]{0:T(128)S(1)}, u32[]{:S(2)}) copy-start(f32[128]{0:T(128)S(1)} %get-tuple-element.369) | copy-start | bytes 1540
  32.3 200.4 %copy-start.64 = (f32[128]{0:T(128)}, f32[128]{0:T(128)S(1)}, u32[]{:S(2)}) copy-start(f32[128]{0:T(128)S(1)} %get-tuple-element.368) | copy-start | bytes 1540
  32.4 154.5 %copy-start.12 = (f32[512,32]{0,1:T(8,128)}, f32[512,32]{0,1:T(8,128)S(1)}, u32[]{:S(2)}) copy-start(f32[512,32]{0,1:T(8,128)S(1)} %fusion.66) | copy-start | bytes 196612
  102.7 42.9 %copy-start.8 = (f32[512,128]{1,0:T(8,128)}, f32[512,128]{1,0:T(8,128)S(1)}, u32[]{:S(2)}) copy-start(f32[512,128]{1,0:T(8,128)S(1)} %get-tuple-element.371) | copy-start | bytes 786436
  143.3 89.5 %copy-start.52 = (f32[128]{0:T(128)}, f32[128]{0:T(128)S(1)}, u32[]{:S(2)}) copy-start(f32[128]{0:T(128)S(1)} %get-tuple-element.353) | copy-start | bytes 1540
  145.6 41.3 %copy-start.14 = (f32[512,10]{0,1:T(8,128)}, f32[512,10]{0,1:T(8,128)S(1)}, u32[]{:S(2)}) copy-start(f32[512,10]{0,1:T(8,128)S(1)} %get-tuple-element.365) | copy-start | bytes 61444
  146.2 121.5 %copy-start.4 = (f32[512,128]{1,0:T(8,128)}, f32[512,128]{1,0:T(8,128)S(1)}, u32[]{:S(2)}) copy-start(f32[512,128]{1,0:T(8,128)S(1)} %get-tuple-element.372) | copy-start | bytes 786436
  186.8 1403.3 %reduce-scatter.5.cloned.1.call-start = ((), (), s32[]{:S(2)}) async-start(), calls=%async_computation.4 | async-start | bytes 2359296 | tf_op jit(solution)/shard_map/reduce_scatter | solution.py:205
  232.8 34.9 %copy-start.7 = (f32[32768]{0:T(1024)}, f32[32768]{0:T(1024)S(1)}, u32[]{:S(2)}) copy-start(f32[32768]{0:T(1024)S(1)} %all-gather.2) | copy-start | bytes 393220
  281.9 77.1 %slice-start = ((f32[32768]{0:T(1024)}), f32[4096]{0:T(1024)S(1)}, s32[]{:S(2)}) async-start(f32[32768]{0:T(1024)} %copy-done.7), calls=%async_computation.7 | async-start | bytes 32768 | tf_op jit(solution)/shard_map/jit(dynamic_index_in_dim)/dynamic_slice | solution.py:17
  463.0 70.7 %copy-start.33 = (f32[4096]{0:T(1024)S(1)}, f32[4096]{0:T(1024)}, u32[]{:S(2)}) copy-start(f32[4096]{0:T(1024)} %copy-done.32) | copy-start | bytes 49156
  463.0 70.7 %copy-start.36 = (f32[2500]{0:T(1024)S(1)}, f32[2500]{0:T(1024)}, u32[]{:S(2)}) copy-start(f32[2500]{0:T(1024)} %get-tuple-element.284) | copy-start | bytes 30004
  533.7 856.0 %copy-start.21 = (f32[512]{0:T(512)S(1)}, f32[512]{0:T(512)}, u32[]{:S(2)}) copy-start(f32[512]{0:T(512)} %copy-done.20) | copy-start | bytes 6148
  533.7 856.0 %copy-start.47 = (f32[512]{0:T(512)S(1)}, f32[512]{0:T(512)}, u32[]{:S(2)}) copy-start(f32[512]{0:T(512)} %get-tuple-element.364) | copy-start | bytes 6148
  1427.1 66.0 %copy-start.3 = (bf16[2,128,2500]{1,0,2:T(2,128)(2,1)S(1)}, bf16[2,128,2500]{1,0,2:T(2,128)(2,1)}, u32[]{:S(2)}) copy-start(bf16[2,128,2500]{1,0,2:T(2,128)(2,1)} %convert_element_type.33) | copy-start | bytes 3840004
  1522.2 38.1 %copy-start.6 = (bf16[4096,128]{1,0:T(8,128)(2,1)S(1)}, bf16[4096,128]{1,0:T(8,128)(2,1)}, u32[]{:S(2)}) copy-start(bf16[4096,128]{1,0:T(8,128)(2,1)} %all-gather.6.cloned.1.call-done) | copy-start | bytes 3145732
  1522.2 194.7 %all-gather.8.cloned.1.call-start = ((), (), s32[]{:S(2)}) async-start(), calls=%async_computation.5 | async-start | bytes 1179648 | tf_op jit(solution)/shard_map/all_gather | solution.py:257
  1560.2 29.9 %copy-start.5 = (f32[512,128]{1,0:T(8,128)S(1)}, f32[512,128]{1,0:T(8,128)}, u32[]{:S(2)}) copy-start(f32[512,128]{1,0:T(8,128)} %copy-done.4) | copy-start | bytes 786436
  1560.2 29.9 %copy-start.42 = (f32[128]{0:T(128)S(1)}, f32[128]{0:T(128)}, u32[]{:S(2)}) copy-start(f32[128]{0:T(128)} %copy-done.41) | copy-start | bytes 1540
  1560.2 29.9 %copy-start.44 = (f32[128]{0:T(128)S(1)}, f32[128]{0:T(128)}, u32[]{:S(2)}) copy-start(f32[128]{0:T(128)} %copy-done.43) | copy-start | bytes 1540
  1560.2 29.9 %copy-start.46 = (f32[128]{0:T(128)S(1)}, f32[128]{0:T(128)}, u32[]{:S(2)}) copy-start(f32[128]{0:T(128)} %copy-done.45) | copy-start | bytes 1540
  1560.3 29.9 %copy-start.51 = (f32[128]{0:T(128)S(1)}, f32[128]{0:T(128)}, u32[]{:S(2)}) copy-start(f32[128]{0:T(128)} %copy-done.50) | copy-start | bytes 1540
  1560.3 67.9 %copy-start.49 = (f32[4,128]{1,0:T(4,128)S(1)}, f32[4,128]{1,0:T(4,128)}, u32[]{:S(2)}) copy-start(f32[4,128]{1,0:T(4,128)} %param.39) | copy-start | bytes 6148
  1560.3 68.0 %copy-start.17 = (f32[512,20]{0,1:T(8,128)S(1)}, f32[512,20]{0,1:T(8,128)}, u32[]{:S(2)}) copy-start(f32[512,20]{0,1:T(8,128)} %copy-done.16) | copy-start | bytes 122884
  1560.3 68.0 %copy-start.19 = (f32[42,128]{1,0:T(8,128)S(1)}, f32[42,128]{1,0:T(8,128)}, u32[]{:S(2)}) copy-start(f32[42,128]{1,0:T(8,128)} %param.42) | copy-start | bytes 64516
  1560.3 69.2 %copy-start.9 = (f32[512,128]{1,0:T(8,128)S(1)}, f32[512,128]{1,0:T(8,128)}, u32[]{:S(2)}) copy-start(f32[512,128]{1,0:T(8,128)} %copy-done.8) | copy-start | bytes 786436
  1560.3 69.2 %copy-start.38 = (f32[128,20]{0,1:T(8,128)S(1)}, f32[128,20]{0,1:T(8,128)}, u32[]{:S(2)}) copy-start(f32[128,20]{0,1:T(8,128)} %param.40) | copy-start | bytes 30724
  1560.3 69.2 %copy-start.53 = (f32[128]{0:T(128)S(1)}, f32[128]{0:T(128)}, u32[]{:S(2)}) copy-start(f32[128]{0:T(128)} %copy-done.52) | copy-start | bytes 1540
  1560.3 69.2 %copy-start.55 = (f32[128]{0:T(128)S(1)}, f32[128]{0:T(128)}, u32[]{:S(2)}) copy-start(f32[128]{0:T(128)} %copy-done.54) | copy-start | bytes 1540
  1560.4 69.2 %copy-start.57 = (f32[128]{0:T(128)S(1)}, f32[128]{0:T(128)}, u32[]{:S(2)}) copy-start(f32[128]{0:T(128)} %copy-done.56) | copy-start | bytes 1540
  1560.4 69.2 %copy-start.65 = (f32[128]{0:T(128)S(1)}, f32[128]{0:T(128)}, u32[]{:S(2)}) copy-start(f32[128]{0:T(128)} %copy-done.64) | copy-start | bytes 1540
  1560.4 112.5 %copy-start.25 = (f32[3,2500]{1,0:T(4,128)S(1)}, f32[3,2500]{1,0:T(4,128)}, u32[]{:S(2)}) copy-start(f32[3,2500]{1,0:T(4,128)} %param.53) | copy-start | bytes 90004
  1560.4 112.5 %copy-start.26 = (f32[3,2500]{1,0:T(4,128)S(1)}, f32[3,2500]{1,0:T(4,128)}, u32[]{:S(2)}) copy-start(f32[3,2500]{1,0:T(4,128)} %param.45) | copy-start | bytes 90004
  1560.4 113.7 %copy-start.29 = (s32[512]{0:T(512)S(1)}, s32[512]{0:T(512)}, u32[]{:S(2)}) copy-start(s32[512]{0:T(512)} %copy-done.28) | copy-start | bytes 6148
  1560.4 113.9 %copy-start.13 = (f32[512,32]{0,1:T(8,128)S(1)}, f32[512,32]{0,1:T(8,128)}, u32[]{:S(2)}) copy-start(f32[512,32]{0,1:T(8,128)} %copy-done.12) | copy-start | bytes 196612
  1560.4 113.9 %copy-start.15 = (f32[512,10]{0,1:T(8,128)S(1)}, f32[512,10]{0,1:T(8,128)}, u32[]{:S(2)}) copy-start(f32[512,10]{0,1:T(8,128)} %copy-done.14) | copy-start | bytes 61444
  1560.4 154.5 %copy-start.58 = (f32[4,128]{1,0:T(4,128)S(1)}, f32[4,128]{1,0:T(4,128)}, u32[]{:S(2)}) copy-start(f32[4,128]{1,0:T(4,128)} %param.55) | copy-start | bytes 6148
  1560.5 154.5 %copy-start.59 = (f32[4,128]{1,0:T(4,128)S(1)}, f32[4,128]{1,0:T(4,128)}, u32[]{:S(2)}) copy-start(f32[4,128]{1,0:T(4,128)} %param.47) | copy-start | bytes 6148
  1560.5 155.1 %copy-start.39 = (f32[128,20]{0,1:T(8,128)S(1)}, f32[128,20]{0,1:T(8,128)}, u32[]{:S(2)}) copy-start(f32[128,20]{0,1:T(8,128)} %param.56) | copy-start | bytes 30724
  1560.5 155.1 %copy-start.40 = (f32[128,20]{0,1:T(8,128)S(1)}, f32[128,20]{0,1:T(8,128)}, u32[]{:S(2)}) copy-start(f32[128,20]{0,1:T(8,128)} %param.48) | copy-start | bytes 30724
  1560.5 155.7 %copy-start.23 = (f32[32,128]{1,0:T(8,128)S(1)}, f32[32,128]{1,0:T(8,128)}, u32[]{:S(2)}) copy-start(f32[32,128]{1,0:T(8,128)} %param.38) | copy-start | bytes 49156
  1560.5 155.7 %copy-start.34 = (f32[32,128]{1,0:T(8,128)S(1)}, f32[32,128]{1,0:T(8,128)}, u32[]{:S(2)}) copy-start(f32[32,128]{1,0:T(8,128)} %param.54) | copy-start | bytes 49156
  1560.5 155.7 %copy-start.35 = (f32[32,128]{1,0:T(8,128)S(1)}, f32[32,128]{1,0:T(8,128)}, u32[]{:S(2)}) copy-start(f32[32,128]{1,0:T(8,128)} %param.46) | copy-start | bytes 49156
  1628.3 108.7 %copy-start.61 = (f32[20]{0:T(128)S(1)}, f32[20]{0:T(128)}, u32[]{:S(2)}) copy-start(f32[20]{0:T(128)} %param.41) | copy-start | bytes 244
  1628.3 108.7 %copy-start.62 = (f32[20]{0:T(128)S(1)}, f32[20]{0:T(128)}, u32[]{:S(2)}) copy-start(f32[20]{0:T(128)} %param.57) | copy-start | bytes 244
  1628.4 108.7 %copy-start.63 = (f32[20]{0:T(128)S(1)}, f32[20]{0:T(128)}, u32[]{:S(2)}) copy-start(f32[20]{0:T(128)} %param.49) | copy-start | bytes 244
  1628.4 109.2 %copy-start.30 = (f32[42,128]{1,0:T(8,128)S(1)}, f32[42,128]{1,0:T(8,128)}, u32[]{:S(2)}) copy-start(f32[42,128]{1,0:T(8,128)} %param.58) | copy-start | bytes 64516
  1628.4 109.2 %copy-start.31 = (f32[42,128]{1,0:T(8,128)S(1)}, f32[42,128]{1,0:T(8,128)}, u32[]{:S(2)}) copy-start(f32[42,128]{1,0:T(8,128)} %param.50) | copy-start | bytes 64516
  1629.5 108.7 %copy-start = (f32[2500,128]{1,0:T(8,128)S(1)}, f32[2500,128]{1,0:T(8,128)}, u32[]{:S(2)}) copy-start(f32[2500,128]{1,0:T(8,128)} %param.35) | copy-start | bytes 3840004
  1672.9 144.3 %all-reduce.13.cloned.1.call-start = ((), (), s32[]{:S(2)}) async-start(), calls=%async_computation.6 | async-start | bytes 7692288 | tf_op jit(solution)/shard_map/psum | solution.py:281
  (9 other events, 126.1 us)
Sparse Core Ops, SparseCore 0:
  30.9 70.4 reduce-scatter.2
  186.9 40.4 all-gather.5
  1522.3 64.0 reduce-scatter.4
  1673.0 40.2 all-gather.7
  1737.1 79.9 all-reduce.12
where the time goes:
time: 1870 us; the launch traced here: 1860 us
  other arithmetic  1190 us (64%)
  blocking collectives  339 us (18%)
  matrix products  155 us (8%)
  waiting for transfers between devices  131 us (7%)
  local copies, waits for them, and re-layouts  28.7 us (2%)
    reduce_sum x1, other arithmetic, negative_loglik(): pi_theta = -dropout + theta * (log_theta - log_both)  856 us
    broadcast_in_dim x1, other arithmetic, recon(): values[:, 1]  103 us
    all_gather x3, blocking collectives, combined_all(): gathered = jax.tree.map(lambda a: lax.all_gather(a, axis), part)  92.2 us
    broadcast_in_dim x1, other arithmetic, recon(): fraction = jnp.exp(values[:, 0] - top[:, None]) / totals[:, None]  70.7 us
    reduce_scatter x1, waiting for transfers between devices, local(): lax.psum_scatter(jnp.dot(inputs16, weight16, preferred_element_type=jnp.f...  69 us
    add x1, other arithmetic, local(): grad_logits[:, 0]  66 us
    psum x1, waiting for transfers between devices, local(): lax.psum((grad_encoder, grad_output, grad_genes), 'cell')  61.9 us
    psum x1, blocking collectives, local(): lax.psum((row_weight_share * jnp.sum(encoder_normed_gradient * encoder_ce...  41.8 us
  transfers between devices with their start and end apart: 5, of which 2 were waited for; matrix products, arithmetic and copies ran while one was open for 5% of the time, Pallas kernels for 0%

commit v1 on v0

v1 whole, which is shorter than its diff:
```python
import functools

import jax
import jax.numpy as jnp
from jax import lax
from jax.experimental import pallas as pl
from jax.experimental.pallas import tpu as pltpu
from jax.sharding import PartitionSpec as P

momentum_decay = 0.9
average_decay = 0.99
norm_epsilon = 0.001
rate_epsilon = 1e-08
step_rates = (110.0, 46000.0, 300000.0, 70000.0, 13000.0, 3700.0, 7600.0, 8000.0)
ln2 = 0.6931471805599453
f32 = jnp.float32
bf16 = jnp.bfloat16
LANES = 128
ROWS = 16
HOT_DEPTH = 144
PARAMS = pltpu.CompilerParams(vmem_limit_bytes=60 << 20)


def silu_slope(value):
    sigma = jax.nn.sigmoid(value)
    return sigma * (1.0 + value * (1.0 - sigma))


def nesterov(weight, momentum, average, grad, rate):
    moment = momentum_decay * momentum + grad
    fresh = weight - rate * (grad + momentum_decay * moment)
    return (fresh, moment, average_decay * average + (1.0 - average_decay) * fresh)


def three_parts(value):
    high = lax.reduce_precision(value, 8, 7)
    rest = value - high
    middle = lax.reduce_precision(rest, 8, 7)
    return high, middle, lax.reduce_precision(rest - middle, 8, 7)


def whole(array):
    return pl.BlockSpec(array.shape, lambda i: (0,) * array.ndim)


def column_blocks(rows, chunk):
    return pl.BlockSpec((rows, chunk), lambda i: (0, i))


def split_rows(genes):
    full = genes // ROWS
    groups = max(d for d in range(1, 14) if full % d == 0)
    return full, groups, genes - full * ROWS


def padded(genes):
    return -(-genes // ROWS) * ROWS


def pick_chunk(cells, most):
    chunk = LANES
    while chunk * 2 <= most and cells % (chunk * 2) == 0:
        chunk *= 2
    return chunk


def tail_rows(ref, start, stop, columns, dtype):
    piece = ref[start:stop, columns]
    filler = jnp.zeros((ROWS - (stop - start), piece.shape[1]), dtype)
    return jnp.concatenate([piece, filler], axis=0)


def encode_kernel(counts_ref, weight_ref, out_ref, library_ref, inputs_ref, *, genes, chunk):
    full, groups, tail = split_rows(genes)

    def group(counted, rows, total):
        inputs_ref[rows, :] = jnp.log(counted + 1.0).astype(bf16)
        return total + counted[:8] + counted[8:]

    def step(i, total):
        rows = pl.ds(pl.multiple_of(i * ROWS, ROWS), ROWS)
        return group(counts_ref[rows, :].astype(f32), rows, total)

    total = lax.fori_loop(0, full, step, jnp.zeros((8, chunk), f32), unroll=4)
    if tail:
        rows = pl.ds(full * ROWS, ROWS)
        counted = tail_rows(counts_ref, full * ROWS, genes, slice(None), jnp.int32).astype(f32)
        total = group(counted, rows, total)
    library_ref[...] = jnp.sum(total, axis=0, keepdims=True)
    out_ref[...] = jnp.dot(weight_ref[...], inputs_ref[...], preferred_element_type=f32)


def encode(counts_t, weight_t):
    genes, cells = counts_t.shape
    chunk = pick_chunk(cells, 512)
    width = weight_t.shape[0]
    return pl.pallas_call(
        functools.partial(encode_kernel, genes=genes, chunk=chunk),
        grid=(cells // chunk,),
        in_specs=[column_blocks(genes, chunk), whole(weight_t)],
        out_specs=[column_blocks(width, chunk), column_blocks(1, chunk)],
        out_shape=[
            jax.ShapeDtypeStruct((width, cells), f32),
            jax.ShapeDtypeStruct((1, cells), f32),
        ],
        scratch_shapes=[pltpu.VMEM((padded(genes), chunk), bf16)],
        compiler_params=PARAMS,
        name="encode",
    )(counts_t, weight_t)


def fill_hidden(long_ref, hidden_ref, top):
    width, chunk = hidden_ref.shape
    long_ref[0:width, :] = hidden_ref[...]
    index = lax.broadcasted_iota(jnp.int32, (HOT_DEPTH - width, chunk), 0)
    extra = jnp.where(index < 3, 1.0, 0.0)
    if top is not None:
        high = (-top).astype(bf16).astype(f32)
        middle = (-top - high).astype(bf16).astype(f32)
        low = (-top - high - middle).astype(bf16).astype(f32)
        extra = jnp.where(index == 3, high, extra)
        extra = jnp.where(index == 4, middle, extra)
        extra = jnp.where(index == 5, low, extra)
    long_ref[width:HOT_DEPTH, :] = extra.astype(bf16)


def totals_kernel(hidden_ref, weight_ref, top_ref, total_ref, long_ref, value_ref, *, genes, chunk):
    size = weight_ref.shape[0]
    fill_hidden(long_ref, hidden_ref, None)
    value_ref[...] = jnp.dot(weight_ref[...], long_ref[...], preferred_element_type=f32)
    count = size // ROWS

    def highest(i, best):
        part = value_ref[pl.ds(pl.multiple_of(i * ROWS, ROWS), ROWS), :]
        return jnp.maximum(best, jnp.maximum(part[:8], part[8:]))

    best = lax.fori_loop(0, count, highest, jnp.full((8, chunk), -jnp.inf, f32), unroll=4)
    top = jnp.max(best, axis=0, keepdims=True)

    def add(i, total):
        part = jnp.exp(value_ref[pl.ds(pl.multiple_of(i * ROWS, ROWS), ROWS), :] - top)
        return total + part[:8] + part[8:]

    total = lax.fori_loop(0, count, add, jnp.zeros((8, chunk), f32), unroll=4)
    top_ref[...] = top
    total_ref[...] = jnp.sum(total, axis=0, keepdims=True)


def totals(hidden, weight, genes):
    width, cells = hidden.shape
    chunk = pick_chunk(cells, 512)
    return pl.pallas_call(
        functools.partial(totals_kernel, genes=genes, chunk=chunk),
        grid=(cells // chunk,),
        in_specs=[column_blocks(width, chunk), whole(weight)],
        out_specs=[column_blocks(1, chunk)] * 2,
        out_shape=[jax.ShapeDtypeStruct((1, cells), f32)] * 2,
        scratch_shapes=[
            pltpu.VMEM((HOT_DEPTH, chunk), bf16),
            pltpu.VMEM((weight.shape[0], chunk), f32),
        ],
        compiler_params=PARAMS,
        name="totals",
    )(hidden, weight)


def likelihood_kernel(
    counts_ref,
    hidden_ref,
    top_ref,
    ratio_ref,
    share_ref,
    weight_ref,
    back_ref,
    theta_ref,
    log_ref,
    slope_ref,
    table_ref,
    slopes_ref,
    loss_ref,
    total_ref,
    grad_hidden_ref,
    grad_weight_ref,
    grad_bias_ref,
    grad_theta_ref,
    long_ref,
    value_ref,
    second_ref,
    *,
    genes,
    chunk,
):
    full, groups, tail = split_rows(genes)
    block = ROWS * groups
    width = hidden_ref.shape[0]

    @pl.when(pl.program_id(0) == 0)
    def _():
        for ref in (grad_weight_ref, grad_bias_ref, grad_theta_ref):
            ref[...] = jnp.zeros_like(ref)

    fill_hidden(long_ref, hidden_ref, top_ref[...])
    tiles = [slice(j, j + LANES) for j in range(0, chunk, LANES)]
    ratio_all = ratio_ref[...]
    share_all = share_ref[...]

    def group(held, rows, read, carry):
        losses, sums = [], []
        theta = theta_ref[rows, :]
        log_theta = log_ref[rows, :]
        log_slope = slope_ref[rows, :]
        table = table_ref[rows, :]
        grad_bias = grad_bias_ref[rows, :]
        grad_theta = grad_theta_ref[rows, :]
        for j, columns in enumerate(tiles):
            count = read(columns)
            counted = count.astype(f32)
            first = value_ref[0, held, columns]
            dropout = value_ref[1, held, columns]
            ratio, share = ratio_all[:, columns], share_all[:, columns]
            rate = jnp.exp(first) * ratio
            near = rate + rate_epsilon
            both = theta + near
            inverse = pl.reciprocal(near * both)
            inverse_both = inverse * near
            inverse_near = inverse * both
            log_fraction = jnp.log2(near * inverse_both)
            log_both = jnp.log2(both)
            pi_theta = (theta * ln2) * (log_theta - log_both) - dropout
            small_pi = jnp.exp(-jnp.abs(dropout))
            small_theta = jnp.exp(-jnp.abs(pi_theta))
            one_pi = 1.0 + small_pi
            one_theta = 1.0 + small_theta
            inverse_ones = pl.reciprocal(one_pi * one_theta)
            sigma_pi = jnp.where(dropout >= 0.0, small_pi, 1.0) * (inverse_ones * one_theta)
            inverse_theta = inverse_ones * one_pi
            zero = count < 1
            sigma_theta = jnp.where(pi_theta >= 0.0, 1.0, small_theta) * inverse_theta
            sigma = jnp.where(zero, sigma_theta, 1.0)
            log_ones = jnp.log2(one_pi * jnp.where(zero, inverse_theta, 1.0))
            upper = jnp.where(zero, jnp.maximum(pi_theta, 0.0), pi_theta)
            gammas = jnp.take_along_axis(table, count, axis=1)
            digammas = jnp.take_along_axis(table, count + LANES // 2, axis=1)
            loss = (jnp.maximum(-dropout, 0.0) - upper) + (
                ln2 * (log_ones - counted * log_fraction) - gammas
            )
            pull = (sigma * theta + counted) * inverse_both
            slope = rate * (pull - counted * inverse_near)
            slopes_ref[rows, columns] = slope
            grad_dropout = (sigma - sigma_pi) * share
            second_ref[rows, columns] = grad_dropout.astype(bf16)
            grad_bias = grad_bias + grad_dropout
            grad_theta = grad_theta + share * (
                pull - ln2 * (sigma * (log_slope - log_both)) - digammas
            )
            losses.append(carry[0][j] + loss[:8] + loss[8:])
            sums.append(carry[1][j] + slope[:8] + slope[8:])
        grad_bias_ref[rows, :] = grad_bias
        grad_theta_ref[rows, :] = grad_theta
        return tuple(losses), tuple(sums)

    def logits(rows, size):
        for k in range(2):
            value_ref[k, 0:size, :] = jnp.dot(
                weight_ref[k, rows, :], long_ref[...], preferred_element_type=f32
            )

    def step(b, carry):
        start = pl.multiple_of(b * block, ROWS)
        logits(pl.ds(start, block), block)

        def inner(i, carry):
            held = pl.multiple_of(i * ROWS, ROWS)
            rows = pl.ds(pl.multiple_of(start + held, ROWS), ROWS)
            return group(pl.ds(held, ROWS), rows, lambda cols: counts_ref[rows, cols], carry)

        return lax.fori_loop(0, groups, inner, carry, unroll=4)

    zeros = tuple(jnp.zeros((8, LANES), f32) for _ in tiles)
    carry = lax.fori_loop(0, full // groups, step, (zeros, zeros))
    if tail:
        rows = pl.ds(full * ROWS, ROWS)
        logits(rows, ROWS)
        carry = group(
            pl.ds(0, ROWS),
            rows,
            lambda cols: tail_rows(counts_ref, full * ROWS, genes, cols, jnp.int32),
            carry,
        )
    for j, columns in enumerate(tiles):
        loss_ref[:, columns] = jnp.sum(carry[0][j], axis=0, keepdims=True)
        total_ref[:, columns] = jnp.sum(carry[1][j], axis=0, keepdims=True)
    grad_weight_ref[...] += lax.dot_general(
        second_ref[...], hidden_ref[...], (((1,), (1,)), ((), ())), preferred_element_type=f32
    )
    grad_hidden_ref[...] = jnp.dot(back_ref[...], second_ref[...], preferred_element_type=f32)


def likelihood(counts_t, hidden, top, ratio, share, weights, back, gene_tables):
    genes, cells = counts_t.shape
    size = weights.shape[1]
    width = hidden.shape[0]
    chunk = pick_chunk(cells, 512)
    groups = split_rows(genes)[1]
    row = column_blocks(1, chunk)
    per_gene = pl.BlockSpec((size, LANES), lambda i: (0, 0))
    return pl.pallas_call(
        functools.partial(likelihood_kernel, genes=genes, chunk=chunk),
        grid=(cells // chunk,),
        in_specs=[column_blocks(genes, chunk), column_blocks(width, chunk), row, row, row]
        + [whole(weights), whole(back)]
        + [whole(a) for a in gene_tables],
        out_specs=[column_blocks(size, chunk), row, row, column_blocks(width, chunk)]
        + [per_gene] * 3,
        out_shape=[
            jax.ShapeDtypeStruct((size, cells), f32),
            jax.ShapeDtypeStruct((1, cells), f32),
            jax.ShapeDtypeStruct((1, cells), f32),
            jax.ShapeDtypeStruct((width, cells), f32),
        ]
        + [jax.ShapeDtypeStruct((size, LANES), f32)] * 3,
        scratch_shapes=[
            pltpu.VMEM((HOT_DEPTH, chunk), bf16),
            pltpu.VMEM((2, ROWS * groups, chunk), f32),
            pltpu.VMEM((size, chunk), bf16),
        ],
        compiler_params=PARAMS,
        name="likelihood",
    )(counts_t, hidden, top, ratio, share, weights, back, *gene_tables)


def frequency_kernel(
    slopes_ref,
    hidden_ref,
    top_ref,
    pull_ref,
    share_ref,
    other_ref,
    weight_ref,
    back_ref,
    grad_hidden_ref,
    grad_weight_ref,
    grad_bias_ref,
    long_ref,
    value_ref,
    first_ref,
    *,
    chunk,
):
    size = weight_ref.shape[0]

    @pl.when(pl.program_id(0) == 0)
    def _():
        for ref in (grad_weight_ref, grad_bias_ref):
            ref[...] = jnp.zeros_like(ref)

    fill_hidden(long_ref, hidden_ref, top_ref[...])
    value_ref[...] = jnp.dot(weight_ref[...], long_ref[...], preferred_element_type=f32)
    tiles = [slice(j, j + LANES) for j in range(0, chunk, LANES)]
    pull_all = pull_ref[...]
    share_all = share_ref[...]

    def step(i, carry):
        rows = pl.ds(pl.multiple_of(i * ROWS, ROWS), ROWS)
        bias = grad_bias_ref[rows, :]
        for columns in tiles:
            grad = share_all[:, columns] * (
                slopes_ref[rows, columns] - jnp.exp(value_ref[rows, columns]) * pull_all[:, columns]
            )
            first_ref[rows, columns] = grad.astype(bf16)
            bias = bias + grad
        grad_bias_ref[rows, :] = bias
        return carry

    lax.fori_loop(0, size // ROWS, step, 0, unroll=2)
    grad_weight_ref[...] += lax.dot_general(
        first_ref[...], hidden_ref[...], (((1,), (1,)), ((), ())), preferred_element_type=f32
    )
    grad_hidden_ref[...] = other_ref[...] + jnp.dot(
        back_ref[...], first_ref[...], preferred_element_type=f32
    )


def frequency(slopes, hidden, top, pull, share, other, weight, back):
    size, cells = slopes.shape
    width = hidden.shape[0]
    chunk = pick_chunk(cells, 512)
    row = column_blocks(1, chunk)
    wide = column_blocks(width, chunk)
    per_gene = pl.BlockSpec((size, LANES), lambda i: (0, 0))
    return pl.pallas_call(
        functools.partial(frequency_kernel, chunk=chunk),
        grid=(cells // chunk,),
        in_specs=[column_blocks(size, chunk), wide, row, row, row, wide]
        + [whole(weight), whole(back)],
        out_specs=[wide, per_gene, per_gene],
        out_shape=[jax.ShapeDtypeStruct((width, cells), f32)]
        + [jax.ShapeDtypeStruct((size, LANES), f32)] * 2,
        scratch_shapes=[
            pltpu.VMEM((HOT_DEPTH, chunk), bf16),
            pltpu.VMEM((size, chunk), f32),
            pltpu.VMEM((size, chunk), bf16),
        ],
        compiler_params=PARAMS,
        name="frequency",
    )(slopes, hidden, top, pull, share, other, weight, back)


def encoder_back_kernel(counts_ref, grad_ref, weight_ref, input_ref, weight_grad_ref):
    inputs = jnp.log(counts_ref[...].astype(f32) + 1.0).astype(bf16)
    weight_grad_ref[...] = lax.dot_general(
        inputs, grad_ref[...], (((1,), (1,)), ((), ())), preferred_element_type=f32
    )
    input_ref[...] = jnp.dot(weight_ref[...], grad_ref[...], preferred_element_type=f32)


def encoder_back(counts_t, grad, weight16):
    genes, cells = counts_t.shape
    width = grad.shape[0]
    block = LANES
    return pl.pallas_call(
        encoder_back_kernel,
        grid=(pl.cdiv(genes, block),),
        in_specs=[
            pl.BlockSpec((block, cells), lambda i: (i, 0)),
            whole(grad),
            pl.BlockSpec((block, width), lambda i: (i, 0)),
        ],
        out_specs=[
            pl.BlockSpec((block, cells), lambda i: (i, 0)),
            pl.BlockSpec((block, width), lambda i: (i, 0)),
        ],
        out_shape=[
            jax.ShapeDtypeStruct((genes, cells), f32),
            jax.ShapeDtypeStruct((genes, width), f32),
        ],
        compiler_params=PARAMS,
        name="encoder_back",
    )(counts_t, grad, weight16)


def local(
    counts,
    batch_index,
    valid_mask,
    noise_draw,
    encoder_weight,
    output_weight,
    gene_vectors,
    batch_shift,
    layer_norm_params,
    head_weight,
    head_bias,
    decoder_input,
    encoder_weight_momentum,
    output_weight_momentum,
    gene_vectors_momentum,
    batch_shift_momentum,
    norm_params_momentum,
    head_weight_momentum,
    head_bias_momentum,
    decoder_input_momentum,
    encoder_weight_average,
    output_weight_average,
    gene_vectors_average,
    batch_shift_average,
    norm_params_average,
    head_weight_average,
    head_bias_average,
    decoder_input_average,
):
    cells, genes = counts.shape
    gene_devices = lax.axis_size("gene")
    genes_all = genes * gene_devices
    slab = cells // gene_devices
    first = lax.axis_index("gene") * slab
    latent = head_bias.shape[0] // 2
    batches = batch_shift.shape[0]
    size = padded(genes)
    gap = size - genes
    everyone = ("gene", "cell")
    dot = functools.partial(jnp.dot, precision=lax.Precision.HIGHEST)

    def dot_nt(left, right):
        return lax.dot_general(
            left, right, (((1,), (1,)), ((), ())), precision=lax.Precision.HIGHEST
        )

    def mine(array):
        return lax.dynamic_slice_in_dim(array, first, slab, 1)

    counts_t = counts.T
    weight16 = encoder_weight.astype(bf16)
    encoder_t = jnp.pad(weight16, ((0, gap), (0, 0))).T

    theta = jnp.pad(jnp.exp(gene_vectors[2]), (0, gap), constant_values=1.0)
    log_theta = jnp.log2(theta + rate_epsilon)

    def spread(column):
        return jnp.broadcast_to(column[:, None], (size, LANES))

    steps = jnp.arange(LANES // 2, dtype=f32)[None, :]
    column = theta[:, None]
    table = jnp.concatenate(
        [
            lax.lgamma(steps + column) - lax.lgamma(column) - lax.lgamma(steps + 1.0),
            lax.digamma(steps + column) - lax.digamma(column),
        ],
        axis=1,
    )
    gene_tables = (
        spread(theta),
        spread(log_theta),
        spread(log_theta + theta / (theta + rate_epsilon) / ln2),
        table,
    )
    genes_first = jnp.transpose(output_weight, (2, 0, 1))
    out16 = jnp.pad(genes_first.astype(bf16), ((0, gap), (0, 0), (0, 0)))
    bias = jnp.pad(gene_vectors[:2].T, ((0, gap), (0, 0)))
    off = (jnp.arange(size) >= genes)[:, None] & (jnp.arange(2) == 0)[None, :]
    bias = jnp.where(off, -1e30, bias)
    parts = jnp.stack(three_parts(bias), axis=2).astype(bf16)
    ones = jnp.broadcast_to((jnp.arange(2) == 0).astype(bf16)[None, :, None], (size, 2, 3))
    rest = jnp.zeros((size, 2, HOT_DEPTH - LANES - 6), bf16)
    weights = jnp.transpose(jnp.concatenate([out16, parts, ones, rest], axis=2), (1, 0, 2))
    backs = jnp.transpose(out16, (1, 2, 0))

    encoded, library = encode(counts_t, encoder_t)
    valid = valid_mask.astype(f32)[None, :]
    hot = (jnp.arange(batches)[:, None] == batch_index[None, :]).astype(f32)
    valid_mine, hot_mine, noise = mine(valid), mine(hot), mine(noise_draw.T)
    pre1 = lax.psum_scatter(encoded, "gene", scatter_dimension=1, tiled=True)
    pre1 = pre1 + dot(batch_shift.T, hot_mine)
    library = lax.psum(library, "gene")
    sum1, square1, tally = lax.psum(
        (
            jnp.sum(valid_mine * pre1, axis=1),
            jnp.sum(valid_mine * pre1 * pre1, axis=1),
            jnp.sum(valid_mine),
        ),
        everyone,
    )
    count = jnp.maximum(tally, 1.0)
    scale = 1.0 / (count * genes_all)
    norms = layer_norm_params[:, :, None]
    mean1 = sum1 / count
    inverse1 = lax.rsqrt(square1 / count - mean1 * mean1 + norm_epsilon)[:, None]
    centered1 = (pre1 - mean1[:, None]) * inverse1
    normed1 = centered1 * norms[0] + norms[1]
    hidden1 = jax.nn.silu(normed1)
    heads = dot(head_weight.T, hidden1) + head_bias[:, None]
    mean_z, log_var = heads[:latent], heads[latent:]
    spread_z = jnp.exp(0.5 * log_var)
    sample = mean_z + spread_z * noise
    diverge = 0.5 * jnp.sum(
        mean_z * mean_z + jnp.exp(log_var) - log_var - 1.0, axis=0, keepdims=True
    )

    pre2_mine = dot(decoder_input.T, jnp.concatenate([sample, hot_mine], axis=0))
    sum2, square2 = lax.psum(
        (jnp.sum(valid_mine * pre2_mine, axis=1), jnp.sum(valid_mine * pre2_mine**2, axis=1)),
        everyone,
    )
    sample_all = lax.all_gather(sample, "gene", axis=1, tiled=True)
    mixed = jnp.concatenate([sample_all, hot], axis=0)
    mean2 = sum2 / count
    inverse2 = lax.rsqrt(square2 / count - mean2 * mean2 + norm_epsilon)[:, None]

    def normed_of(values):
        centered = (values - mean2[:, None]) * inverse2
        return centered, centered * norms[2] + norms[3]

    centered2, normed2 = normed_of(dot(decoder_input.T, mixed))
    hidden2 = jax.nn.silu(normed2).astype(bf16)

    top_here, total_here = totals(hidden2, weights[0], genes)
    tops = lax.all_gather(jnp.concatenate([top_here, total_here], axis=0), "gene")
    top = jnp.max(tops[:, 0], axis=0, keepdims=True)
    total = jnp.sum(tops[:, 1] * jnp.exp(tops[:, 0] - top), axis=0, keepdims=True)
    share = scale * valid
    slopes, loss, pull, grad_hidden2, grad_out1, grad_bias1, grad_theta = likelihood(
        counts_t, hidden2, top, library / total, share, weights, backs[1], gene_tables
    )
    pull, loss = lax.psum((pull, loss), "gene")
    diverge_all = lax.all_gather(diverge, "gene", axis=1, tiled=True)
    cell_loss = (valid * (loss + diverge_all) / genes_all)[0]
    grad_hidden2, grad_out0, grad_bias0 = frequency(
        slopes, hidden2, top, pull / total, share, grad_hidden2, weights[0], backs[0]
    )
    grad_genes = jnp.stack(
        [
            jnp.sum(grad_bias0, axis=1),
            jnp.sum(grad_bias1, axis=1),
            jnp.sum(grad_theta, axis=1) * theta,
        ]
    )[:, :genes]

    grad_normed2 = grad_hidden2 * silu_slope(normed2)
    gain2_grad, shift2_grad = lax.psum(
        (jnp.sum(grad_normed2 * centered2, axis=1), jnp.sum(grad_normed2, axis=1)), everyone
    )
    factor2 = inverse2 * norms[2]
    latent_rows = decoder_input[:latent]
    grad_sample = lax.psum_scatter(
        dot(latent_rows, factor2 * grad_normed2), "gene", scatter_dimension=1, tiled=True
    )
    centered2_mine, _ = normed_of(pre2_mine)
    grad_sample = grad_sample - valid_mine / count * dot(
        latent_rows,
        factor2 * (shift2_grad[:, None] + centered2_mine * gain2_grad[:, None]),
    )
    mixed_mine = valid_mine * jnp.concatenate([sample, hot_mine], axis=0)
    grad_mixing = factor2[:, 0] * (
        dot_nt(mixed, grad_normed2)
        - (
            jnp.sum(mixed_mine, axis=1, keepdims=True) * shift2_grad
            + dot_nt(mixed_mine, centered2_mine) * gain2_grad
        )
        / count
    )
    grad_mean = grad_sample + scale * valid_mine * mean_z
    grad_log = (
        grad_sample * noise * spread_z * 0.5
        + scale * valid_mine * (jnp.exp(log_var) - 1.0) * 0.5
    )
    grad_heads_out = jnp.concatenate([grad_mean, grad_log], axis=0)
    grad_heads = dot_nt(hidden1, grad_heads_out)
    grad_head_bias = jnp.sum(grad_heads_out, axis=1)
    grad_normed1 = dot(head_weight, grad_heads_out) * silu_slope(normed1)
    gain1_grad, shift1_grad = lax.psum(
        (jnp.sum(grad_normed1 * centered1, axis=1), jnp.sum(grad_normed1, axis=1)), everyone
    )
    grad_pre1 = (inverse1 * norms[0]) * (
        grad_normed1
        - valid_mine / count * (shift1_grad[:, None] + centered1 * gain1_grad[:, None])
    )
    grad_shift = dot_nt(hot_mine, grad_pre1)
    grad_pre16 = lax.all_gather(grad_pre1.astype(bf16), "gene", axis=1, tiled=True)
    input_grad, grad_encoder = encoder_back(counts_t, grad_pre16, weight16)
    grad_shift, grad_heads, grad_head_bias, grad_mixing = lax.psum(
        (grad_shift, grad_heads, grad_head_bias, grad_mixing), everyone
    )
    grad_norms = jnp.stack([gain1_grad, shift1_grad, gain2_grad, shift2_grad])
    grad_encoder, grad_out0, grad_out1, grad_genes = lax.psum(
        (grad_encoder, grad_out0[:genes], grad_out1[:genes], grad_genes), "cell"
    )
    grad_output = jnp.transpose(jnp.stack([grad_out0, grad_out1], axis=1), (1, 2, 0))
    weights_in = (
        encoder_weight,
        output_weight,
        gene_vectors,
        batch_shift,
        layer_norm_params,
        head_weight,
        head_bias,
        decoder_input,
    )
    momenta = (
        encoder_weight_momentum,
        output_weight_momentum,
        gene_vectors_momentum,
        batch_shift_momentum,
        norm_params_momentum,
        head_weight_momentum,
        head_bias_momentum,
        decoder_input_momentum,
    )
    averages = (
        encoder_weight_average,
        output_weight_average,
        gene_vectors_average,
        batch_shift_average,
        norm_params_average,
        head_weight_average,
        head_bias_average,
        decoder_input_average,
    )
    grads = (
        grad_encoder,
        grad_output,
        grad_genes,
        grad_shift,
        grad_norms,
        grad_heads,
        grad_head_bias,
        grad_mixing,
    )
    fresh, moments, means = zip(
        *[nesterov(*group) for group in zip(weights_in, momenta, averages, grads, step_rates)]
    )
    return (cell_loss, input_grad.T, *fresh, *moments, *means)


def solution(mesh):
    cells, genes = P("cell"), P("gene", None)
    weight_specs = (genes, P(None, None, "gene"), P(None, "gene"), P(), P(), P(), P(), P())
    return jax.shard_map(
        local,
        mesh=mesh,
        in_specs=(P("cell", "gene"), cells, cells, P("cell", None)) + weight_specs * 3,
        out_specs=(cells, P("cell", "gene")) + weight_specs * 3,
        check_vma=False,
    )
```

time: 1870 us -> 857 us (0.46)
  other arithmetic: 1190 us -> 52.8 us
  Pallas kernels: 0 us -> 287 us
  matrix products: 155 us -> 19 us
  waiting for transfers between devices: 131 us -> 51.3 us
  blocking collectives: 339 us -> 373 us
  local copies, waits for them, and re-layouts: 28.7 us -> 53.2 us
    reduce_sum x8, other arithmetic: 916 us -> 11.3 us  [the longest x1 3.85 us: local(): jnp.sum(grad_normed2, axis=1)]
    pallas_call x0 -> x5, Pallas kernels: none -> 287 us  [the longest x1 168 us: likelihood(): pl.pallas_call(functools.partial(likelihood_kernel, genes=genes, chunk=ch...]
    broadcast_in_dim x2 -> x0, other arithmetic: 174 us -> none  [the longest x1 103 us: recon(): values[:, 1]]
    dot_general x14 -> x11, matrix products: 155 us -> 19 us  [the longest x4 4.81 us: dot_nt(): lax.dot_general(left, right, (((1,), (1,)), ((), ())), precision=lax.Prec...]
    reduce_scatter x2, waiting for transfers between devices: 69 us -> 0.01 us  [the longest x1 0.01 us: local(): pre1 = lax.psum_scatter(encoded, 'gene', scatter_dimension=1, tiled=True)]
    add x15 -> x1, other arithmetic: 66.2 us -> 0.78 us  [local(): sample = mean_z + spread_z * noise]
    psum x7 -> x8, blocking collectives: 247 us -> 285 us  [the longest x1 41.5 us: local(): lax.psum((jnp.sum(grad_normed1 * centered1, axis=1), jnp.sum(grad_normed1...]
  transfers between devices with their start and end apart: 5 -> 4, of which waited for: 2 -> 1; matrix products, arithmetic and copies ran while one was open for 5% -> 7% of each run, Pallas kernels for 0% -> 0%
where the time goes in v1:
time: 857 us; the launch traced here: 852 us
  blocking collectives  373 us (44%)
  Pallas kernels  287 us (33%)
  local copies, waits for them, and re-layouts  53.2 us (6%)
  other arithmetic  52.8 us (6%)
  waiting for transfers between devices  51.3 us (6%)
  matrix products  19 us (2%)
  between operations  15.6 us (2%)
    pallas_call x1, Pallas kernels, likelihood(): pl.pallas_call(functools.partial(likelihood_kernel, genes=genes, chunk=ch...  168 us
    psum x1, waiting for transfers between devices, local(): lax.psum((grad_encoder, grad_out0[:genes], grad_out1[:genes], grad_genes)...  51.2 us
    psum x1, blocking collectives, local(): lax.psum((jnp.sum(grad_normed1 * centered1, axis=1), jnp.sum(grad_normed1...  41.5 us
    psum x1, blocking collectives, local(): lax.psum((grad_shift, grad_heads, grad_head_bias, grad_mixing), everyone)  41.3 us
    psum x1, blocking collectives, local(): library = lax.psum(library, 'gene')  39.5 us
    pallas_call x1, Pallas kernels, encoder_back(): pl.pallas_call(encoder_back_kernel, grid=(pl.cdiv(genes, block),), in_spe...  39.4 us
    psum x1, blocking collectives, local(): lax.psum((jnp.sum(valid_mine * pre2_mine, axis=1), jnp.sum(valid_mine * p...  39.3 us
    pallas_call x1, Pallas kernels, frequency(): pl.pallas_call(functools.partial(frequency_kernel, chunk=chunk), grid=(ce...  37.7 us
  transfers between devices with their start and end apart: 4, of which 1 were waited for; matrix products, arithmetic and copies ran while one was open for 7% of the time, Pallas kernels for 0%

profile of v1, /device:TPU:0, one launch (start us, length us, event | category | flops | bytes accessed | tf_op | source)
XLA Modules:
  0.0 852.4 jit_solution(17392147331433625246)
XLA Ops:
  7.2 1.4 convert_element_type.36.weight_ref
  8.7 1.1 copy.159.weight_ref
  9.8 20.6 %encode.1 = (f32[128,4096]{1,0:T(8,128)}, f32[1,4096]{1,0:T(1,128)}) custom-call(s32[2500,4096]{1,0:T(8,128)} %bitcast.110, bf16[128,2512]{1,0:T(8,128)(2,1)} %copy.159.weight_ref), custom_call_target="tpu_custom_call" | custom-call | tf_op jit(solution)/shard_map/encode/pallas_call | solution.py:97
  30.4 0.7 copy-done.17
  32.0 2.1 convert_element_type.39
  34.1 3.4 copy.162
  37.5 1.3 pad_bitcast_fusion.1
  38.9 5.3 concatenate.22
  44.2 2.6 copy.168.weight_ref
  46.8 0.8 iota_compare_fusion
  47.7 0.7 fusion.100
  48.4 1.6 copy.166.weight_ref
  50.0 39.5 %psum.145 = f32[1,4096]{1,0:T(1,128)S(1)} all-reduce(f32[1,4096]{1,0:T(1,128)S(1)} %copy-done.36), channel_id=1, replica_groups=mesh['gene'=8,'cell'=4] {'gene'}, use_global_device_ids=true, to_apply=%region_12.13 | all-reduce | flops 4096 | bytes 32768 | tf_op jit(solution)/shard_map/psum | solution.py:534
  89.6 14.9 %subtract_subtract_fusion = (f32[2512,64]{1,0:T(8,128)S(1)}, f32[2512,64]{1,0:T(8,128)S(1)}) fusion(f32[64]{0:T(128)S(1)} %copy-done.71, f32[2512]{0:T(1024)S(1)} %get-tuple-element.319, f32[2512]{0:T(1024)S(1)} %get-tuple-element.323, f32[2512]{0:T(1024)S(1)} %get-tuple-element.322), kind=kLoop, calls=%fused_computation.27 | loop fusion | flops 16076800 | bytes 1316544 | tf_op jit(solution)/shard_map/sub | solution.py:506
  104.5 1.5 pad_maximum_fusion.table_ref
  106.0 1.1 slice_bitcast_fusion.3
  107.1 1.4 fusion.35
  108.5 37.2 %all-reduce.8 = (f32[128]{0:T(128)S(1)}, f32[]{:T(128)}, f32[128]{0:T(128)S(1)}) all-reduce(f32[128]{0:T(128)S(1)} %get-tuple-element.245, f32[]{:T(128)} %get-tuple-element.300, f32[128]{0:T(128)S(1)} %get-tuple-element.244), channel_id=1, replica_groups=mesh['gene'=8,'cell'=4] {'gene','cell'}, use_global_device_ids=true, to_apply=%region_2.3 | all-reduce | flops 257 | bytes 2056 | tf_op jit(solution)/shard_map/psum | solution.py:535
  147.3 0.8 fusion.56
  148.1 30.9 %all_gather.15 = f32[10,4096]{1,0:T(8,128)S(1)} all-gather(f32[10,512]{1,0:T(8,128)S(1)} %fusion.56), channel_id=1, replica_groups=mesh['gene'=8,'cell'=4] {'gene'}, dimensions={1}, use_global_device_ids=true | all-gather | bytes 184320 | tf_op jit(solution)/shard_map/all_gather | solution.py:564
  179.0 1.3 multiply_reduce_fusion.3
  180.3 39.3 %all-reduce.7 = (f32[128]{0:T(128)S(1)}, f32[128]{0:T(128)S(1)}) all-reduce(f32[128]{0:T(128)S(1)} %get-tuple-element.243, f32[128]{0:T(128)S(1)} %get-tuple-element.242), channel_id=1, replica_groups=mesh['gene'=8,'cell'=4] {'gene','cell'}, use_global_device_ids=true, to_apply=%region_8.9 | all-reduce | flops 256 | bytes 2048 | tf_op jit(solution)/shard_map/psum | solution.py:560
  219.6 0.7 fusion.95
  220.3 4.1 multiply_convert_fusion
  224.5 21.6 %totals.1 = (f32[1,4096]{1,0:T(1,128)}, f32[1,4096]{1,0:T(1,128)}) custom-call(bf16[128,4096]{1,0:T(8,128)(2,1)} %get-tuple-element.332.hidden_ref, bf16[2512,144]{1,0:T(8,128)(2,1)} %copy.166.weight_ref), custom_call_target="tpu_custom_call" | custom-call | tf_op jit(solution)/shard_map/totals/pallas_call | solution.py:152
  246.1 0.8 maximum_bitcast_fusion.1
  246.9 30.7 %all-gather.2 = f32[8,2,4096]{2,1,0:T(2,128)S(1)} all-gather(f32[1,2,4096]{2,1,0:T(2,128)S(1)} %maximum_bitcast_fusion.1), channel_id=2, replica_groups=mesh['gene'=8,'cell'=4] {'gene'}, dimensions={0}, use_global_device_ids=true | all-gather | bytes 294912 | tf_op jit(solution)/shard_map/all_gather | solution.py:577
  278.7 0.6 div.72.ratio_ref
  279.3 1.4 broadcast_in_dim.26.theta_ref
  280.8 1.5 broadcast_in_dim.27.log_ref
  282.2 1.5 broadcast_in_dim.28.slope_ref
  283.7 168.2 %likelihood.1 = (f32[2512,4096]{1,0:T(8,128)}, f32[1,4096]{1,0:T(1,128)}, f32[1,4096]{1,0:T(1,128)}, f32[128,4096]{1,0:T(8,128)}, f32[2512,128]{1,0:T(8,128)}, /*index=5*/f32[2512,128]{1,0:T(8,128)}, f32[2512,128]{1,0:T(8,128)}) custom-call(s32[2500,4096]{1,0:T(8,128)} %bitcast.111, bf16[128,4096]{1,0:T(8,128)(2,1)} %get-tuple-element.332.hidden_ref, ...), custom_call_target="tpu_custom_call" | custom-call | tf_op jit(solution)/shard_map/likelihood/pallas_call | solution.py:307
  451.9 37.5 %all-reduce.9 = (f32[1,4096]{1,0:T(1,128)}, f32[1,4096]{1,0:T(1,128)S(1)}) all-reduce(f32[1,4096]{1,0:T(1,128)} %get-tuple-element.46, f32[1,4096]{1,0:T(1,128)} %get-tuple-element.48), channel_id=1, replica_groups=mesh['gene'=8,'cell'=4] {'gene'}, use_global_device_ids=true, to_apply=%region_14.15 | all-reduce | flops 8192 | bytes 65536 | tf_op jit(solution)/shard_map/psum | solution.py:584
  490.1 37.7 %frequency.1 = (f32[128,4096]{1,0:T(8,128)}, f32[2512,128]{1,0:T(8,128)}, f32[2512,128]{1,0:T(8,128)}) custom-call(f32[2512,4096]{1,0:T(8,128)} %get-tuple-element.47.slopes_ref, bf16[128,4096]{1,0:T(8,128)(2,1)} %get-tuple-element.332.hidden_ref, f32[1,4096]{1,0:T(1,128)} %bitcast.117, f32[1,4096]{1,0:T(1,128)} %div.78.pull_ref, f32[1,4096]{1,0:T(1,128)} %bitcast.119, ...), custom_call_target="tpu_custom_call" | custom-call | tf_op jit(solution)/shard_map/frequency/pallas_call | solution.py:391
  527.8 3.8 fusion.97
  531.7 2.7 convolution_bitcast_fusion
  534.5 1.7 reduce_sum.155
  536.2 1.7 reduce_sum.157
  538.0 1.7 reduce_sum.156
  539.8 11.8 %psum.155 = f32[3,2500]{1,0:T(4,128)} all-reduce(f32[3,2500]{1,0:T(4,128)S(1)} %pad_maximum_fusion.8), channel_id=1, replica_groups=mesh['gene'=8,'cell'=4] {'cell'}, use_global_device_ids=true, to_apply=%region_32.33 | all-reduce | flops 7500 | bytes 60000 | tf_op jit(solution)/shard_map/psum | solution.py:644
  551.6 2.5 slice_bitcast_fusion.1
  554.0 37.2 %all-reduce.6 = (f32[128]{0:T(128)}, f32[128]{0:T(128)}) all-reduce(f32[128]{0:T(128)} %get-tuple-element.241, f32[128]{0:T(128)} %get-tuple-element.240), channel_id=1, replica_groups=mesh['gene'=8,'cell'=4] {'gene','cell'}, use_global_device_ids=true, to_apply=%region_21.22 | all-reduce | flops 256 | bytes 2048 | tf_op jit(solution)/shard_map/psum | solution.py:599
  591.2 1.5 multiply_add_fusion.4
  592.7 1.3 multiply_reduce_fusion.5
  594.0 1.3 broadcast_multiply_fusion.1
  595.3 2.0 multiply_add_fusion.6
  598.0 2.4 fusion.98
  600.4 41.5 %all-reduce.5 = (f32[128]{0:T(128)S(1)}, f32[128]{0:T(128)}) all-reduce(f32[128]{0:T(128)} %get-tuple-element.247, f32[128]{0:T(128)} %get-tuple-element.246), channel_id=1, replica_groups=mesh['gene'=8,'cell'=4] {'gene','cell'}, use_global_device_ids=true, to_apply=%region_25.26 | all-reduce | flops 256 | bytes 2048 | tf_op jit(solution)/shard_map/psum | solution.py:630
  641.9 1.9 fusion.99
  644.1 1.2 fusion.33
  645.4 2.3 fusion.31
  647.7 1.1 slice_bitcast_fusion
  649.3 1.0 fusion.53
  650.3 41.3 %all-reduce.4 = (f32[32,128]{1,0:T(8,128)S(1)}, f32[128,20]{0,1:T(8,128)S(1)}, f32[20]{0:T(128)S(1)}, f32[42,128]{1,0:T(8,128)S(1)}) all-reduce(f32[32,128]{1,0:T(8,128)S(1)} %fusion.53, f32[128,20]{0,1:T(8,128)S(1)} %fusion.63, f32[20]{0:T(128)S(1)} %fusion.62, ...), channel_id=1, replica_groups=mesh['gene'=8,'cell'=4] {'gene','cell'}, use_global_device_ids=true, to_apply=%region_33.34 | all-reduce | flops 12052 | bytes 96416 | tf_op jit(solution)/shard_map/psum | solution.py:640
  691.6 39.4 %encoder_back.1 = (f32[2500,4096]{1,0:T(8,128)}, f32[2500,128]{1,0:T(8,128)}) custom-call(s32[2500,4096]{1,0:T(8,128)} %bitcast.112, bf16[128,4096]{1,0:T(8,128)(2,1)} %all-gather.6.cloned.1.call-done.grad_ref, bf16[2500,128]{1,0:T(8,128)(2,1)} %copy-done.2), custom_call_target="tpu_custom_call" | custom-call | tf_op jit(solution)/shard_map/encoder_back/pallas_call | solution.py:421
  732.2 26.0 %all-gather.3 = f32[8,1,512]{2,1,0:T(1,128)S(1)} all-gather(f32[1,1,512]{2,1,0:T(1,128)S(1)} %bitcast.125), channel_id=3, replica_groups=mesh['gene'=8,'cell'=4] {'gene'}, dimensions={0}, use_global_device_ids=true | all-gather | bytes 18432 | tf_op jit(solution)/shard_map/all_gather | solution.py:585
  760.1 0.6 multiply_add_fusion.7
  760.7 0.6 multiply_multiply_fusion.2
  761.4 51.2 %all-reduce.13.cloned.1.call-done = (f32[2500,128]{1,0:T(8,128)}, f32[2500,1,128]{2,0,1:T(8,128)}, f32[2500,1,128]{2,0,1:T(8,128)}) async-done(((f32[2500,128]{1,0:T(8,128)}, f32[2500,1,128]{2,0,1:T(8,128)}, f32[2500,1,128]{2,0,1:T(8,128)}), (f32[2500,128]{1,0:T(8,128)}, f32[2500,1,128]{2,0,1:T(8,128)}, f32[2500,1,128]{2,0,1:T(8,128)})) %all-reduce.13.cloned.1.call-update) | async-done | bytes 3840016 | tf_op jit(solution)/shard_map/psum | solution.py:644
  812.5 4.3 fusion.2
  816.8 8.9 %copy.174 = f32[2,128,2500]{1,0,2:T(2,128)} copy(f32[2,128,2500]{1,2,0:T(8,128)S(1)} %get-tuple-element.285) | data formatting | bytes 5120000
  825.7 8.8 %copy.175 = f32[2,128,2500]{1,0,2:T(2,128)} copy(f32[2,128,2500]{1,2,0:T(8,128)S(1)} %get-tuple-element.302) | data formatting | bytes 5120000
  834.5 8.9 %copy.176 = f32[2,128,2500]{1,0,2:T(2,128)} copy(f32[2,128,2500]{1,2,0:T(8,128)S(1)} %get-tuple-element.284) | data formatting | bytes 5120000
  843.4 2.3 multiply_add_fusion.1
  (191 shorter events, 8.5 us)
Async XLA Ops:
  7.2 99.9 %reduce-scatter.3.cloned.1.call-start = ((), (), s32[]{:S(2)}) async-start(), calls=%async_computation.2 | async-start | bytes 2359296 | tf_op jit(solution)/shard_map/reduce_scatter | solution.py:532
  9.8 22.2 %copy-start = (f32[2,128,2500]{1,0,2:T(2,128)S(1)}, f32[2,128,2500]{1,0,2:T(2,128)}, u32[]{:S(2)}) copy-start(f32[2,128,2500]{1,0,2:T(2,128)} %param.33) | copy-start | bytes 7680004
  30.4 564.9 %reduce-scatter.5.cloned.1.call-start = ((), (), s32[]{:S(2)}) async-start(), calls=%async_computation.3 | async-start | bytes 294912 | tf_op jit(solution)/shard_map/reduce_scatter | solution.py:604
  31.2 58.3 %copy-start.18 = (f32[2500]{0:T(1024)}, f32[2500]{0:T(1024)S(1)}, u32[]{:S(2)}) copy-start(f32[2500]{0:T(1024)S(1)} %exponential_reduce_fusion) | copy-start | bytes 30004
  44.2 3.4 copy-start.38
  46.8 3.2 copy-start.20
  46.8 3.2 copy-start.36
  47.7 59.5 %copy-start.12 = (pred[32,4096]{1,0:T(32,128)(4,1)}, pred[32,4096]{1,0:T(32,128)(4,1)S(1)}, u32[]{:S(2)}) copy-start(pred[32,4096]{1,0:T(32,128)(4,1)S(1)} %get-tuple-element.315) | copy-start | bytes 393220
  47.7 42.0 %copy-start.71 = (f32[64]{0:T(128)S(1)}, f32[64]{0:T(128)}, u32[]{:S(2)}) copy-start(f32[64]{0:T(128)} %compare_select_fusion.3) | copy-start | bytes 772
  47.7 99.2 %copy-start.67 = (f32[128]{0:T(128)}, f32[128]{0:T(128)S(1)}, u32[]{:S(2)}) copy-start(f32[128]{0:T(128)S(1)} %get-tuple-element.327) | copy-start | bytes 1540
  47.7 99.2 %copy-start.68 = (f32[128]{0:T(128)}, f32[128]{0:T(128)S(1)}, u32[]{:S(2)}) copy-start(f32[128]{0:T(128)S(1)} %get-tuple-element.328) | copy-start | bytes 1540
  47.7 172.6 %copy-start.60 = (f32[128]{0:T(128)}, f32[128]{0:T(128)S(1)}, u32[]{:S(2)}) copy-start(f32[128]{0:T(128)S(1)} %get-tuple-element.326) | copy-start | bytes 1540
  47.7 172.6 %copy-start.62 = (f32[128]{0:T(128)}, f32[128]{0:T(128)S(1)}, u32[]{:S(2)}) copy-start(f32[128]{0:T(128)S(1)} %get-tuple-element.329) | copy-start | bytes 1540
  48.4 130.6 %copy-start.26 = (f32[512]{0:T(512)}, f32[512]{0:T(512)S(1)}, u32[]{:S(2)}) copy-start(f32[512]{0:T(512)S(1)} %get-tuple-element.301) | copy-start | bytes 6148
  48.4 130.6 %copy-start.9 = (f32[32,512]{1,0:T(8,128)}, f32[32,512]{1,0:T(8,128)S(1)}, u32[]{:S(2)}) copy-start(f32[32,512]{1,0:T(8,128)S(1)} %constant_dynamic-slice_fusion) | copy-start | bytes 196612
  106.0 41.1 %copy-start.28 = (f32[128,20]{0,1:T(8,128)S(1)}, f32[128,20]{0,1:T(8,128)}, u32[]{:S(2)}) copy-start(f32[128,20]{0,1:T(8,128)} %param.37) | copy-start | bytes 30724
  106.0 41.1 %copy-start.50 = (f32[20]{0:T(128)S(1)}, f32[20]{0:T(128)}, u32[]{:S(2)}) copy-start(f32[20]{0:T(128)} %param.38) | copy-start | bytes 244
  107.1 71.9 %copy-start.30 = (f32[42,128]{1,0:T(8,128)S(1)}, f32[42,128]{1,0:T(8,128)}, u32[]{:S(2)}) copy-start(f32[42,128]{1,0:T(8,128)} %param.39) | copy-start | bytes 64516
  146.9 77.6 %copy-start.43 = (f32[128]{0:T(128)}, f32[128]{0:T(128)S(1)}, u32[]{:S(2)}) copy-start(f32[128]{0:T(128)S(1)} %get-tuple-element.292) | copy-start | bytes 1540
  146.9 77.6 %copy-start.45 = (f32[128]{0:T(128)}, f32[128]{0:T(128)S(1)}, u32[]{:S(2)}) copy-start(f32[128]{0:T(128)S(1)} %get-tuple-element.293) | copy-start | bytes 1540
  220.3 4.2 copy-start.53
  220.3 4.2 copy-start.55
  220.3 311.4 %copy-start.47 = (f32[128]{0:T(128)}, f32[128]{0:T(128)S(1)}, u32[]{:S(2)}) copy-start(f32[128]{0:T(128)S(1)} %get-tuple-element.295) | copy-start | bytes 1540
  224.5 53.4 %copy-start.25 = (s32[4096]{0:T(1024)S(1)}, s32[4096]{0:T(1024)}, u32[]{:S(2)}) copy-start(s32[4096]{0:T(1024)} %param.30) | copy-start | bytes 49156
  277.8 4.4 copy-start.11
  490.1 37.7 %copy-start.61 = (f32[128]{0:T(128)S(1)}, f32[128]{0:T(128)}, u32[]{:S(2)}) copy-start(f32[128]{0:T(128)} %copy-done.60) | copy-start | bytes 1540
  490.1 37.7 %copy-start.63 = (f32[128]{0:T(128)S(1)}, f32[128]{0:T(128)}, u32[]{:S(2)}) copy-start(f32[128]{0:T(128)} %copy-done.62) | copy-start | bytes 1540
  534.4 157.2 %all-gather.6.cloned.1.call-start = ((), (), s32[]{:S(2)}) async-start(), calls=%async_computation.4 | async-start | bytes 1179648 | tf_op jit(solution)/shard_map/all_gather | solution.py:638
  534.5 3.5 copy-start.19
  551.6 41.2 %copy-start.10 = (f32[32,512]{1,0:T(8,128)S(1)}, f32[32,512]{1,0:T(8,128)}, u32[]{:S(2)}) copy-start(f32[32,512]{1,0:T(8,128)} %copy-done.9) | copy-start | bytes 196612
  597.3 3.1 copy-start.15
  597.3 44.6 %copy-start.42 = (f32[512]{0:T(512)S(1)}, f32[512]{0:T(512)}, u32[]{:S(2)}) copy-start(f32[512]{0:T(512)} %get-tuple-element.325) | copy-start | bytes 6148
  597.3 44.6 %copy-start.44 = (f32[128]{0:T(128)S(1)}, f32[128]{0:T(128)}, u32[]{:S(2)}) copy-start(f32[128]{0:T(128)} %copy-done.43) | copy-start | bytes 1540
  597.3 44.6 %copy-start.46 = (f32[128]{0:T(128)S(1)}, f32[128]{0:T(128)}, u32[]{:S(2)}) copy-start(f32[128]{0:T(128)} %copy-done.45) | copy-start | bytes 1540
  597.3 44.6 %copy-start.52 = (f32[128]{0:T(128)S(1)}, f32[128]{0:T(128)}, u32[]{:S(2)}) copy-start(f32[128]{0:T(128)} %get-tuple-element.291) | copy-start | bytes 1540
  597.9 46.1 %copy-start.27 = (f32[512]{0:T(512)S(1)}, f32[512]{0:T(512)}, u32[]{:S(2)}) copy-start(f32[512]{0:T(512)} %copy-done.26) | copy-start | bytes 6148
  597.9 46.1 %copy-start.49 = (f32[42]{0:T(128)S(1)}, f32[42]{0:T(128)}, u32[]{:S(2)}) copy-start(f32[42]{0:T(128)} %multiply_reduce_fusion.5) | copy-start | bytes 508
  597.9 46.1 %copy-start.54 = (f32[128]{0:T(128)S(1)}, f32[128]{0:T(128)}, u32[]{:S(2)}) copy-start(f32[128]{0:T(128)} %copy-done.53) | copy-start | bytes 1540
  597.9 46.1 %copy-start.56 = (f32[128]{0:T(128)S(1)}, f32[128]{0:T(128)}, u32[]{:S(2)}) copy-start(f32[128]{0:T(128)} %copy-done.55) | copy-start | bytes 1540
  597.9 46.1 %copy-start.57 = (f32[128]{0:T(128)S(1)}, f32[128]{0:T(128)}, u32[]{:S(2)}) copy-start(f32[128]{0:T(128)} %get-tuple-element.254) | copy-start | bytes 1540
  598.0 46.1 %copy-start.58 = (f32[128]{0:T(128)S(1)}, f32[128]{0:T(128)}, u32[]{:S(2)}) copy-start(f32[128]{0:T(128)} %get-tuple-element.255) | copy-start | bytes 1540
  598.0 47.4 %copy-start.48 = (f32[128]{0:T(128)S(1)}, f32[128]{0:T(128)}, u32[]{:S(2)}) copy-start(f32[128]{0:T(128)} %copy-done.47) | copy-start | bytes 1540
  643.8 168.7 %all-reduce.13.cloned.1.call-start = ((), (), s32[]{:S(2)}) async-start(), calls=%async_computation.5 | async-start | bytes 7692288 | tf_op jit(solution)/shard_map/psum | solution.py:644
  647.7 43.9 %copy-start.66 = (f32[512]{0:T(512)S(1)}, f32[512]{0:T(512)}, u32[]{:S(2)}) copy-start(f32[512]{0:T(512)} %get-tuple-element.312) | copy-start | bytes 6148
  731.0 27.2 %copy-start.39 = (f32[4,128]{1,0:T(4,128)S(1)}, f32[4,128]{1,0:T(4,128)}, u32[]{:S(2)}) copy-start(f32[4,128]{1,0:T(4,128)} %param.36) | copy-start | bytes 6148
  731.0 27.2 %copy-start.59 = (f32[128]{0:T(128)S(1)}, f32[128]{0:T(128)}, u32[]{:S(2)}) copy-start(f32[128]{0:T(128)} %get-tuple-element.253) | copy-start | bytes 1540
  731.0 27.2 %copy-start.64 = (f32[4,128]{1,0:T(4,128)S(1)}, f32[4,128]{1,0:T(4,128)}, u32[]{:S(2)}) copy-start(f32[4,128]{1,0:T(4,128)} %param.52) | copy-start | bytes 6148
  731.0 27.2 %copy-start.65 = (f32[4,128]{1,0:T(4,128)S(1)}, f32[4,128]{1,0:T(4,128)}, u32[]{:S(2)}) copy-start(f32[4,128]{1,0:T(4,128)} %param.44) | copy-start | bytes 6148
  731.1 27.8 %copy-start.29 = (f32[128,20]{0,1:T(8,128)S(1)}, f32[128,20]{0,1:T(8,128)}, u32[]{:S(2)}) copy-start(f32[128,20]{0,1:T(8,128)} %param.37) | copy-start | bytes 30724
  731.1 27.7 %copy-start.40 = (f32[128,20]{0,1:T(8,128)S(1)}, f32[128,20]{0,1:T(8,128)}, u32[]{:S(2)}) copy-start(f32[128,20]{0,1:T(8,128)} %param.53) | copy-start | bytes 30724
  731.1 27.7 %copy-start.41 = (f32[128,20]{0,1:T(8,128)S(1)}, f32[128,20]{0,1:T(8,128)}, u32[]{:S(2)}) copy-start(f32[128,20]{0,1:T(8,128)} %param.45) | copy-start | bytes 30724
  731.1 28.3 %copy-start.23 = (f32[32,128]{1,0:T(8,128)S(1)}, f32[32,128]{1,0:T(8,128)}, u32[]{:S(2)}) copy-start(f32[32,128]{1,0:T(8,128)} %param.35) | copy-start | bytes 49156
  731.1 28.3 %copy-start.34 = (f32[32,128]{1,0:T(8,128)S(1)}, f32[32,128]{1,0:T(8,128)}, u32[]{:S(2)}) copy-start(f32[32,128]{1,0:T(8,128)} %param.51) | copy-start | bytes 49156
  731.1 28.3 %copy-start.35 = (f32[32,128]{1,0:T(8,128)S(1)}, f32[32,128]{1,0:T(8,128)}, u32[]{:S(2)}) copy-start(f32[32,128]{1,0:T(8,128)} %param.43) | copy-start | bytes 49156
  731.1 28.9 %copy-start.31 = (f32[42,128]{1,0:T(8,128)S(1)}, f32[42,128]{1,0:T(8,128)}, u32[]{:S(2)}) copy-start(f32[42,128]{1,0:T(8,128)} %param.39) | copy-start | bytes 64516
  731.1 28.9 %copy-start.32 = (f32[42,128]{1,0:T(8,128)S(1)}, f32[42,128]{1,0:T(8,128)}, u32[]{:S(2)}) copy-start(f32[42,128]{1,0:T(8,128)} %param.55) | copy-start | bytes 64516
  731.2 28.9 %copy-start.33 = (f32[42,128]{1,0:T(8,128)S(1)}, f32[42,128]{1,0:T(8,128)}, u32[]{:S(2)}) copy-start(f32[42,128]{1,0:T(8,128)} %param.47) | copy-start | bytes 64516
  731.2 29.5 %copy-start.21 = (f32[4096]{0:T(1024)S(1)}, f32[4096]{0:T(1024)}, u32[]{:S(2)}) copy-start(f32[4096]{0:T(1024)} %copy-done.20) | copy-start | bytes 49156
  731.2 29.5 %copy-start.37 = (f32[1,4096]{1,0:T(1,128)S(1)}, f32[1,4096]{1,0:T(1,128)}, u32[]{:S(2)}) copy-start(f32[1,4096]{1,0:T(1,128)} %get-tuple-element.261) | copy-start | bytes 49156
  731.2 81.4 %copy-start.1 = (f32[2,128,2500]{1,0,2:T(2,128)S(1)}, f32[2,128,2500]{1,0,2:T(2,128)}, u32[]{:S(2)}) copy-start(f32[2,128,2500]{1,0,2:T(2,128)} %param.33) | copy-start | bytes 7680004
  825.7 17.7 %copy-start.6 = (f32[2500,128]{1,0:T(8,128)S(1)}, f32[2500,128]{1,0:T(8,128)}, u32[]{:S(2)}) copy-start(f32[2500,128]{1,0:T(8,128)} %get-tuple-element.263) | copy-start | bytes 3840004
  834.5 8.9 %copy-start.3 = (f32[2500,128]{1,0:T(8,128)S(1)}, f32[2500,128]{1,0:T(8,128)}, u32[]{:S(2)}) copy-start(f32[2500,128]{1,0:T(8,128)} %param.32) | copy-start | bytes 3840004
  834.5 8.9 %copy-start.4 = (f32[2500,128]{1,0:T(8,128)S(1)}, f32[2500,128]{1,0:T(8,128)}, u32[]{:S(2)}) copy-start(f32[2500,128]{1,0:T(8,128)} %param.48) | copy-start | bytes 3840004
  834.5 8.9 %copy-start.5 = (f32[2500,128]{1,0:T(8,128)S(1)}, f32[2500,128]{1,0:T(8,128)}, u32[]{:S(2)}) copy-start(f32[2500,128]{1,0:T(8,128)} %param.40) | copy-start | bytes 3840004
  (12 other events, 14.6 us)
Sparse Core Ops, SparseCore 0:
  30.5 70.8 reduce-scatter.2
  534.5 57.6 reduce-scatter.4
  643.9 40.4 all-gather.5
  731.3 81.1 all-reduce.12

commit v2 on v1

--- a/solution.py
+++ b/solution.py
@@ -19,11 +19,14 @@
 ROWS = 16
 HOT_DEPTH = 144
 PARAMS = pltpu.CompilerParams(vmem_limit_bytes=60 << 20)
-
-
-def silu_slope(value):
-    sigma = jax.nn.sigmoid(value)
-    return sigma * (1.0 + value * (1.0 - sigma))
+IN_VMEM = pl.BlockSpec(memory_space=pltpu.VMEM)
+MESH = pl.DeviceIdType.MESH
+
+
+def talking(number):
+    return pltpu.CompilerParams(
+        collective_id=number, has_side_effects=True, vmem_limit_bytes=60 << 20
+    )
 
 
 def nesterov(weight, momentum, average, grad, rate):
@@ -70,7 +73,7 @@
     return jnp.concatenate([piece, filler], axis=0)
 
 
-def encode_kernel(counts_ref, weight_ref, out_ref, library_ref, inputs_ref, *, genes, chunk):
+def encode_kernel(counts_ref, weight_ref, out_ref, inputs_ref, *, genes, chunk):
     full, groups, tail = split_rows(genes)
 
     def group(counted, rows, total):
@@ -86,8 +89,11 @@
         rows = pl.ds(full * ROWS, ROWS)
         counted = tail_rows(counts_ref, full * ROWS, genes, slice(None), jnp.int32).astype(f32)
         total = group(counted, rows, total)
-    library_ref[...] = jnp.sum(total, axis=0, keepdims=True)
-    out_ref[...] = jnp.dot(weight_ref[...], inputs_ref[...], preferred_element_type=f32)
+    width = weight_ref.shape[0]
+    out_ref[0:width, :] = jnp.dot(weight_ref[...], inputs_ref[...], preferred_element_type=f32)
+    row = lax.broadcasted_iota(jnp.int32, (8, chunk), 0)
+    library = jnp.sum(total, axis=0, keepdims=True)
+    out_ref[width : width + 8, :] = jnp.where(row == 0, library, 0.0)
 
 
 def encode(counts_t, weight_t):
@@ -98,15 +104,518 @@
         functools.partial(encode_kernel, genes=genes, chunk=chunk),
         grid=(cells // chunk,),
         in_specs=[column_blocks(genes, chunk), whole(weight_t)],
-        out_specs=[column_blocks(width, chunk), column_blocks(1, chunk)],
-        out_shape=[
-            jax.ShapeDtypeStruct((width, cells), f32),
-            jax.ShapeDtypeStruct((1, cells), f32),
-        ],
+        out_specs=column_blocks(width + 8, chunk),
+        out_shape=jax.ShapeDtypeStruct((width + 8, cells), f32),
         scratch_shapes=[pltpu.VMEM((padded(genes), chunk), bf16)],
         compiler_params=PARAMS,
         name="encode",
     )(counts_t, weight_t)
+
+
+class Team:
+    def __init__(self, gene_only):
+        self.genes, self.cells = lax.axis_size("gene"), lax.axis_size("cell")
+        self.gene, self.cell = lax.axis_index("gene"), lax.axis_index("cell")
+        self.gene_only = gene_only
+        self.size = self.genes if gene_only else self.genes * self.cells
+        self.me = self.gene if gene_only else self.gene * self.cells + self.cell
+
+    def others(self, act):
+        def one(step, carry):
+            other = lax.rem(self.me + step, self.size)
+            if self.gene_only:
+                act(other, (other, self.cell))
+            else:
+                act(other, (other // self.cells, lax.rem(other, self.cells)))
+            return carry
+
+        lax.fori_loop(1, self.size, one, 0)
+
+    def greet(self):
+        barrier = pltpu.get_barrier_semaphore()
+
+        def act(other, place):
+            pl.semaphore_signal(barrier, inc=1, device_id=place, device_id_type=MESH)
+
+        self.others(act)
+        pl.semaphore_wait(barrier, self.size - 1)
+
+    def send(self, source, target, sems):
+        def act(other, place):
+            pltpu.make_async_remote_copy(
+                src_ref=source(other),
+                dst_ref=target,
+                send_sem=sems.at[0],
+                recv_sem=sems.at[1],
+                device_id=place,
+                device_id_type=MESH,
+            ).start()
+
+        self.others(act)
+
+
+def await_bytes(ref, sem):
+    pltpu.make_async_copy(ref, ref, sem).wait()
+
+
+def fold_lanes(values):
+    return sum(values[:, j : j + LANES] for j in range(0, values.shape[1], LANES))
+
+
+def row_sums(folded):
+    return jnp.sum(jnp.transpose(folded), axis=0, keepdims=True)
+
+
+def box_sum(box):
+    def add(i, total):
+        return total + box[i]
+
+    return lax.fori_loop(1, box.shape[0], add, box[0])
+
+
+def eight_rows(rows):
+    filler = jnp.zeros((8 - len(rows), LANES), f32)
+    return jnp.concatenate([*rows, filler], axis=0) if len(rows) < 8 else jnp.concatenate(rows, 0)
+
+
+def columns_of(rows):
+    turned = jnp.transpose(jnp.concatenate([eight_rows(rows), jnp.zeros((120, LANES), f32)], 0))
+    return [turned[:, i : i + 1] for i in range(len(rows))]
+
+
+def exact(left, right, left_dim, right_dim):
+    return lax.dot_general(
+        left,
+        right,
+        (((left_dim,), (right_dim,)), ((), ())),
+        precision=lax.Precision.HIGHEST,
+        preferred_element_type=f32,
+    )
+
+
+def hot_rows(index, batches):
+    rows = lax.broadcasted_iota(jnp.int32, (batches, index.shape[1]), 0)
+    return jnp.where(rows == index, 1.0, 0.0)
+
+
+def sigmoid(value):
+    return 1.0 / (1.0 + jnp.exp(-value))
+
+
+def slope_of(value):
+    sigma = sigmoid(value)
+    return sigma * (1.0 + value * (1.0 - sigma))
+
+
+def pack_layout(latent_pad, batches):
+    mixing = slice(8, 8 + latent_pad + batches)
+    heads = slice(mixing.stop, mixing.stop + 2 * latent_pad)
+    return mixing, heads, slice(heads.stop, heads.stop + batches)
+
+
+def middle_kernel(
+    encoded_ref,
+    index_ref,
+    valid_ref,
+    noise_ref,
+    pack_ref,
+    hidden_ref,
+    centered_ref,
+    sample_ref,
+    share_ref,
+    stats_ref,
+    first_ref,
+    heads_ref,
+    rest_ref,
+    slab_box,
+    box1,
+    box2,
+    slab_sems,
+    sems1,
+    sems2,
+    sample_sems,
+    *,
+    batches,
+    latent,
+    genes_all,
+):
+    group, everyone = Team(True), Team(False)
+    width, slab = first_ref.shape
+    cells = hidden_ref.shape[1]
+    pad = sample_ref.shape[0]
+    mixing_rows, heads_rows, shift_rows = pack_layout(pad, batches)
+    mixing = pack_ref[mixing_rows, :]
+
+    def part(other):
+        return pl.ds(pl.multiple_of(other * slab, LANES), slab)
+
+    mine = part(group.me)
+    everyone.greet()
+    group.send(lambda other: encoded_ref.at[:, part(other)], slab_box.at[group.me], slab_sems)
+    slab_box[group.me] = encoded_ref[:, mine]
+    hot = hot_rows(index_ref[:, mine], batches)
+    valid = valid_ref[:, mine].astype(f32)
+    shift = exact(pack_ref[shift_rows, :], hot, 0, 0)
+    gain1, bias1, gain2, bias2, head_bias = columns_of([pack_ref[i : i + 1, :] for i in range(5)])
+    others = slab_box.at[pl.ds(0, group.size - 1)]
+    await_bytes(others, slab_sems.at[0])
+    await_bytes(others, slab_sems.at[1])
+    total = box_sum(slab_box)
+    rest_ref[0:1, :] = total[width : width + 1, :]
+    pre1 = total[0:width, :] + shift
+
+    def reduced(rows, box, sems):
+        box[everyone.me] = eight_rows(rows)
+        everyone.send(lambda other: box.at[everyone.me], box.at[everyone.me], sems)
+        others = box.at[pl.ds(0, everyone.size - 1)]
+
+        def finish():
+            await_bytes(others, sems.at[0])
+            await_bytes(others, sems.at[1])
+            return box_sum(box)
+
+        return finish
+
+    weighed = valid * pre1
+    sums = reduced(
+        [
+            row_sums(fold_lanes(weighed)),
+            row_sums(fold_lanes(weighed * pre1)),
+            jnp.broadcast_to(jnp.sum(valid, axis=1, keepdims=True), (1, LANES)),
+        ],
+        box1,
+        sems1,
+    )()
+    count = jnp.maximum(sums[2:3], 1.0)
+    mean1 = sums[0:1] / count
+    inverse1 = lax.rsqrt(sums[1:2] / count - mean1 * mean1 + norm_epsilon)
+    mean_col, inverse_col = columns_of([mean1, inverse1])
+    centered1 = (pre1 - mean_col) * inverse_col
+    first_ref[...] = centered1
+    normed1 = centered1 * gain1 + bias1
+    hidden1 = normed1 * sigmoid(normed1)
+    heads = exact(pack_ref[heads_rows, :], hidden1, 1, 0) + head_bias[0 : 2 * pad]
+    heads_ref[...] = heads
+    mean_z, log_var = heads[0:pad], heads[pad : 2 * pad]
+    noise = jnp.concatenate([noise_ref[:, mine], jnp.zeros((pad - latent, slab), f32)], axis=0)
+    sample = mean_z + jnp.exp(0.5 * log_var) * noise
+    rest_ref[1:2, :] = 0.5 * jnp.sum(
+        mean_z * mean_z + jnp.exp(log_var) - log_var - 1.0, axis=0, keepdims=True
+    )
+    sample_ref[:, mine] = sample
+    group.send(lambda other: sample_ref.at[:, mine], sample_ref.at[:, mine], sample_sems)
+    pre2 = exact(mixing, jnp.concatenate([sample, hot], axis=0), 0, 0)
+    weighed = valid * pre2
+    finish = reduced(
+        [row_sums(fold_lanes(weighed)), row_sums(fold_lanes(weighed * pre2))], box2, sems2
+    )
+    scale = 1.0 / (count * genes_all)
+    share_ref[...] = valid_ref[...].astype(f32) * scale[:, 0:1]
+    sums = finish()
+    mean2 = sums[0:1] / count
+    inverse2 = lax.rsqrt(sums[1:2] / count - mean2 * mean2 + norm_epsilon)
+    stats_ref[...] = eight_rows([inverse1, inverse2, count, scale])
+    mean_col, inverse_col = columns_of([mean2, inverse2])
+    others = sample_ref.at[:, pl.ds(0, (group.size - 1) * slab)]
+    await_bytes(others, sample_sems.at[0])
+    await_bytes(others, sample_sems.at[1])
+    piece = pick_chunk(cells, 512)
+
+    def decode(i, carry):
+        columns = pl.ds(pl.multiple_of(i * piece, LANES), piece)
+        mixed = jnp.concatenate(
+            [sample_ref[:, columns], hot_rows(index_ref[:, columns], batches)], axis=0
+        )
+        centered = (exact(mixing, mixed, 0, 0) - mean_col) * inverse_col
+        centered_ref[:, columns] = centered
+        normed = centered * gain2 + bias2
+        hidden_ref[:, columns] = (normed * sigmoid(normed)).astype(bf16)
+        return carry
+
+    lax.fori_loop(0, cells // piece, decode, 0)
+
+
+def middle(encoded, index, valid, noise, pack, batches, pad, genes_all):
+    cells = index.shape[1]
+    width = LANES
+    genes_axis = lax.axis_size("gene")
+    devices = genes_axis * lax.axis_size("cell")
+    slab = cells // genes_axis
+    return pl.pallas_call(
+        functools.partial(
+            middle_kernel, batches=batches, latent=noise.shape[0], genes_all=genes_all
+        ),
+        out_shape=[
+            jax.ShapeDtypeStruct((width, cells), bf16),
+            jax.ShapeDtypeStruct((width, cells), f32),
+            jax.ShapeDtypeStruct((pad, cells), f32),
+            jax.ShapeDtypeStruct((1, cells), f32),
+            jax.ShapeDtypeStruct((8, LANES), f32),
+            jax.ShapeDtypeStruct((width, slab), f32),
+            jax.ShapeDtypeStruct((2 * pad, slab), f32),
+            jax.ShapeDtypeStruct((2, slab), f32),
+        ],
+        in_specs=[IN_VMEM] * 5,
+        out_specs=[IN_VMEM] * 8,
+        scratch_shapes=[
+            pltpu.VMEM((genes_axis, width + 8, slab), f32),
+            pltpu.VMEM((devices, 8, LANES), f32),
+            pltpu.VMEM((devices, 8, LANES), f32),
+        ]
+        + [pltpu.SemaphoreType.DMA((2,))] * 4,
+        compiler_params=talking(1),
+        name="middle",
+    )(encoded, index, valid, noise, pack)
+
+
+def tops_kernel(tops_ref, rest_ref, out_ref, box, sems, back_sems):
+    group = Team(True)
+    slab = rest_ref.shape[1]
+
+    def part(other):
+        return pl.ds(pl.multiple_of(other * slab, LANES), slab)
+
+    mine = part(group.me)
+    group.greet()
+    group.send(lambda other: tops_ref.at[:, part(other)], box.at[group.me], sems)
+    box[group.me] = tops_ref[:, mine]
+    others = box.at[pl.ds(0, group.size - 1)]
+    await_bytes(others, sems.at[0])
+    await_bytes(others, sems.at[1])
+
+    def highest(i, best):
+        return jnp.maximum(best, box[i, 0:1, :])
+
+    top = lax.fori_loop(1, group.size, highest, box[0, 0:1, :])
+
+    def add(i, total):
+        return total + box[i, 1:2, :] * jnp.exp(box[i, 0:1, :] - top)
+
+    total = lax.fori_loop(0, group.size, add, jnp.zeros_like(top))
+    inverse = 1.0 / total
+    out_ref[0:1, mine] = top
+    out_ref[1:2, mine] = rest_ref[0:1, :] * inverse
+    out_ref[2:3, mine] = inverse
+    out_ref[3:4, mine] = inverse
+    group.send(lambda other: out_ref.at[:, mine], out_ref.at[:, mine], back_sems)
+    others = out_ref.at[:, pl.ds(0, (group.size - 1) * slab)]
+    await_bytes(others, back_sems.at[0])
+    await_bytes(others, back_sems.at[1])
+
+
+def combine_tops(tops, rest):
+    group = lax.axis_size("gene")
+    slab = rest.shape[1]
+    return pl.pallas_call(
+        tops_kernel,
+        out_shape=jax.ShapeDtypeStruct((4, tops.shape[1]), f32),
+        in_specs=[IN_VMEM] * 2,
+        out_specs=IN_VMEM,
+        scratch_shapes=[pltpu.VMEM((group, 2, slab), f32)] + [pltpu.SemaphoreType.DMA((2,))] * 2,
+        compiler_params=talking(2),
+        name="combine_tops",
+    )(tops, rest)
+
+
+def sums_kernel(sums_ref, rows_ref, rest_ref, valid_ref, out_ref, box, sems, back_sems, *, genes_all):
+    group = Team(True)
+    slab = rest_ref.shape[1]
+
+    def part(other):
+        return pl.ds(pl.multiple_of(other * slab, LANES), slab)
+
+    mine = part(group.me)
+    group.greet()
+    group.send(lambda other: sums_ref.at[:, part(other)], box.at[group.me], sems)
+    box[group.me] = sums_ref[:, mine]
+    others = box.at[pl.ds(0, group.size - 1)]
+    await_bytes(others, sems.at[0])
+    await_bytes(others, sems.at[1])
+    total = box_sum(box)
+    out_ref[0:1, mine] = total[0:1] * rows_ref[2:3, mine]
+    out_ref[1:2, mine] = (
+        valid_ref[:, mine].astype(f32) * (total[1:2] + rest_ref[1:2, :]) / genes_all
+    )
+    group.send(lambda other: out_ref.at[:, mine], out_ref.at[:, mine], back_sems)
+    others = out_ref.at[:, pl.ds(0, (group.size - 1) * slab)]
+    await_bytes(others, back_sems.at[0])
+    await_bytes(others, back_sems.at[1])
+
+
+def combine_sums(sums, rows, rest, valid, genes_all):
+    group = lax.axis_size("gene")
+    slab = rest.shape[1]
+    return pl.pallas_call(
+        functools.partial(sums_kernel, genes_all=genes_all),
+        out_shape=jax.ShapeDtypeStruct((2, sums.shape[1]), f32),
+        in_specs=[IN_VMEM] * 4,
+        out_specs=IN_VMEM,
+        scratch_shapes=[pltpu.VMEM((group, 2, slab), f32)] + [pltpu.SemaphoreType.DMA((2,))] * 2,
+        compiler_params=talking(3),
+        name="combine_sums",
+    )(sums, rows, rest, valid)
+
+
+def middle_back_kernel(
+    grad_ref,
+    centered_ref,
+    sample_ref,
+    index_ref,
+    valid_ref,
+    noise_ref,
+    pack_ref,
+    stats_ref,
+    first_ref,
+    heads_ref,
+    grad16_ref,
+    small_ref,
+    norms_ref,
+    part_ref,
+    slab_box,
+    box1,
+    box2,
+    slab_sems,
+    sems1,
+    sems2,
+    grad_sems,
+    *,
+    batches,
+    latent,
+):
+    group, everyone = Team(True), Team(False)
+    width, slab = first_ref.shape
+    cells = grad_ref.shape[1]
+    pad = sample_ref.shape[0]
+    mixing_rows, heads_rows, _ = pack_layout(pad, batches)
+    depth = pad + batches
+
+    def part(other):
+        return pl.ds(pl.multiple_of(other * slab, LANES), slab)
+
+    mine = part(group.me)
+    inverse1, inverse2 = stats_ref[0:1, :], stats_ref[1:2, :]
+    count, scale = stats_ref[2:3, 0:1], stats_ref[3:4, 0:1]
+    factor2 = inverse2 * pack_ref[2:3, :]
+    gain1, bias1, gain2, bias2, factor1 = columns_of(
+        [pack_ref[i : i + 1, :] for i in range(4)] + [inverse1 * pack_ref[0:1, :]]
+    )
+    latent_rows = pack_ref[8 : 8 + pad, :] * factor2
+    piece = pick_chunk(cells, 512)
+
+    def gather(i, carry):
+        gains, shifts, products = carry
+        columns = pl.ds(pl.multiple_of(i * piece, LANES), piece)
+        centered = centered_ref[:, columns]
+        grad = grad_ref[:, columns] * slope_of(centered * gain2 + bias2)
+        part_ref[:, columns] = exact(latent_rows, grad, 1, 0)
+        mixed = jnp.concatenate(
+            [sample_ref[:, columns], hot_rows(index_ref[:, columns], batches)], axis=0
+        )
+        return (
+            gains + fold_lanes(grad * centered),
+            shifts + fold_lanes(grad),
+            products + exact(mixed, grad, 1, 1),
+        )
+
+    zeros = jnp.zeros((width, LANES), f32)
+    gains, shifts, products = lax.fori_loop(
+        0, cells // piece, gather, (zeros, zeros, jnp.zeros((depth, width), f32))
+    )
+    everyone.greet()
+
+    def reduced(rows, box, sems):
+        box[everyone.me] = eight_rows(rows)
+        everyone.send(lambda other: box.at[everyone.me], box.at[everyone.me], sems)
+        others = box.at[pl.ds(0, everyone.size - 1)]
+
+        def finish():
+            await_bytes(others, sems.at[0])
+            await_bytes(others, sems.at[1])
+            return box_sum(box)
+
+        return finish
+
+    finish = reduced([row_sums(gains), row_sums(shifts)], box1, sems1)
+    group.send(lambda other: part_ref.at[:, part(other)], slab_box.at[group.me], slab_sems)
+    slab_box[group.me] = part_ref[:, mine]
+    hot = hot_rows(index_ref[:, mine], batches)
+    valid = valid_ref[:, mine].astype(f32)
+    mixed = valid * jnp.concatenate([sample_ref[:, mine], hot], axis=0)
+    centered2 = centered_ref[:, mine]
+    share = valid / count
+    mixed_sum = jnp.sum(mixed, axis=1, keepdims=True)
+    mixed_product = exact(mixed, centered2, 1, 1)
+    noise = jnp.concatenate([noise_ref[:, mine], jnp.zeros((pad - latent, slab), f32)], axis=0)
+    mean_z, log_var = heads_ref[0:pad, :], heads_ref[pad : 2 * pad, :]
+    log_factor = 0.5 * noise * jnp.exp(0.5 * log_var)
+    scaled = valid * scale
+    grad_log_own = scaled * (jnp.exp(log_var) - 1.0) * 0.5
+    centered1 = first_ref[...]
+    normed1 = centered1 * gain1 + bias1
+    sigma1 = sigmoid(normed1)
+    hidden1 = normed1 * sigma1
+    slope1 = sigma1 * (1.0 + normed1 * (1.0 - sigma1))
+
+    sums = finish()
+    gain2_grad, shift2_grad = sums[0:1], sums[1:2]
+    small_ref[0:depth, :] = factor2 * (
+        products - (mixed_sum * shift2_grad + mixed_product * gain2_grad) / count
+    )
+    gain_col, shift_col = columns_of([gain2_grad, shift2_grad])
+    pulled = exact(latent_rows, shift_col + centered2 * gain_col, 1, 0)
+    others = slab_box.at[pl.ds(0, group.size - 1)]
+    await_bytes(others, slab_sems.at[0])
+    await_bytes(others, slab_sems.at[1])
+    grad_sample = box_sum(slab_box) - share * pulled
+    grad_heads = jnp.concatenate(
+        [grad_sample + scaled * mean_z, grad_sample * log_factor + grad_log_own], axis=0
+    )
+    grad_normed1 = exact(pack_ref[heads_rows, :], grad_heads, 0, 0) * slope1
+    finish = reduced(
+        [row_sums(fold_lanes(grad_normed1 * centered1)), row_sums(fold_lanes(grad_normed1))],
+        box2,
+        sems2,
+    )
+    small_ref[depth : depth + 2 * pad, :] = exact(grad_heads, hidden1, 1, 1)
+    small_ref[depth + 2 * pad : depth + 4 * pad, :] = fold_lanes(grad_heads)
+    sums = finish()
+    gain1_grad, shift1_grad = sums[0:1], sums[1:2]
+    norms_ref[...] = eight_rows([gain1_grad, shift1_grad, gain2_grad, shift2_grad])
+    gain_col, shift_col = columns_of([gain1_grad, shift1_grad])
+    grad_pre1 = factor1 * (grad_normed1 - share * (shift_col + centered1 * gain_col))
+    grad16_ref[:, mine] = grad_pre1.astype(bf16)
+    group.send(lambda other: grad16_ref.at[:, mine], grad16_ref.at[:, mine], grad_sems)
+    small_ref[depth + 4 * pad :, :] = exact(hot, grad_pre1, 1, 1)
+    others = grad16_ref.at[:, pl.ds(0, (group.size - 1) * slab)]
+    await_bytes(others, grad_sems.at[0])
+    await_bytes(others, grad_sems.at[1])
+
+
+def middle_back(grad, centered, sample, index, valid, noise, pack, stats, first, heads, batches):
+    cells = index.shape[1]
+    width, slab = first.shape
+    pad = sample.shape[0]
+    genes_axis = lax.axis_size("gene")
+    devices = genes_axis * lax.axis_size("cell")
+    return pl.pallas_call(
+        functools.partial(middle_back_kernel, batches=batches, latent=noise.shape[0]),
+        out_shape=[
+            jax.ShapeDtypeStruct((width, cells), bf16),
+            jax.ShapeDtypeStruct((5 * pad + 2 * batches, LANES), f32),
+            jax.ShapeDtypeStruct((8, LANES), f32),
+        ],
+        in_specs=[IN_VMEM] * 10,
+        out_specs=[IN_VMEM] * 3,
+        scratch_shapes=[
+            pltpu.VMEM((pad, cells), f32),
+            pltpu.VMEM((genes_axis, pad, slab), f32),
+            pltpu.VMEM((devices, 8, LANES), f32),
+            pltpu.VMEM((devices, 8, LANES), f32),
+        ]
+        + [pltpu.SemaphoreType.DMA((2,))] * 4,
+        compiler_params=talking(4),
+        name="middle_back",
+    )(grad, centered, sample, index, valid, noise, pack, stats, first, heads)
 
 
 def fill_hidden(long_ref, hidden_ref, top):
@@ -124,7 +633,7 @@
     long_ref[width:HOT_DEPTH, :] = extra.astype(bf16)
 
 
-def totals_kernel(hidden_ref, weight_ref, top_ref, total_ref, long_ref, value_ref, *, genes, chunk):
+def totals_kernel(hidden_ref, weight_ref, out_ref, long_ref, value_ref, *, chunk):
     size = weight_ref.shape[0]
     fill_hidden(long_ref, hidden_ref, None)
     value_ref[...] = jnp.dot(weight_ref[...], long_ref[...], preferred_element_type=f32)
@@ -142,19 +651,19 @@
         return total + part[:8] + part[8:]
 
     total = lax.fori_loop(0, count, add, jnp.zeros((8, chunk), f32), unroll=4)
-    top_ref[...] = top
-    total_ref[...] = jnp.sum(total, axis=0, keepdims=True)
-
-
-def totals(hidden, weight, genes):
+    out_ref[0:1, :] = top
+    out_ref[1:2, :] = jnp.sum(total, axis=0, keepdims=True)
+
+
+def totals(hidden, weight):
     width, cells = hidden.shape
     chunk = pick_chunk(cells, 512)
     return pl.pallas_call(
-        functools.partial(totals_kernel, genes=genes, chunk=chunk),
+        functools.partial(totals_kernel, chunk=chunk),
         grid=(cells // chunk,),
         in_specs=[column_blocks(width, chunk), whole(weight)],
-        out_specs=[column_blocks(1, chunk)] * 2,
-        out_shape=[jax.ShapeDtypeStruct((1, cells), f32)] * 2,
+        out_specs=column_blocks(2, chunk),
+        out_shape=jax.ShapeDtypeStruct((2, cells), f32),
         scratch_shapes=[
             pltpu.VMEM((HOT_DEPTH, chunk), bf16),
             pltpu.VMEM((weight.shape[0], chunk), f32),
@@ -167,8 +676,7 @@
 def likelihood_kernel(
     counts_ref,
     hidden_ref,
-    top_ref,
-    ratio_ref,
+    rows_ref,
     share_ref,
     weight_ref,
     back_ref,
@@ -177,8 +685,7 @@
     slope_ref,
     table_ref,
     slopes_ref,
-    loss_ref,
-    total_ref,
+    sums_ref,
     grad_hidden_ref,
     grad_weight_ref,
     grad_bias_ref,
@@ -199,9 +706,9 @@
         for ref in (grad_weight_ref, grad_bias_ref, grad_theta_ref):
             ref[...] = jnp.zeros_like(ref)
 
-    fill_hidden(long_ref, hidden_ref, top_ref[...])
+    fill_hidden(long_ref, hidden_ref, rows_ref[0:1, :])
     tiles = [slice(j, j + LANES) for j in range(0, chunk, LANES)]
-    ratio_all = ratio_ref[...]
+    ratio_all = rows_ref[1:2, :]
     share_all = share_ref[...]
 
     def group(held, rows, read, carry):
@@ -288,15 +795,15 @@
             carry,
         )
     for j, columns in enumerate(tiles):
-        loss_ref[:, columns] = jnp.sum(carry[0][j], axis=0, keepdims=True)
-        total_ref[:, columns] = jnp.sum(carry[1][j], axis=0, keepdims=True)
+        sums_ref[0:1, columns] = jnp.sum(carry[1][j], axis=0, keepdims=True)
+        sums_ref[1:2, columns] = jnp.sum(carry[0][j], axis=0, keepdims=True)
     grad_weight_ref[...] += lax.dot_general(
         second_ref[...], hidden_ref[...], (((1,), (1,)), ((), ())), preferred_element_type=f32
     )
     grad_hidden_ref[...] = jnp.dot(back_ref[...], second_ref[...], preferred_element_type=f32)
 
 
-def likelihood(counts_t, hidden, top, ratio, share, weights, back, gene_tables):
+def likelihood(counts_t, hidden, rows, share, weights, back, gene_tables):
     genes, cells = counts_t.shape
     size = weights.shape[1]
     width = hidden.shape[0]
@@ -307,15 +814,18 @@
     return pl.pallas_call(
         functools.partial(likelihood_kernel, genes=genes, chunk=chunk),
         grid=(cells // chunk,),
-        in_specs=[column_blocks(genes, chunk), column_blocks(width, chunk), row, row, row]
-        + [whole(weights), whole(back)]
+        in_specs=[column_blocks(genes, chunk), column_blocks(width, chunk)]
+        + [column_blocks(rows.shape[0], chunk), row, whole(weights), whole(back)]
         + [whole(a) for a in gene_tables],
-        out_specs=[column_blocks(size, chunk), row, row, column_blocks(width, chunk)]
+        out_specs=[
+            column_blocks(size, chunk),
+            column_blocks(2, chunk),
+            column_blocks(width, chunk),
+        ]
         + [per_gene] * 3,
         out_shape=[
             jax.ShapeDtypeStruct((size, cells), f32),
-            jax.ShapeDtypeStruct((1, cells), f32),
-            jax.ShapeDtypeStruct((1, cells), f32),
+            jax.ShapeDtypeStruct((2, cells), f32),
             jax.ShapeDtypeStruct((width, cells), f32),
         ]
         + [jax.ShapeDtypeStruct((size, LANES), f32)] * 3,
@@ -326,13 +836,13 @@
         ],
         compiler_params=PARAMS,
         name="likelihood",
-    )(counts_t, hidden, top, ratio, share, weights, back, *gene_tables)
+    )(counts_t, hidden, rows, share, weights, back, *gene_tables)
 
 
 def frequency_kernel(
     slopes_ref,
     hidden_ref,
-    top_ref,
+    rows_ref,
     pull_ref,
     share_ref,
     other_ref,
@@ -354,10 +864,10 @@
         for ref in (grad_weight_ref, grad_bias_ref):
             ref[...] = jnp.zeros_like(ref)
 
-    fill_hidden(long_ref, hidden_ref, top_ref[...])
+    fill_hidden(long_ref, hidden_ref, rows_ref[0:1, :])
     value_ref[...] = jnp.dot(weight_ref[...], long_ref[...], preferred_element_type=f32)
     tiles = [slice(j, j + LANES) for j in range(0, chunk, LANES)]
-    pull_all = pull_ref[...]
+    pull_all = pull_ref[0:1, :]
     share_all = share_ref[...]
 
     def step(i, carry):
@@ -381,7 +891,7 @@
     )
 
 
-def frequency(slopes, hidden, top, pull, share, other, weight, back):
+def frequency(slopes, hidden, rows, pull, share, other, weight, back):
     size, cells = slopes.shape
     width = hidden.shape[0]
     chunk = pick_chunk(cells, 512)
@@ -391,8 +901,8 @@
     return pl.pallas_call(
         functools.partial(frequency_kernel, chunk=chunk),
         grid=(cells // chunk,),
-        in_specs=[column_blocks(size, chunk), wide, row, row, row, wide]
-        + [whole(weight), whole(back)],
+        in_specs=[column_blocks(size, chunk), wide, column_blocks(rows.shape[0], chunk)]
+        + [column_blocks(2, chunk), row, wide, whole(weight), whole(back)],
         out_specs=[wide, per_gene, per_gene],
         out_shape=[jax.ShapeDtypeStruct((width, cells), f32)]
         + [jax.ShapeDtypeStruct((size, LANES), f32)] * 2,
@@ -403,7 +913,7 @@
         ],
         compiler_params=PARAMS,
         name="frequency",
-    )(slopes, hidden, top, pull, share, other, weight, back)
+    )(slopes, hidden, rows, pull, share, other, weight, back)
 
 
 def encoder_back_kernel(counts_ref, grad_ref, weight_ref, input_ref, weight_grad_ref):
@@ -472,23 +982,10 @@
     cells, genes = counts.shape
     gene_devices = lax.axis_size("gene")
     genes_all = genes * gene_devices
-    slab = cells // gene_devices
-    first = lax.axis_index("gene") * slab
     latent = head_bias.shape[0] // 2
     batches = batch_shift.shape[0]
     size = padded(genes)
     gap = size - genes
-    everyone = ("gene", "cell")
-    dot = functools.partial(jnp.dot, precision=lax.Precision.HIGHEST)
-
-    def dot_nt(left, right):
-        return lax.dot_general(
-            left, right, (((1,), (1,)), ((), ())), precision=lax.Precision.HIGHEST
-        )
-
-    def mine(array):
-        return lax.dynamic_slice_in_dim(array, first, slab, 1)
-
     counts_t = counts.T
     weight16 = encoder_weight.astype(bf16)
     encoder_t = jnp.pad(weight16, ((0, gap), (0, 0))).T
@@ -525,67 +1022,38 @@
     weights = jnp.transpose(jnp.concatenate([out16, parts, ones, rest], axis=2), (1, 0, 2))
     backs = jnp.transpose(out16, (1, 2, 0))
 
-    encoded, library = encode(counts_t, encoder_t)
-    valid = valid_mask.astype(f32)[None, :]
-    hot = (jnp.arange(batches)[:, None] == batch_index[None, :]).astype(f32)
-    valid_mine, hot_mine, noise = mine(valid), mine(hot), mine(noise_draw.T)
-    pre1 = lax.psum_scatter(encoded, "gene", scatter_dimension=1, tiled=True)
-    pre1 = pre1 + dot(batch_shift.T, hot_mine)
-    library = lax.psum(library, "gene")
-    sum1, square1, tally = lax.psum(
-        (
-            jnp.sum(valid_mine * pre1, axis=1),
-            jnp.sum(valid_mine * pre1 * pre1, axis=1),
-            jnp.sum(valid_mine),
-        ),
-        everyone,
-    )
-    count = jnp.maximum(tally, 1.0)
-    scale = 1.0 / (count * genes_all)
-    norms = layer_norm_params[:, :, None]
-    mean1 = sum1 / count
-    inverse1 = lax.rsqrt(square1 / count - mean1 * mean1 + norm_epsilon)[:, None]
-    centered1 = (pre1 - mean1[:, None]) * inverse1
-    normed1 = centered1 * norms[0] + norms[1]
-    hidden1 = jax.nn.silu(normed1)
-    heads = dot(head_weight.T, hidden1) + head_bias[:, None]
-    mean_z, log_var = heads[:latent], heads[latent:]
-    spread_z = jnp.exp(0.5 * log_var)
-    sample = mean_z + spread_z * noise
-    diverge = 0.5 * jnp.sum(
-        mean_z * mean_z + jnp.exp(log_var) - log_var - 1.0, axis=0, keepdims=True
-    )
-
-    pre2_mine = dot(decoder_input.T, jnp.concatenate([sample, hot_mine], axis=0))
-    sum2, square2 = lax.psum(
-        (jnp.sum(valid_mine * pre2_mine, axis=1), jnp.sum(valid_mine * pre2_mine**2, axis=1)),
-        everyone,
-    )
-    sample_all = lax.all_gather(sample, "gene", axis=1, tiled=True)
-    mixed = jnp.concatenate([sample_all, hot], axis=0)
-    mean2 = sum2 / count
-    inverse2 = lax.rsqrt(square2 / count - mean2 * mean2 + norm_epsilon)[:, None]
-
-    def normed_of(values):
-        centered = (values - mean2[:, None]) * inverse2
-        return centered, centered * norms[2] + norms[3]
-
-    centered2, normed2 = normed_of(dot(decoder_input.T, mixed))
-    hidden2 = jax.nn.silu(normed2).astype(bf16)
-
-    top_here, total_here = totals(hidden2, weights[0], genes)
-    tops = lax.all_gather(jnp.concatenate([top_here, total_here], axis=0), "gene")
-    top = jnp.max(tops[:, 0], axis=0, keepdims=True)
-    total = jnp.sum(tops[:, 1] * jnp.exp(tops[:, 0] - top), axis=0, keepdims=True)
-    share = scale * valid
-    slopes, loss, pull, grad_hidden2, grad_out1, grad_bias1, grad_theta = likelihood(
-        counts_t, hidden2, top, library / total, share, weights, backs[1], gene_tables
-    )
-    pull, loss = lax.psum((pull, loss), "gene")
-    diverge_all = lax.all_gather(diverge, "gene", axis=1, tiled=True)
-    cell_loss = (valid * (loss + diverge_all) / genes_all)[0]
+    pad = 16
+    heads_t = jnp.pad(head_weight.T.reshape(2, latent, -1), ((0, 0), (0, pad - latent), (0, 0)))
+    bias_row = jnp.pad(head_bias.reshape(2, latent), ((0, 0), (0, pad - latent))).reshape(1, -1)
+    bias_row = jnp.pad(bias_row, ((0, 0), (0, LANES - 2 * pad)))
+    pack = jnp.concatenate(
+        [
+            layer_norm_params,
+            bias_row,
+            jnp.zeros((3, LANES), f32),
+            decoder_input[:latent],
+            jnp.zeros((pad - latent, LANES), f32),
+            decoder_input[latent:],
+            heads_t.reshape(2 * pad, -1),
+            batch_shift,
+        ],
+        axis=0,
+    )
+    index, valid, noise = batch_index[None, :], valid_mask[None, :], noise_draw.T
+
+    encoded = encode(counts_t, encoder_t)
+    hidden2, centered2, sample, share, stats, centered1, heads, rest_rows = middle(
+        encoded, index, valid, noise, pack, batches, pad, genes_all
+    )
+    rows = combine_tops(totals(hidden2, weights[0]), rest_rows)
+    slopes, sums, grad_hidden2, grad_out1, grad_bias1, grad_theta = likelihood(
+        counts_t, hidden2, rows, share, weights, backs[1], gene_tables
+    )
+    pull = combine_sums(sums, rows, rest_rows, valid, genes_all)
+    cell_loss = pull[1]
+
     grad_hidden2, grad_out0, grad_bias0 = frequency(
-        slopes, hidden2, top, pull / total, share, grad_hidden2, weights[0], backs[0]
+        slopes, hidden2, rows, pull, share, grad_hidden2, weights[0], backs[0]
     )
     grad_genes = jnp.stack(
         [
@@ -594,53 +1062,19 @@
             jnp.sum(grad_theta, axis=1) * theta,
         ]
     )[:, :genes]
-
-    grad_normed2 = grad_hidden2 * silu_slope(normed2)
-    gain2_grad, shift2_grad = lax.psum(
-        (jnp.sum(grad_normed2 * centered2, axis=1), jnp.sum(grad_normed2, axis=1)), everyone
-    )
-    factor2 = inverse2 * norms[2]
-    latent_rows = decoder_input[:latent]
-    grad_sample = lax.psum_scatter(
-        dot(latent_rows, factor2 * grad_normed2), "gene", scatter_dimension=1, tiled=True
-    )
-    centered2_mine, _ = normed_of(pre2_mine)
-    grad_sample = grad_sample - valid_mine / count * dot(
-        latent_rows,
-        factor2 * (shift2_grad[:, None] + centered2_mine * gain2_grad[:, None]),
-    )
-    mixed_mine = valid_mine * jnp.concatenate([sample, hot_mine], axis=0)
-    grad_mixing = factor2[:, 0] * (
-        dot_nt(mixed, grad_normed2)
-        - (
-            jnp.sum(mixed_mine, axis=1, keepdims=True) * shift2_grad
-            + dot_nt(mixed_mine, centered2_mine) * gain2_grad
-        )
-        / count
-    )
-    grad_mean = grad_sample + scale * valid_mine * mean_z
-    grad_log = (
-        grad_sample * noise * spread_z * 0.5
-        + scale * valid_mine * (jnp.exp(log_var) - 1.0) * 0.5
-    )
-    grad_heads_out = jnp.concatenate([grad_mean, grad_log], axis=0)
-    grad_heads = dot_nt(hidden1, grad_heads_out)
-    grad_head_bias = jnp.sum(grad_heads_out, axis=1)
-    grad_normed1 = dot(head_weight, grad_heads_out) * silu_slope(normed1)
-    gain1_grad, shift1_grad = lax.psum(
-        (jnp.sum(grad_normed1 * centered1, axis=1), jnp.sum(grad_normed1, axis=1)), everyone
-    )
-    grad_pre1 = (inverse1 * norms[0]) * (
-        grad_normed1
-        - valid_mine / count * (shift1_grad[:, None] + centered1 * gain1_grad[:, None])
-    )
-    grad_shift = dot_nt(hot_mine, grad_pre1)
-    grad_pre16 = lax.all_gather(grad_pre1.astype(bf16), "gene", axis=1, tiled=True)
+    grad_pre16, small, norm_rows = middle_back(
+        grad_hidden2, centered2, sample, index, valid, noise, pack, stats, centered1, heads, batches
+    )
     input_grad, grad_encoder = encoder_back(counts_t, grad_pre16, weight16)
-    grad_shift, grad_heads, grad_head_bias, grad_mixing = lax.psum(
-        (grad_shift, grad_heads, grad_head_bias, grad_mixing), everyone
-    )
-    grad_norms = jnp.stack([gain1_grad, shift1_grad, gain2_grad, shift2_grad])
+    small = lax.psum(small, ("gene", "cell"))
+    depth = pad + batches
+    grad_mixing = jnp.concatenate([small[:latent], small[pad:depth]], axis=0)
+    grad_heads = small[depth : depth + 2 * pad].reshape(2, pad, -1)[:, :latent]
+    grad_heads = grad_heads.reshape(2 * latent, -1).T
+    grad_head_bias = jnp.sum(small[depth + 2 * pad : depth + 4 * pad], axis=1)
+    grad_head_bias = grad_head_bias.reshape(2, pad)[:, :latent].reshape(-1)
+    grad_shift = small[depth + 4 * pad :]
+    grad_norms = norm_rows[:4]
     grad_encoder, grad_out0, grad_out1, grad_genes = lax.psum(
         (grad_encoder, grad_out0[:genes], grad_out1[:genes], grad_genes), "cell"
     )

time: 857 us -> 716 us (0.84)
  blocking collectives: 373 us -> 10.9 us
  Pallas kernels: 287 us -> 440 us
  waiting for transfers between devices: 51.3 us -> 146 us
  matrix products: 19 us -> 0 us
  other arithmetic: 52.8 us -> 36.9 us
    psum x7 -> x0, blocking collectives: 273 us -> none  [the longest x1 41.5 us: local(): lax.psum((jnp.sum(grad_normed1 * centered1, axis=1), jnp.sum(grad_normed1...]
    pallas_call x1 -> x5, Pallas kernels: 21.6 us -> 175 us  [the longest x1 81.4 us: middle(): pl.pallas_call(functools.partial(middle_kernel, batches=batches, latent=n...]
    all_gather x3 -> x0, blocking collectives: 87.6 us -> none  [the longest x1 30.9 us: local(): sample_all = lax.all_gather(sample, 'gene', axis=1, tiled=True)]
    psum x0 -> x1, waiting for transfers between devices: none -> 63.7 us  [local(): small = lax.psum(small, ('gene', 'cell'))]
    psum x1, waiting for transfers between devices: 51.2 us -> 82.5 us  [local(): lax.psum((grad_encoder, grad_out0[:genes], grad_out1[:genes], grad_genes)...]
    dot_general x11 -> x0, matrix products: 19 us -> none  [the longest x4 4.81 us: dot_nt(): lax.dot_general(left, right, (((1,), (1,)), ((), ())), precision=lax.Prec...]
    unnamed x147 -> x65, local copies, waits for them, and re-layouts: 28.6 us -> 28.6 us
  transfers between devices with their start and end apart: 4 -> 2, of which waited for: 1 -> 2; matrix products, arithmetic and copies ran while one was open for 7% -> 2% of each run, Pallas kernels for 0% -> 6%
where the time goes in v2:
time: 716 us; the launch traced here: 710 us
  Pallas kernels  440 us (61%)
  waiting for transfers between devices  146 us (20%)
  local copies, waits for them, and re-layouts  60.5 us (8%)
  other arithmetic  36.9 us (5%)
  between operations  14.8 us (2%)
  blocking collectives  10.9 us (2%)
    pallas_call x1, Pallas kernels, likelihood(): pl.pallas_call(functools.partial(likelihood_kernel, genes=genes, chunk=ch...  167 us
    psum x1, waiting for transfers between devices, local(): lax.psum((grad_encoder, grad_out0[:genes], grad_out1[:genes], grad_genes)...  82.5 us
    pallas_call x1, Pallas kernels, middle(): pl.pallas_call(functools.partial(middle_kernel, batches=batches, latent=n...  81.4 us
    psum x1, waiting for transfers between devices, local(): small = lax.psum(small, ('gene', 'cell'))  63.7 us
    pallas_call x1, Pallas kernels, middle_back(): pl.pallas_call(functools.partial(middle_back_kernel, batches=batches, lat...  47.7 us
    pallas_call x1, Pallas kernels, encoder_back(): pl.pallas_call(encoder_back_kernel, grid=(pl.cdiv(genes, block),), in_spe...  39.6 us
    pallas_call x1, Pallas kernels, frequency(): pl.pallas_call(functools.partial(frequency_kernel, chunk=chunk), grid=(ce...  37.7 us
    unnamed x65, local copies, waits for them, and re-layouts  28.6 us
  transfers between devices with their start and end apart: 2, of which 2 were waited for; matrix products, arithmetic and copies ran while one was open for 2% of the time, Pallas kernels for 6%

profile of v2, /device:TPU:0, one launch (start us, length us, event | category | flops | bytes accessed | tf_op | source)
XLA Modules:
  0.0 709.7 jit_solution(16398904841281372842)
XLA Ops:
  7.2 0.0 all-reduce.11.cloned.1.call-start
  7.3 0.6 compare_select_fusion.3
  7.9 1.3 slice.59
  9.2 0.8 exponential_reduce_fusion
  10.0 0.8 slice_bitcast_fusion.5
  10.8 0.1 fusion.40
  10.9 0.6 copy.110
  11.6 0.6 copy.109
  12.2 2.9 convert_element_type.30
  15.1 1.4 copy.108
  16.5 1.3 pad_bitcast_fusion.1
  17.8 0.1 broadcast_in_dim.52
  17.9 6.0 concatenate.14
  24.0 2.6 copy.113.weight_ref
  26.6 0.1 reshape.315
  26.7 0.1 reshape.316
  26.8 0.2 select_select_fusion
  26.9 1.4 convert_element_type.29.weight_ref
  28.4 1.1 copy.107.weight_ref
  29.5 1.1 slice_bitcast_fusion.3
  30.6 1.5 copy.112.weight_ref
  32.1 20.5 %encode.1.encoded_ref = f32[136,4096]{1,0:T(8,128)} custom-call(s32[2500,4096]{1,0:T(8,128)} %bitcast.53, bf16[128,2512]{1,0:T(8,128)(2,1)} %copy.107.weight_ref), custom_call_target="tpu_custom_call" | custom-call | tf_op jit(solution)/shard_map/encode/pallas_call | solution.py:103
  52.6 4.3 concatenate.13.pack_ref
  56.9 81.4 %middle.1 = (bf16[128,4096]{1,0:T(8,128)(2,1)}, f32[128,4096]{1,0:T(8,128)}, f32[16,4096]{1,0:T(8,128)}, f32[1,4096]{1,0:T(1,128)}, f32[8,128]{1,0:T(8,128)}, /*...) custom-call(f32[136,4096]{1,0:T(8,128)} %encode.1.encoded_ref, s32[1,4096]{1,0:T(1,128)} %bitcast.64, ...), custom_call_target="tpu_custom_call" | custom-call | tf_op jit(solution)/shard_map/middle/pallas_call | solution.py:344
  138.3 21.4 %totals.1.tops_ref = f32[2,4096]{1,0:T(2,128)} custom-call(bf16[128,4096]{1,0:T(8,128)(2,1)} %get-tuple-element.48.hidden_ref, bf16[2512,144]{1,0:T(8,128)(2,1)} %copy.112.weight_ref), custom_call_target="tpu_custom_call" | custom-call | tf_op jit(solution)/shard_map/totals/pallas_call | solution.py:661
  159.8 13.7 %combine_tops.1.rows_ref = f32[4,4096]{1,0:T(4,128)} custom-call(f32[2,4096]{1,0:T(2,128)} %totals.1.tops_ref, f32[2,512]{1,0:T(2,128)} %get-tuple-element.49.rest_ref), custom_call_target="tpu_custom_call" | custom-call | tf_op jit(solution)/shard_map/combine_tops/pallas_call | solution.py:409
  173.5 15.1 %subtract_subtract_fusion = (f32[2512,64]{1,0:T(8,128)S(1)}, f32[2512,64]{1,0:T(8,128)S(1)}) fusion(f32[64]{0:T(128)S(1)} %copy-done.30, f32[2512]{0:T(1024)S(1)} %get-tuple-element.243, f32[2512]{0:T(1024)S(1)} %get-tuple-element.247, f32[2512]{0:T(1024)S(1)} %get-tuple-element.246), kind=kLoop, calls=%fused_computation.17 | loop fusion | flops 16076800 | bytes 1316544 | tf_op jit(solution)/shard_map/sub | solution.py:1003
  188.6 1.5 pad_maximum_fusion.table_ref
  190.0 1.4 broadcast_in_dim.55.log_ref
  191.5 1.5 broadcast_in_dim.56.slope_ref
  192.9 1.4 broadcast_in_dim.54.theta_ref
  194.4 167.5 %likelihood.1 = (f32[2512,4096]{1,0:T(8,128)}, f32[2,4096]{1,0:T(2,128)}, f32[128,4096]{1,0:T(8,128)}, f32[2512,128]{1,0:T(8,128)}, f32[2512,128]{1,0:T(8,128)}, /*index=5*/f32[2512,128]{1,0:T(8,128)}) custom-call(s32[2500,4096]{1,0:T(8,128)} %bitcast.54, bf16[128,4096]{1,0:T(8,128)(2,1)} %get-tuple-element.48.hidden_ref, f32[4,4096]{1,0:T(4,128)} %combine_tops.1.rows_ref, ...), custom_call_target="tpu_custom_call" | custom-call | tf_op jit(solution)/shard_map/likelihood/pallas_call | solution.py:814
  361.9 10.9 %combine_sums.1.pull_ref = f32[2,4096]{1,0:T(2,128)} custom-call(f32[2,4096]{1,0:T(2,128)} %get-tuple-element.51.sums_ref, f32[4,4096]{1,0:T(4,128)} %combine_tops.1.rows_ref, f32[2,512]{1,0:T(2,128)} %get-tuple-element.49.rest_ref, s32[1,4096]{1,0:T(1,128)} %bitcast.62), custom_call_target="tpu_custom_call" | custom-call | tf_op jit(solution)/shard_map/combine_sums/pallas_call | solution.py:448
  372.7 37.7 %frequency.1 = (f32[128,4096]{1,0:T(8,128)}, f32[2512,128]{1,0:T(8,128)}, f32[2512,128]{1,0:T(8,128)}) custom-call(f32[2512,4096]{1,0:T(8,128)} %get-tuple-element.52.slopes_ref, bf16[128,4096]{1,0:T(8,128)(2,1)} %get-tuple-element.48.hidden_ref, f32[4,4096]{1,0:T(4,128)} %combine_tops.1.rows_ref, f32[2,4096]{1,0:T(2,128)} %combine_sums.1.pull_ref, ...), custom_call_target="tpu_custom_call" | custom-call | tf_op jit(solution)/shard_map/frequency/pallas_call | solution.py:901
  410.4 47.7 %middle_back.1 = (bf16[128,4096]{1,0:T(8,128)(2,1)}, f32[144,128]{1,0:T(8,128)}, f32[8,128]{1,0:T(8,128)}) custom-call(f32[128,4096]{1,0:T(8,128)} %get-tuple-element.54.grad_ref, f32[128,4096]{1,0:T(8,128)} %get-tuple-element.55.centered_ref, f32[16,4096]{1,0:T(8,128)} %get-tuple-element.56.sample_ref, s32[1,4096]{1,0:T(1,128)} %bitcast.65, ...), custom_call_target="tpu_custom_call" | custom-call | tf_op jit(solution)/shard_map/middle_back/pallas_call | solution.py:600
  458.2 0.0 all-reduce.11.cloned.1.call-update
  458.2 0.0 all-reduce.13.cloned.1.call-start
  458.3 1.1 slice_bitcast_fusion.1
  459.4 0.6 copy-done.7
  460.0 1.1 slice_bitcast_fusion
  461.1 39.6 %encoder_back.1 = (f32[2500,4096]{1,0:T(8,128)}, f32[2500,128]{1,0:T(8,128)}) custom-call(s32[2500,4096]{1,0:T(8,128)} %bitcast.55, bf16[128,4096]{1,0:T(8,128)(2,1)} %get-tuple-element.60.grad_ref, bf16[2500,128]{1,0:T(8,128)(2,1)} %copy-done.1), custom_call_target="tpu_custom_call" | custom-call | tf_op jit(solution)/shard_map/encoder_back/pallas_call | solution.py:931
  500.7 0.0 all-reduce.13.cloned.1.call-update
  500.7 1.3 copy-done.3
  502.0 0.4 reduce_sum.36
  502.5 1.9 reduce_sum.37
  504.5 1.8 reduce_sum.38
  506.3 0.6 slice.64
  507.0 10.9 %psum.38 = f32[3,2500]{1,0:T(4,128)S(1)} all-reduce(f32[3,2500]{1,0:T(4,128)S(1)} %pad_maximum_fusion.1), channel_id=1, replica_groups=mesh['gene'=8,'cell'=4] {'cell'}, use_global_device_ids=true, to_apply=%region_6.7 | all-reduce | flops 7500 | bytes 60000 | tf_op jit(solution)/shard_map/psum | solution.py:1078
  517.9 0.6 multiply_add_fusion.9
  518.5 0.7 multiply_add_fusion.2
  519.2 63.7 %all-reduce.11.cloned.1.call-done = f32[144,128]{1,0:T(8,128)} async-done(((f32[144,128]{1,0:T(8,128)}), f32[144,128]{1,0:T(8,128)}) %all-reduce.11.cloned.1.call-update) | async-done | bytes 73744 | tf_op jit(solution)/shard_map/psum | solution.py:1069
  582.9 1.5 fusion.48
  584.4 0.1 reshape.321
  584.5 0.1 reshape.322
  584.6 0.7 slice.84
  585.3 0.5 multiply_add_fusion.11
  585.8 0.6 multiply_add_fusion.8
  586.4 0.6 multiply_add_fusion.4
  587.1 82.5 %all-reduce.13.cloned.1.call-done = (f32[2500,128]{1,0:T(8,128)}, f32[2500,1,128]{2,0,1:T(8,128)}, f32[2500,1,128]{2,0,1:T(8,128)}) async-done(((f32[2500,128]{1,0:T(8,128)}, f32[2500,1,128]{2,0,1:T(8,128)}, f32[2500,1,128]{2,0,1:T(8,128)}), (f32[2500,128]{1,0:T(8,128)}, f32[2500,1,128]{2,0,1:T(8,128)}, f32[2500,1,128]{2,0,1:T(8,128)})) %all-reduce.13.cloned.1.call-update) | async-done | bytes 3840016 | tf_op jit(solution)/shard_map/psum | solution.py:1078
  669.5 4.3 fusion
  673.8 8.9 %copy.120 = f32[2,128,2500]{1,0,2:T(2,128)} copy(f32[2,128,2500]{1,2,0:T(8,128)S(1)} %get-tuple-element.221) | data formatting | bytes 5120000
  682.6 8.8 %copy.118 = f32[2,128,2500]{1,0,2:T(2,128)} copy(f32[2,128,2500]{1,2,0:T(8,128)S(1)} %get-tuple-element.222) | data formatting | bytes 5120000
  691.5 8.9 %copy.119 = f32[2,128,2500]{1,0,2:T(2,128)} copy(f32[2,128,2500]{1,2,0:T(8,128)S(1)} %get-tuple-element.228) | data formatting | bytes 5120000
  700.3 2.3 multiply_add_fusion
  (82 shorter events, 0.4 us)
Async XLA Ops:
  7.2 575.7 %all-reduce.11.cloned.1.call-start = ((), (), s32[]{:S(2)}) async-start(), calls=%async_computation | async-start | bytes 147456 | tf_op jit(solution)/shard_map/psum | solution.py:1069
  24.0 2.6 copy-start.27
  24.0 2.8 copy-start.14
  28.3 1.2 copy-start.1
  32.1 20.5 %slice-start = ((f32[42,128]{1,0:T(8,128)}), f32[10,128]{1,0:T(8,128)S(1)}, s32[]{:S(2)}) async-start(f32[42,128]{1,0:T(8,128)} %param.39), calls=%async_computation.2 | async-start | bytes 16384 | tf_op jit(solution)/shard_map/slice | solution.py:1034
  32.1 20.5 %copy-start.12 = (f32[32,128]{1,0:T(8,128)S(1)}, f32[32,128]{1,0:T(8,128)}, u32[]{:S(2)}) copy-start(f32[32,128]{1,0:T(8,128)} %param.35) | copy-start | bytes 49156
  32.1 20.5 %copy-start.13 = (f32[32,128]{1,0:T(8,128)S(1)}, f32[32,128]{1,0:T(8,128)}, u32[]{:S(2)}) copy-start(f32[32,128]{1,0:T(8,128)} %slice.59) | copy-start | bytes 49156
  32.1 20.5 %copy-start.23 = (f32[4,128]{1,0:T(4,128)S(1)}, f32[4,128]{1,0:T(4,128)}, u32[]{:S(2)}) copy-start(f32[4,128]{1,0:T(4,128)} %param.36) | copy-start | bytes 6148
  138.3 35.2 %copy-start.30 = (f32[64]{0:T(128)S(1)}, f32[64]{0:T(128)}, u32[]{:S(2)}) copy-start(f32[64]{0:T(128)} %compare_select_fusion.3) | copy-start | bytes 772
  410.4 47.8 %copy-start.8 = (f32[2512,128]{1,0:T(8,128)S(1)}, f32[2512,128]{1,0:T(8,128)}, u32[]{:S(2)}) copy-start(f32[2512,128]{1,0:T(8,128)} %get-tuple-element.63) | copy-start | bytes 3858436
  458.2 1.8 copy-start.7
  458.2 211.3 %all-reduce.13.cloned.1.call-start = ((), (), s32[]{:S(2)}) async-start(), calls=%async_computation.1 | async-start | bytes 7692288 | tf_op jit(solution)/shard_map/psum | solution.py:1078
  500.7 1.3 copy-start.3
  502.4 3.9 copy-start.9
  502.4 15.4 %copy-start.24 = (f32[4,128]{1,0:T(4,128)S(1)}, f32[4,128]{1,0:T(4,128)}, u32[]{:S(2)}) copy-start(f32[4,128]{1,0:T(4,128)} %param.52) | copy-start | bytes 6148
  502.4 15.4 %copy-start.25 = (f32[4,128]{1,0:T(4,128)S(1)}, f32[4,128]{1,0:T(4,128)}, u32[]{:S(2)}) copy-start(f32[4,128]{1,0:T(4,128)} %param.44) | copy-start | bytes 6148
  502.4 15.4 %copy-start.26 = (f32[8,128]{1,0:T(8,128)S(1)}, f32[8,128]{1,0:T(8,128)}, u32[]{:S(2)}) copy-start(f32[8,128]{1,0:T(8,128)} %get-tuple-element.69) | copy-start | bytes 12292
  502.5 16.0 %copy-start.10 = (f32[3,2500]{1,0:T(4,128)S(1)}, f32[3,2500]{1,0:T(4,128)}, u32[]{:S(2)}) copy-start(f32[3,2500]{1,0:T(4,128)} %param.34) | copy-start | bytes 90004
  502.5 16.0 %copy-start.15 = (f32[3,2500]{1,0:T(4,128)S(1)}, f32[3,2500]{1,0:T(4,128)}, u32[]{:S(2)}) copy-start(f32[3,2500]{1,0:T(4,128)} %param.50) | copy-start | bytes 90004
  502.5 16.0 %copy-start.16 = (f32[3,2500]{1,0:T(4,128)S(1)}, f32[3,2500]{1,0:T(4,128)}, u32[]{:S(2)}) copy-start(f32[3,2500]{1,0:T(4,128)} %param.42) | copy-start | bytes 90004
  502.5 80.4 %copy-start.19 = (f32[32,128]{1,0:T(8,128)S(1)}, f32[32,128]{1,0:T(8,128)}, u32[]{:S(2)}) copy-start(f32[32,128]{1,0:T(8,128)} %param.43) | copy-start | bytes 49156
  502.5 80.4 %copy-start.20 = (f32[32,128]{1,0:T(8,128)S(1)}, f32[32,128]{1,0:T(8,128)}, u32[]{:S(2)}) copy-start(f32[32,128]{1,0:T(8,128)} %param.51) | copy-start | bytes 49156
  502.5 167.0 %copy-start = (f32[2,128,2500]{1,0,2:T(2,128)S(1)}, f32[2,128,2500]{1,0,2:T(2,128)}, u32[]{:S(2)}) copy-start(f32[2,128,2500]{1,0,2:T(2,128)} %param.33) | copy-start | bytes 7680004
  504.4 80.9 %copy-start.28 = (f32[20]{0:T(128)S(1)}, f32[20]{0:T(128)}, u32[]{:S(2)}) copy-start(f32[20]{0:T(128)} %param.54) | copy-start | bytes 244
  504.4 80.8 %copy-start.29 = (f32[20]{0:T(128)S(1)}, f32[20]{0:T(128)}, u32[]{:S(2)}) copy-start(f32[20]{0:T(128)} %param.46) | copy-start | bytes 244
  504.4 81.4 %copy-start.21 = (f32[128,20]{0,1:T(8,128)S(1)}, f32[128,20]{0,1:T(8,128)}, u32[]{:S(2)}) copy-start(f32[128,20]{0,1:T(8,128)} %param.53) | copy-start | bytes 30724
  504.4 81.4 %copy-start.22 = (f32[128,20]{0,1:T(8,128)S(1)}, f32[128,20]{0,1:T(8,128)}, u32[]{:S(2)}) copy-start(f32[128,20]{0,1:T(8,128)} %param.45) | copy-start | bytes 30724
  504.4 82.0 %copy-start.11 = (f32[42,128]{1,0:T(8,128)S(1)}, f32[42,128]{1,0:T(8,128)}, u32[]{:S(2)}) copy-start(f32[42,128]{1,0:T(8,128)} %param.39) | copy-start | bytes 64516
  504.5 81.9 %copy-start.17 = (f32[42,128]{1,0:T(8,128)S(1)}, f32[42,128]{1,0:T(8,128)}, u32[]{:S(2)}) copy-start(f32[42,128]{1,0:T(8,128)} %param.55) | copy-start | bytes 64516
  504.5 81.9 %copy-start.18 = (f32[42,128]{1,0:T(8,128)S(1)}, f32[42,128]{1,0:T(8,128)}, u32[]{:S(2)}) copy-start(f32[42,128]{1,0:T(8,128)} %param.47) | copy-start | bytes 64516
  682.6 17.7 %copy-start.6 = (f32[2500,128]{1,0:T(8,128)S(1)}, f32[2500,128]{1,0:T(8,128)}, u32[]{:S(2)}) copy-start(f32[2500,128]{1,0:T(8,128)} %get-tuple-element.200) | copy-start | bytes 3840004
  691.5 8.9 %copy-start.2 = (f32[2500,128]{1,0:T(8,128)S(1)}, f32[2500,128]{1,0:T(8,128)}, u32[]{:S(2)}) copy-start(f32[2500,128]{1,0:T(8,128)} %param.32) | copy-start | bytes 3840004
  691.5 8.9 %copy-start.4 = (f32[2500,128]{1,0:T(8,128)S(1)}, f32[2500,128]{1,0:T(8,128)}, u32[]{:S(2)}) copy-start(f32[2500,128]{1,0:T(8,128)} %param.48) | copy-start | bytes 3840004
  691.5 8.9 %copy-start.5 = (f32[2500,128]{1,0:T(8,128)S(1)}, f32[2500,128]{1,0:T(8,128)}, u32[]{:S(2)}) copy-start(f32[2500,128]{1,0:T(8,128)} %param.40) | copy-start | bytes 3840004
Sparse Core Ops, SparseCore 0:
  458.3 124.5 all-reduce.10
  587.2 82.2 all-reduce.12

commit v3 on v2

--- a/solution.py
+++ b/solution.py
@@ -17,7 +17,8 @@
 bf16 = jnp.bfloat16
 LANES = 128
 ROWS = 16
-HOT_DEPTH = 144
+WIDE = 2 * LANES
+HOT_DEPTH = 2 * LANES
 PARAMS = pltpu.CompilerParams(vmem_limit_bytes=60 << 20)
 IN_VMEM = pl.BlockSpec(memory_space=pltpu.VMEM)
 MESH = pl.DeviceIdType.MESH
@@ -33,13 +34,6 @@
     moment = momentum_decay * momentum + grad
     fresh = weight - rate * (grad + momentum_decay * moment)
     return (fresh, moment, average_decay * average + (1.0 - average_decay) * fresh)
-
-
-def three_parts(value):
-    high = lax.reduce_precision(value, 8, 7)
-    rest = value - high
-    middle = lax.reduce_precision(rest, 8, 7)
-    return high, middle, lax.reduce_precision(rest - middle, 8, 7)
 
 
 def whole(array):
@@ -73,8 +67,84 @@
     return jnp.concatenate([piece, filler], axis=0)
 
 
-def encode_kernel(counts_ref, weight_ref, out_ref, inputs_ref, *, genes, chunk):
+def prepare_kernel(
+    output_ref,
+    vectors_ref,
+    weights_ref,
+    theta_ref,
+    log_ref,
+    slope_ref,
+    gammas_ref,
+    digammas_ref,
+    *,
+    genes,
+):
+    block = theta_ref.shape[0]
+    turned = jnp.transpose(
+        jnp.concatenate([vectors_ref[...], jnp.zeros((block - 3, block), f32)], axis=0)
+    )
+    row = pl.program_id(0) * block + lax.broadcasted_iota(jnp.int32, (block, 1), 0)
+    inside = row < genes
+    lane = lax.broadcasted_iota(jnp.int32, (block, LANES), 1)
+    for k in range(2):
+        weight = jnp.where(inside, output_ref[pl.ds(k, block, stride=2), :], 0.0)
+        weights_ref[k, :, 0:LANES] = weight.astype(bf16)
+        bias = jnp.where(inside, turned[:, k : k + 1], 0.0 if k else -1e30)
+        high = bias.astype(bf16).astype(f32)
+        middle = (bias - high).astype(bf16).astype(f32)
+        low = (bias - high - middle).astype(bf16).astype(f32)
+        extra = jnp.where(lane == 0, high, jnp.where(lane == 1, middle, 0.0))
+        extra = jnp.where(lane == 2, low, extra)
+        if k == 0:
+            extra = jnp.where((lane >= 3) & (lane < 6), 1.0, extra)
+        weights_ref[k, :, LANES : 2 * LANES] = extra.astype(bf16)
+    theta = jnp.where(inside, jnp.exp(turned[:, 2:3]), 1.0) + jnp.zeros((block, LANES), f32)
+    log_theta = jnp.log2(theta + rate_epsilon)
+    theta_ref[...] = theta
+    log_ref[...] = log_theta
+    slope_ref[...] = ln2 * log_theta + theta / (theta + rate_epsilon)
+    step = lane.astype(f32)
+    climb = theta + step
+    upper = jnp.where(
+        lax.broadcasted_iota(jnp.int32, (LANES, LANES), 0)
+        < lax.broadcasted_iota(jnp.int32, (LANES, LANES), 1),
+        1.0,
+        0.0,
+    )
+    gammas_ref[...] = exact(jnp.log2(climb / (step + 1.0)), upper, 1, 0)
+    digammas_ref[...] = exact(1.0 / climb, upper, 1, 0)
+
+
+def prepare(output_rows, vectors, genes):
+    size = padded(genes)
+    block = LANES
+    table = pl.BlockSpec((block, LANES), lambda i: (i, 0))
+    return pl.pallas_call(
+        functools.partial(prepare_kernel, genes=genes),
+        grid=(pl.cdiv(size, block),),
+        in_specs=[
+            pl.BlockSpec((2 * block, LANES), lambda i: (i, 0)),
+            pl.BlockSpec((3, block), lambda i: (0, i)),
+        ],
+        out_specs=[pl.BlockSpec((2, block, HOT_DEPTH), lambda i: (0, i, 0))] + [table] * 5,
+        out_shape=[jax.ShapeDtypeStruct((2, size, HOT_DEPTH), bf16)]
+        + [jax.ShapeDtypeStruct((size, LANES), f32)] * 5,
+        compiler_params=PARAMS,
+        name="prepare",
+    )(output_rows, vectors)
+
+
+def encode_kernel(counts_ref, encoder_ref, out_ref, inputs_ref, weight_ref, *, genes, chunk):
     full, groups, tail = split_rows(genes)
+    width = encoder_ref.shape[1]
+
+    @pl.when(pl.program_id(0) == 0)
+    def _():
+        weight_ref[0 : full * ROWS, :] = encoder_ref[0 : full * ROWS, :].astype(bf16)
+        if tail:
+            weight_ref[full * ROWS :, :] = tail_rows(
+                encoder_ref, full * ROWS, genes, slice(None), f32
+            ).astype(bf16)
 
     def group(counted, rows, total):
         inputs_ref[rows, :] = jnp.log(counted + 1.0).astype(bf16)
@@ -89,27 +159,31 @@
         rows = pl.ds(full * ROWS, ROWS)
         counted = tail_rows(counts_ref, full * ROWS, genes, slice(None), jnp.int32).astype(f32)
         total = group(counted, rows, total)
-    width = weight_ref.shape[0]
-    out_ref[0:width, :] = jnp.dot(weight_ref[...], inputs_ref[...], preferred_element_type=f32)
+    out_ref[0:width, :] = lax.dot_general(
+        weight_ref[...], inputs_ref[...], (((0,), (0,)), ((), ())), preferred_element_type=f32
+    )
     row = lax.broadcasted_iota(jnp.int32, (8, chunk), 0)
     library = jnp.sum(total, axis=0, keepdims=True)
     out_ref[width : width + 8, :] = jnp.where(row == 0, library, 0.0)
 
 
-def encode(counts_t, weight_t):
+def encode(counts_t, weight):
     genes, cells = counts_t.shape
     chunk = pick_chunk(cells, 512)
-    width = weight_t.shape[0]
+    width = weight.shape[1]
     return pl.pallas_call(
         functools.partial(encode_kernel, genes=genes, chunk=chunk),
         grid=(cells // chunk,),
-        in_specs=[column_blocks(genes, chunk), whole(weight_t)],
+        in_specs=[column_blocks(genes, chunk), whole(weight)],
         out_specs=column_blocks(width + 8, chunk),
         out_shape=jax.ShapeDtypeStruct((width + 8, cells), f32),
-        scratch_shapes=[pltpu.VMEM((padded(genes), chunk), bf16)],
+        scratch_shapes=[
+            pltpu.VMEM((padded(genes), chunk), bf16),
+            pltpu.VMEM((padded(genes), width), bf16),
+        ],
         compiler_params=PARAMS,
         name="encode",
-    )(counts_t, weight_t)
+    )(counts_t, weight)
 
 
 class Team:
@@ -467,22 +541,50 @@
     stats_ref,
     first_ref,
     heads_ref,
+    output_ref,
+    genes_ref,
     grad16_ref,
     small_ref,
     norms_ref,
+    output_sum_ref,
+    genes_sum_ref,
     part_ref,
     slab_box,
     box1,
     box2,
+    output_box,
+    half_box,
+    half_give,
+    genes_box,
     slab_sems,
     sems1,
     sems2,
     grad_sems,
+    output_sems,
+    genes_sems,
     *,
     batches,
     latent,
 ):
     group, everyone = Team(True), Team(False)
+    cell = lax.axis_index("cell")
+    bit, near, far = lax.rem(cell, 2), cell + 1 - 2 * lax.rem(cell, 2), lax.rem(cell + 2, 4)
+    half = output_ref.shape[1] // 2
+
+    def swap(source, target, other, number):
+        copy = pltpu.make_async_remote_copy(
+            src_ref=source,
+            dst_ref=target,
+            send_sem=output_sems.at[number, 0],
+            recv_sem=output_sems.at[number, 1],
+            device_id=(group.gene, other),
+            device_id_type=MESH,
+        )
+        copy.start()
+        return copy
+
+    def rows_of(number):
+        return pl.ds(pl.multiple_of(number * half, 8), half)
     width, slab = first_ref.shape
     cells = grad_ref.shape[1]
     pad = sample_ref.shape[0]
@@ -493,6 +595,23 @@
         return pl.ds(pl.multiple_of(other * slab, LANES), slab)
 
     mine = part(group.me)
+    everyone.greet()
+    swap1 = swap(output_ref.at[1 - bit], output_box, near, 0)
+    genes_box[cell] = genes_ref[...]
+
+    def tell(step, carry):
+        other = lax.rem(cell + step, group.cells)
+        pltpu.make_async_remote_copy(
+            src_ref=genes_ref,
+            dst_ref=genes_box.at[cell],
+            send_sem=genes_sems.at[0],
+            recv_sem=genes_sems.at[1],
+            device_id=(group.gene, other),
+            device_id_type=MESH,
+        ).start()
+        return carry
+
+    lax.fori_loop(1, group.cells, tell, 0)
     inverse1, inverse2 = stats_ref[0:1, :], stats_ref[1:2, :]
     count, scale = stats_ref[2:3, 0:1], stats_ref[3:4, 0:1]
     factor2 = inverse2 * pack_ref[2:3, :]
@@ -521,7 +640,6 @@
     gains, shifts, products = lax.fori_loop(
         0, cells // piece, gather, (zeros, zeros, jnp.zeros((depth, width), f32))
     )
-    everyone.greet()
 
     def reduced(rows, box, sems):
         box[everyone.me] = eight_rows(rows)
@@ -538,6 +656,11 @@
     finish = reduced([row_sums(gains), row_sums(shifts)], box1, sems1)
     group.send(lambda other: part_ref.at[:, part(other)], slab_box.at[group.me], slab_sems)
     slab_box[group.me] = part_ref[:, mine]
+    swap1.wait()
+    own, given = rows_of(far // 2), rows_of(cell // 2)
+    half_give[...] = output_ref[bit, own] + output_box[own]
+    swap2 = swap(half_give, half_box, far, 1)
+    output_sum_ref[bit, given] = output_ref[bit, given] + output_box[given]
     hot = hot_rows(index_ref[:, mine], batches)
     valid = valid_ref[:, mine].astype(f32)
     mixed = valid * jnp.concatenate([sample_ref[:, mine], hot], axis=0)
@@ -576,6 +699,9 @@
         box2,
         sems2,
     )
+    swap2.wait()
+    output_sum_ref[bit, given] = output_sum_ref[bit, given] + half_box[...]
+    swap3 = swap(output_sum_ref.at[bit, given], output_sum_ref.at[bit, given], far, 2)
     small_ref[depth : depth + 2 * pad, :] = exact(grad_heads, hidden1, 1, 1)
     small_ref[depth + 2 * pad : depth + 4 * pad, :] = fold_lanes(grad_heads)
     sums = finish()
@@ -586,12 +712,33 @@
     grad16_ref[:, mine] = grad_pre1.astype(bf16)
     group.send(lambda other: grad16_ref.at[:, mine], grad16_ref.at[:, mine], grad_sems)
     small_ref[depth + 4 * pad :, :] = exact(hot, grad_pre1, 1, 1)
+    others = genes_box.at[pl.ds(0, group.cells - 1)]
+    await_bytes(others, genes_sems.at[0])
+    await_bytes(others, genes_sems.at[1])
+    genes_sum_ref[...] = box_sum(genes_box)
+    swap3.wait()
+    swap4 = swap(output_sum_ref.at[bit], output_sum_ref.at[bit], near, 3)
+    swap4.wait()
     others = grad16_ref.at[:, pl.ds(0, (group.size - 1) * slab)]
     await_bytes(others, grad_sems.at[0])
     await_bytes(others, grad_sems.at[1])
 
 
-def middle_back(grad, centered, sample, index, valid, noise, pack, stats, first, heads, batches):
+def middle_back(
+    grad,
+    centered,
+    sample,
+    index,
+    valid,
+    noise,
+    pack,
+    stats,
+    first,
+    heads,
+    output_grad,
+    genes_grad,
+    batches,
+):
     cells = index.shape[1]
     width, slab = first.shape
     pad = sample.shape[0]
@@ -603,19 +750,172 @@
             jax.ShapeDtypeStruct((width, cells), bf16),
             jax.ShapeDtypeStruct((5 * pad + 2 * batches, LANES), f32),
             jax.ShapeDtypeStruct((8, LANES), f32),
+            jax.ShapeDtypeStruct(output_grad.shape, f32),
+            jax.ShapeDtypeStruct(genes_grad.shape, f32),
         ],
-        in_specs=[IN_VMEM] * 10,
-        out_specs=[IN_VMEM] * 3,
+        in_specs=[IN_VMEM] * 12,
+        out_specs=[IN_VMEM] * 5,
         scratch_shapes=[
             pltpu.VMEM((pad, cells), f32),
             pltpu.VMEM((genes_axis, pad, slab), f32),
             pltpu.VMEM((devices, 8, LANES), f32),
             pltpu.VMEM((devices, 8, LANES), f32),
+            pltpu.VMEM(output_grad.shape[1:], f32),
+            pltpu.VMEM((output_grad.shape[1] // 2, LANES), f32),
+            pltpu.VMEM((output_grad.shape[1] // 2, LANES), f32),
+            pltpu.VMEM((devices // genes_axis, *genes_grad.shape), f32),
         ]
-        + [pltpu.SemaphoreType.DMA((2,))] * 4,
+        + [pltpu.SemaphoreType.DMA((2,))] * 4
+        + [pltpu.SemaphoreType.DMA((4, 2)), pltpu.SemaphoreType.DMA((2,))],
         compiler_params=talking(4),
         name="middle_back",
-    )(grad, centered, sample, index, valid, noise, pack, stats, first, heads)
+    )(
+        grad,
+        centered,
+        sample,
+        index,
+        valid,
+        noise,
+        pack,
+        stats,
+        first,
+        heads,
+        output_grad,
+        genes_grad,
+    )
+
+
+def last_sums_kernel(
+    grad_ref, small_ref, sum_ref, total_ref, box, half_box, half_give, small_box, sems, small_sems
+):
+    group, everyone = Team(True), Team(False)
+    cell = lax.axis_index("cell")
+    bit, near, far = lax.rem(cell, 2), cell + 1 - 2 * lax.rem(cell, 2), lax.rem(cell + 2, 4)
+    high = cell // 2
+    size = grad_ref.shape[0]
+    half, quarter = size // 2, size // 4
+    everyone.greet()
+
+    def swap(source, target, other, sems):
+        copy = pltpu.make_async_remote_copy(
+            src_ref=source,
+            dst_ref=target,
+            send_sem=sems.at[0],
+            recv_sem=sems.at[1],
+            device_id=other,
+            device_id_type=MESH,
+        )
+        copy.start()
+        return copy
+
+    total_ref[...] = small_ref[...]
+    rounds = []
+    for step in (1, 2):
+        other = near if step == 1 else far
+        rounds.append((group.gene, other))
+    step = 1
+    while step < group.genes:
+        flip = group.gene + step - 2 * step * lax.rem(group.gene // step, 2)
+        rounds.append((flip, cell))
+        step *= 2
+
+    def small_round(number):
+        source = small_ref if number == 0 else small_box.at[1, number - 1]
+        return swap(source, small_box.at[0, number], rounds[number], small_sems.at[number])
+
+    def small_end(copy, number):
+        copy.wait()
+        source = small_ref[...] if number == 0 else small_box[1, number - 1]
+        small_box[1, number] = source + small_box[0, number]
+
+    def half_of(number):
+        return pl.ds(pl.multiple_of(number * half, 8), half)
+
+    def quarter_of(number):
+        return pl.ds(pl.multiple_of(bit * half + number * quarter, 8), quarter)
+
+    copy = swap(grad_ref.at[half_of(1 - bit)], box, (group.gene, near), sems.at[0])
+    small = small_round(0)
+    copy.wait()
+
+    def inside(number):
+        return pl.ds(pl.multiple_of(number * quarter, 8), quarter)
+
+    half_give[...] = grad_ref[quarter_of(1 - high), :] + box[inside(1 - high), :]
+    copy = swap(half_give, half_box, (group.gene, far), sems.at[1])
+    small_end(small, 0)
+    small = small_round(1)
+    small_end(small, 1)
+    small = small_round(2)
+    copy.wait()
+    mine = quarter_of(high)
+    sum_ref[mine, :] = grad_ref[mine, :] + box[inside(high), :] + half_box[...]
+    copy = swap(sum_ref.at[mine], sum_ref.at[mine], (group.gene, far), sems.at[2])
+    small_end(small, 2)
+    for number in range(3, len(rounds)):
+        small_end(small_round(number), number)
+    total_ref[...] = small_box[1, len(rounds) - 1]
+    copy.wait()
+    copy = swap(sum_ref.at[half_of(bit)], sum_ref.at[half_of(bit)], (group.gene, near), sems.at[3])
+    copy.wait()
+
+
+def last_sums(grad, small):
+    rounds = 2
+    while 2 ** (rounds - 2) < lax.axis_size("gene"):
+        rounds += 1
+    size = grad.shape[0]
+    return pl.pallas_call(
+        last_sums_kernel,
+        out_shape=[
+            jax.ShapeDtypeStruct(grad.shape, f32),
+            jax.ShapeDtypeStruct(small.shape, f32),
+        ],
+        in_specs=[IN_VMEM] * 2,
+        out_specs=[IN_VMEM] * 2,
+        scratch_shapes=[
+            pltpu.VMEM((size // 2, LANES), f32),
+            pltpu.VMEM((size // 4, LANES), f32),
+            pltpu.VMEM((size // 4, LANES), f32),
+            pltpu.VMEM((2, rounds, *small.shape), f32),
+            pltpu.SemaphoreType.DMA((4, 2)),
+            pltpu.SemaphoreType.DMA((rounds, 2)),
+        ],
+        compiler_params=talking(5),
+        name="last_sums",
+    )(grad, small)
+
+
+def update_kernel(*refs):
+    groups, outs = refs[:8], refs[8:]
+    encoder, output = groups[:4], groups[4:]
+    fresh, moment, mean = nesterov(*[ref[...] for ref in encoder], step_rates[0])
+    for ref, value in zip(outs[:3], (fresh, moment, mean)):
+        ref[...] = value
+    rows = output[3].shape[1]
+    for k in range(2):
+        here = pl.ds(k, rows, stride=2)
+        old = [ref[here, :] for ref in output[:3]]
+        for ref, value in zip(outs[3:], nesterov(*old, output[3][k], step_rates[1])):
+            ref[here, :] = value
+
+
+def update(encoder, encoder_grad, output, output_grad):
+    genes = encoder[0].shape[0]
+    block = 2 * LANES
+    one = pl.BlockSpec((block, LANES), lambda i: (i, 0))
+    two = pl.BlockSpec((2 * block, LANES), lambda i: (i, 0))
+    both = pl.BlockSpec((2, block, LANES), lambda i: (0, i, 0))
+    return pl.pallas_call(
+        update_kernel,
+        grid=(pl.cdiv(genes, block),),
+        in_specs=[one] * 4 + [two] * 3 + [both],
+        out_specs=[one] * 3 + [two] * 3,
+        out_shape=[jax.ShapeDtypeStruct(encoder[0].shape, f32)] * 3
+        + [jax.ShapeDtypeStruct(output[0].shape, f32)] * 3,
+        compiler_params=PARAMS,
+        name="update",
+    )(*encoder, encoder_grad, *output, output_grad)
 
 
 def fill_hidden(long_ref, hidden_ref, top):
@@ -633,44 +933,100 @@
     long_ref[width:HOT_DEPTH, :] = extra.astype(bf16)
 
 
-def totals_kernel(hidden_ref, weight_ref, out_ref, long_ref, value_ref, *, chunk):
-    size = weight_ref.shape[0]
+def sweep(blocks, block, groups, pieces, logits, terms, back, carry):
+    def rows_of(number):
+        return pl.ds(pl.multiple_of(number * block, ROWS), block)
+
+    logits(0, rows_of(0), block, pieces)
+
+    def beside(i, later, earlier):
+        acts = [
+            lambda piece=piece: logits(1 - i, rows_of(later), block, [piece]) for piece in pieces
+        ]
+        if back is not None:
+            acts.append(lambda: back(1 - i, rows_of(earlier), block))
+        spaced = []
+        for step in range(groups):
+            spaced.append(acts.pop(0) if acts and step % 2 == 0 else lambda: None)
+        return spaced + acts
+
+    def pair(p, carry):
+        first = 2 * p
+        last, ahead = jnp.maximum(first - 1, 0), jnp.minimum(first + 2, blocks - 1)
+        carry = terms(0, first, carry, beside(0, first + 1, last))
+        return terms(1, first + 1, carry, beside(1, ahead, first))
+
+    carry = lax.fori_loop(0, blocks // 2, pair, carry)
+    if back is not None and blocks > 1:
+        back(1, rows_of(blocks // 2 * 2 - 1), block)
+    if blocks % 2:
+        carry = terms(0, blocks - 1, carry, ())
+        if back is not None:
+            back(0, rows_of(blocks - 1), block)
+    return carry
+
+
+def logit_pieces(ks, chunk):
+    width = min(chunk, WIDE)
+    return [(k, slice(j, j + width)) for k in range(ks) for j in range(0, chunk, width)]
+
+
+def totals_kernel(hidden_ref, weight_ref, out_ref, long_ref, even_ref, odd_ref, *, genes, chunk):
+    full, groups, tail = split_rows(genes)
+    block = ROWS * groups
+    blocks = full // groups
+    values = (even_ref, odd_ref)
     fill_hidden(long_ref, hidden_ref, None)
-    value_ref[...] = jnp.dot(weight_ref[...], long_ref[...], preferred_element_type=f32)
-    count = size // ROWS
-
-    def highest(i, best):
-        part = value_ref[pl.ds(pl.multiple_of(i * ROWS, ROWS), ROWS), :]
-        return jnp.maximum(best, jnp.maximum(part[:8], part[8:]))
-
-    best = lax.fori_loop(0, count, highest, jnp.full((8, chunk), -jnp.inf, f32), unroll=4)
+    pieces = logit_pieces(1, chunk)
+
+    def logits(i, rows, size, which):
+        for _, columns in which:
+            values[i][0:size, columns] = jnp.dot(
+                weight_ref[0, rows, :], long_ref[:, columns], preferred_element_type=f32
+            )
+
+    def online(value_ref, size, carry, beside=()):
+        best, total = carry
+        fresh = best
+        for i in range(0, size, 8):
+            fresh = jnp.maximum(fresh, value_ref[i : i + 8, :])
+        total = total * jnp.exp2((best - fresh) * (1.0 / ln2))
+        for i in range(0, size, 8):
+            for act in beside[i // 8 :: size // 8]:
+                act()
+            total = total + jnp.exp2((value_ref[i : i + 8, :] - fresh) * (1.0 / ln2))
+        return fresh, total
+
+    def terms(i, number, carry, beside):
+        return online(values[i], block, carry, beside)
+
+    carry = (jnp.full((8, chunk), -jnp.inf, f32), jnp.zeros((8, chunk), f32))
+    carry = sweep(blocks, block, groups, pieces, logits, terms, None, carry)
+    if tail:
+        logits(1, pl.ds(full * ROWS, ROWS), ROWS, pieces)
+        carry = online(odd_ref, ROWS, carry)
+    best, total = carry
     top = jnp.max(best, axis=0, keepdims=True)
-
-    def add(i, total):
-        part = jnp.exp(value_ref[pl.ds(pl.multiple_of(i * ROWS, ROWS), ROWS), :] - top)
-        return total + part[:8] + part[8:]
-
-    total = lax.fori_loop(0, count, add, jnp.zeros((8, chunk), f32), unroll=4)
+    total = total * jnp.exp2((best - top) * (1.0 / ln2))
     out_ref[0:1, :] = top
     out_ref[1:2, :] = jnp.sum(total, axis=0, keepdims=True)
 
 
-def totals(hidden, weight):
+def totals(hidden, weights, genes):
     width, cells = hidden.shape
     chunk = pick_chunk(cells, 512)
+    groups = split_rows(genes)[1]
     return pl.pallas_call(
-        functools.partial(totals_kernel, chunk=chunk),
+        functools.partial(totals_kernel, genes=genes, chunk=chunk),
         grid=(cells // chunk,),
-        in_specs=[column_blocks(width, chunk), whole(weight)],
+        in_specs=[column_blocks(width, chunk), whole(weights)],
         out_specs=column_blocks(2, chunk),
         out_shape=jax.ShapeDtypeStruct((2, cells), f32),
-        scratch_shapes=[
-            pltpu.VMEM((HOT_DEPTH, chunk), bf16),
-            pltpu.VMEM((weight.shape[0], chunk), f32),
-        ],
+        scratch_shapes=[pltpu.VMEM((HOT_DEPTH, chunk), bf16)]
+        + [pltpu.VMEM((ROWS * groups, chunk), f32)] * 2,
         compiler_params=PARAMS,
         name="totals",
-    )(hidden, weight)
+    )(hidden, weights)
 
 
 def likelihood_kernel(
@@ -679,11 +1035,11 @@
     rows_ref,
     share_ref,
     weight_ref,
-    back_ref,
     theta_ref,
     log_ref,
     slope_ref,
-    table_ref,
+    gammas_ref,
+    digammas_ref,
     slopes_ref,
     sums_ref,
     grad_hidden_ref,
@@ -691,14 +1047,17 @@
     grad_bias_ref,
     grad_theta_ref,
     long_ref,
-    value_ref,
-    second_ref,
+    even_ref,
+    odd_ref,
+    even_grad_ref,
+    odd_grad_ref,
     *,
     genes,
     chunk,
 ):
     full, groups, tail = split_rows(genes)
     block = ROWS * groups
+    blocks = full // groups
     width = hidden_ref.shape[0]
 
     @pl.when(pl.program_id(0) == 0)
@@ -707,103 +1066,126 @@
             ref[...] = jnp.zeros_like(ref)
 
     fill_hidden(long_ref, hidden_ref, rows_ref[0:1, :])
-    tiles = [slice(j, j + LANES) for j in range(0, chunk, LANES)]
+    wide = min(WIDE, chunk)
+    tiles = [slice(j, j + wide) for j in range(0, chunk, wide)]
     ratio_all = rows_ref[1:2, :]
     share_all = share_ref[...]
 
-    def group(held, rows, read, carry):
+    def two(x):
+        return jnp.concatenate([x] * (wide // LANES), axis=1)
+
+    def look(t, c):
+        return jnp.concatenate([jnp.take_along_axis(t, c[:, q:q+LANES], axis=1) for q in range(0, wide, LANES)], axis=1)
+
+    def group(value_ref, grad_ref, held, span, read, carry):
         losses, sums = [], []
-        theta = theta_ref[rows, :]
-        log_theta = log_ref[rows, :]
-        log_slope = slope_ref[rows, :]
-        table = table_ref[rows, :]
-        grad_bias = grad_bias_ref[rows, :]
-        grad_theta = grad_theta_ref[rows, :]
+        theta = two(theta_ref.at[span][held, :])
+        log_theta = two(log_ref.at[span][held, :])
+        log_slope = two(slope_ref.at[span][held, :])
+        gammas = gammas_ref.at[span][held, :]
+        digammas = digammas_ref.at[span][held, :]
+        grad_bias = grad_bias_ref.at[span][held, :]
+        grad_theta = grad_theta_ref.at[span][held, :]
         for j, columns in enumerate(tiles):
             count = read(columns)
             counted = count.astype(f32)
-            first = value_ref[0, held, columns]
-            dropout = value_ref[1, held, columns]
-            ratio, share = ratio_all[:, columns], share_all[:, columns]
-            rate = jnp.exp(first) * ratio
+            minus = value_ref[1, held, columns] * (-1.0 / ln2)
+            share = share_all[:, columns]
+            rate = jnp.exp2(value_ref[0, held, columns] * (1.0 / ln2)) * ratio_all[:, columns]
             near = rate + rate_epsilon
             both = theta + near
-            inverse = pl.reciprocal(near * both)
-            inverse_both = inverse * near
-            inverse_near = inverse * both
-            log_fraction = jnp.log2(near * inverse_both)
+            inverse_both = 1.0 / both
             log_both = jnp.log2(both)
-            pi_theta = (theta * ln2) * (log_theta - log_both) - dropout
-            small_pi = jnp.exp(-jnp.abs(dropout))
-            small_theta = jnp.exp(-jnp.abs(pi_theta))
-            one_pi = 1.0 + small_pi
-            one_theta = 1.0 + small_theta
-            inverse_ones = pl.reciprocal(one_pi * one_theta)
-            sigma_pi = jnp.where(dropout >= 0.0, small_pi, 1.0) * (inverse_ones * one_theta)
-            inverse_theta = inverse_ones * one_pi
+            upper = jnp.maximum(minus, 0.0)
+            lower = jnp.minimum(minus, 0.0)
+            one_pi = 1.0 + jnp.exp2(lower - upper)
+            sigma_pi = jnp.exp2(lower) * (1.0 / one_pi)
             zero = count < 1
-            sigma_theta = jnp.where(pi_theta >= 0.0, 1.0, small_theta) * inverse_theta
-            sigma = jnp.where(zero, sigma_theta, 1.0)
-            log_ones = jnp.log2(one_pi * jnp.where(zero, inverse_theta, 1.0))
-            upper = jnp.where(zero, jnp.maximum(pi_theta, 0.0), pi_theta)
-            gammas = jnp.take_along_axis(table, count, axis=1)
-            digammas = jnp.take_along_axis(table, count + LANES // 2, axis=1)
-            loss = (jnp.maximum(-dropout, 0.0) - upper) + (
-                ln2 * (log_ones - counted * log_fraction) - gammas
+            pi_theta = theta * (log_theta - log_both) + minus
+            inflated = jnp.where(zero, pi_theta, 1e30)
+            small = jnp.exp2(-jnp.abs(inflated))
+            inverse_theta = 1.0 / (1.0 + small)
+            sigma = jnp.where(inflated >= 0.0, 1.0, small) * inverse_theta
+            loss = (upper - jnp.where(zero, jnp.maximum(pi_theta, 0.0), pi_theta)) + (
+                jnp.log2(one_pi * inverse_theta)
+                - counted * (jnp.log2(near) - log_both)
+                - look(gammas, count)
             )
             pull = (sigma * theta + counted) * inverse_both
-            slope = rate * (pull - counted * inverse_near)
-            slopes_ref[rows, columns] = slope
+            slope = rate * (pull - counted * (1.0 / near))
+            slopes_ref.at[span][held, columns] = slope
             grad_dropout = (sigma - sigma_pi) * share
-            second_ref[rows, columns] = grad_dropout.astype(bf16)
-            grad_bias = grad_bias + grad_dropout
-            grad_theta = grad_theta + share * (
-                pull - ln2 * (sigma * (log_slope - log_both)) - digammas
-            )
+            grad_ref[held, columns] = grad_dropout.astype(bf16)
+            grad_bias = grad_bias + fold_lanes(grad_dropout)
+            grad_theta = grad_theta + fold_lanes(share * (
+                (pull - sigma * (log_slope - ln2 * log_both))
+                - look(digammas, count)
+            ))
             losses.append(carry[0][j] + loss[:8] + loss[8:])
             sums.append(carry[1][j] + slope[:8] + slope[8:])
-        grad_bias_ref[rows, :] = grad_bias
-        grad_theta_ref[rows, :] = grad_theta
+        grad_bias_ref.at[span][held, :] = grad_bias
+        grad_theta_ref.at[span][held, :] = grad_theta
         return tuple(losses), tuple(sums)
 
-    def logits(rows, size):
-        for k in range(2):
-            value_ref[k, 0:size, :] = jnp.dot(
-                weight_ref[k, rows, :], long_ref[...], preferred_element_type=f32
+    pieces = logit_pieces(2, chunk)
+    values, grads = (even_ref, odd_ref), (even_grad_ref, odd_grad_ref)
+
+    def logits(i, rows, size, which):
+        for k, columns in which:
+            values[i][k, 0:size, columns] = jnp.dot(
+                weight_ref[k, rows, :], long_ref[:, columns], preferred_element_type=f32
             )
 
-    def step(b, carry):
-        start = pl.multiple_of(b * block, ROWS)
-        logits(pl.ds(start, block), block)
-
-        def inner(i, carry):
-            held = pl.multiple_of(i * ROWS, ROWS)
-            rows = pl.ds(pl.multiple_of(start + held, ROWS), ROWS)
-            return group(pl.ds(held, ROWS), rows, lambda cols: counts_ref[rows, cols], carry)
-
-        return lax.fori_loop(0, groups, inner, carry, unroll=4)
-
-    zeros = tuple(jnp.zeros((8, LANES), f32) for _ in tiles)
-    carry = lax.fori_loop(0, full // groups, step, (zeros, zeros))
+    def back(i, rows, size):
+        grad = grads[i][0:size, :]
+        grad_weight_ref[rows, :] += lax.dot_general(
+            grad, hidden_ref[...], (((1,), (1,)), ((), ())), preferred_element_type=f32
+        )
+        grad_hidden_ref[...] += lax.dot_general(
+            weight_ref[1, rows, 0:width],
+            grad,
+            (((0,), (0,)), ((), ())),
+            preferred_element_type=f32,
+        )
+
+    def terms(buffer, number, carry, beside):
+        span = pl.ds(pl.multiple_of(number * block, ROWS), block)
+        for i in range(groups):
+            for act in beside[i::groups]:
+                act()
+            held = slice(i * ROWS, (i + 1) * ROWS)
+            carry = group(
+                values[buffer],
+                grads[buffer],
+                held,
+                span,
+                lambda columns, held=held: counts_ref.at[span][held, columns],
+                carry,
+            )
+        return carry
+
+    grad_hidden_ref[...] = jnp.zeros_like(grad_hidden_ref)
+    odd_grad_ref[...] = jnp.zeros_like(odd_grad_ref)
+    carry = tuple(jnp.zeros((8, wide), f32) for _ in tiles)
+    carry = sweep(blocks, block, groups, pieces, logits, terms, back, (carry, carry))
     if tail:
         rows = pl.ds(full * ROWS, ROWS)
-        logits(rows, ROWS)
+        logits(1, rows, ROWS, pieces)
         carry = group(
-            pl.ds(0, ROWS),
+            odd_ref,
+            odd_grad_ref,
+            slice(0, ROWS),
             rows,
             lambda cols: tail_rows(counts_ref, full * ROWS, genes, cols, jnp.int32),
             carry,
         )
+        back(1, rows, ROWS)
     for j, columns in enumerate(tiles):
         sums_ref[0:1, columns] = jnp.sum(carry[1][j], axis=0, keepdims=True)
-        sums_ref[1:2, columns] = jnp.sum(carry[0][j], axis=0, keepdims=True)
-    grad_weight_ref[...] += lax.dot_general(
-        second_ref[...], hidden_ref[...], (((1,), (1,)), ((), ())), preferred_element_type=f32
-    )
-    grad_hidden_ref[...] = jnp.dot(back_ref[...], second_ref[...], preferred_element_type=f32)
-
-
-def likelihood(counts_t, hidden, rows, share, weights, back, gene_tables):
+        sums_ref[1:2, columns] = jnp.sum(carry[0][j], axis=0, keepdims=True) * ln2
+
+
+def likelihood(counts_t, hidden, rows, share, weights, gene_tables):
     genes, cells = counts_t.shape
     size = weights.shape[1]
     width = hidden.shape[0]
@@ -815,7 +1197,7 @@
         functools.partial(likelihood_kernel, genes=genes, chunk=chunk),
         grid=(cells // chunk,),
         in_specs=[column_blocks(genes, chunk), column_blocks(width, chunk)]
-        + [column_blocks(rows.shape[0], chunk), row, whole(weights), whole(back)]
+        + [column_blocks(rows.shape[0], chunk), row, whole(weights)]
         + [whole(a) for a in gene_tables],
         out_specs=[
             column_blocks(size, chunk),
@@ -829,14 +1211,12 @@
             jax.ShapeDtypeStruct((width, cells), f32),
         ]
         + [jax.ShapeDtypeStruct((size, LANES), f32)] * 3,
-        scratch_shapes=[
-            pltpu.VMEM((HOT_DEPTH, chunk), bf16),
-            pltpu.VMEM((2, ROWS * groups, chunk), f32),
-            pltpu.VMEM((size, chunk), bf16),
-        ],
+        scratch_shapes=[pltpu.VMEM((HOT_DEPTH, chunk), bf16)]
+        + [pltpu.VMEM((2, ROWS * groups, chunk), f32)] * 2
+        + [pltpu.VMEM((ROWS * groups, chunk), bf16)] * 2,
         compiler_params=PARAMS,
         name="likelihood",
-    )(counts_t, hidden, rows, share, weights, back, *gene_tables)
+    )(counts_t, hidden, rows, share, weights, *gene_tables)
 
 
 def frequency_kernel(
@@ -847,73 +1227,121 @@
     share_ref,
     other_ref,
     weight_ref,
-    back_ref,
+    second_ref,
+    dropout_ref,
+    theta_ref,
+    scale_ref,
     grad_hidden_ref,
     grad_weight_ref,
+    genes_ref,
+    long_ref,
+    even_ref,
+    odd_ref,
+    even_grad_ref,
+    odd_grad_ref,
     grad_bias_ref,
-    long_ref,
-    value_ref,
-    first_ref,
     *,
+    genes,
     chunk,
 ):
-    size = weight_ref.shape[0]
+    full, groups, tail = split_rows(genes)
+    block = ROWS * groups
+    blocks = full // groups
+    size = weight_ref.shape[1]
+    width = hidden_ref.shape[0]
+    values, grads = (even_ref, odd_ref), (even_grad_ref, odd_grad_ref)
 
     @pl.when(pl.program_id(0) == 0)
     def _():
-        for ref in (grad_weight_ref, grad_bias_ref):
-            ref[...] = jnp.zeros_like(ref)
+        grad_weight_ref[0] = jnp.zeros((size, LANES), f32)
+        grad_weight_ref[1] = second_ref[...]
+        grad_bias_ref[...] = jnp.zeros_like(grad_bias_ref)
 
     fill_hidden(long_ref, hidden_ref, rows_ref[0:1, :])
-    value_ref[...] = jnp.dot(weight_ref[...], long_ref[...], preferred_element_type=f32)
-    tiles = [slice(j, j + LANES) for j in range(0, chunk, LANES)]
-    pull_all = pull_ref[0:1, :]
-    share_all = share_ref[...]
-
-    def step(i, carry):
-        rows = pl.ds(pl.multiple_of(i * ROWS, ROWS), ROWS)
-        bias = grad_bias_ref[rows, :]
-        for columns in tiles:
-            grad = share_all[:, columns] * (
-                slopes_ref[rows, columns] - jnp.exp(value_ref[rows, columns]) * pull_all[:, columns]
+    pieces = logit_pieces(1, chunk)
+    share = share_ref[...]
+    pulled = pull_ref[0:1, :] * share
+
+    def logits(i, rows, size, which):
+        for _, columns in which:
+            values[i][0:size, columns] = jnp.dot(
+                weight_ref[0, rows, :], long_ref[:, columns], preferred_element_type=f32
             )
-            first_ref[rows, columns] = grad.astype(bf16)
-            bias = bias + grad
-        grad_bias_ref[rows, :] = bias
+
+    def group(buffer, held, span):
+        exponent = jnp.exp2(values[buffer][held, :] * (1.0 / ln2))
+        grad = slopes_ref.at[span][held, :] * share - exponent * pulled
+        grads[buffer][held, :] = grad.astype(bf16)
+        grad_bias_ref.at[span][held, :] += fold_lanes(grad)
+
+    def terms(buffer, number, carry, beside):
+        span = pl.ds(pl.multiple_of(number * block, ROWS), block)
+        for i in range(groups):
+            for act in beside[i::groups]:
+                act()
+            group(buffer, slice(i * ROWS, (i + 1) * ROWS), span)
         return carry
 
-    lax.fori_loop(0, size // ROWS, step, 0, unroll=2)
-    grad_weight_ref[...] += lax.dot_general(
-        first_ref[...], hidden_ref[...], (((1,), (1,)), ((), ())), preferred_element_type=f32
-    )
-    grad_hidden_ref[...] = other_ref[...] + jnp.dot(
-        back_ref[...], first_ref[...], preferred_element_type=f32
-    )
-
-
-def frequency(slopes, hidden, rows, pull, share, other, weight, back):
+    def back(i, rows, size):
+        grad = grads[i][0:size, :]
+        grad_weight_ref[0, rows, :] += lax.dot_general(
+            grad, hidden_ref[...], (((1,), (1,)), ((), ())), preferred_element_type=f32
+        )
+        grad_hidden_ref[...] += lax.dot_general(
+            weight_ref[0, rows, 0:width],
+            grad,
+            (((0,), (0,)), ((), ())),
+            preferred_element_type=f32,
+        )
+
+    grad_hidden_ref[...] = other_ref[...]
+    odd_grad_ref[...] = jnp.zeros_like(odd_grad_ref)
+    sweep(blocks, block, groups, pieces, logits, terms, back, 0)
+    if tail:
+        rows = pl.ds(full * ROWS, ROWS)
+        logits(1, rows, ROWS, pieces)
+        group(1, slice(0, ROWS), rows)
+        back(1, rows, ROWS)
+
+    @pl.when(pl.program_id(0) == pl.num_programs(0) - 1)
+    def _():
+        ones = jnp.ones((8, LANES), f32)
+        parts = (grad_bias_ref[...], dropout_ref[...], theta_ref[...] * scale_ref[...])
+        for i, values in enumerate(parts):
+            genes_ref[i : i + 1, :] = exact(ones, values, 1, 1)[0:1]
+        genes_ref[3:4, :] = jnp.zeros((1, size), f32)
+
+
+def frequency(slopes, hidden, rows, pull, share, other, weights, second, dropout, theta, scale, genes):
     size, cells = slopes.shape
     width = hidden.shape[0]
     chunk = pick_chunk(cells, 512)
+    groups = split_rows(genes)[1]
     row = column_blocks(1, chunk)
     wide = column_blocks(width, chunk)
-    per_gene = pl.BlockSpec((size, LANES), lambda i: (0, 0))
     return pl.pallas_call(
-        functools.partial(frequency_kernel, chunk=chunk),
+        functools.partial(frequency_kernel, genes=genes, chunk=chunk),
         grid=(cells // chunk,),
         in_specs=[column_blocks(size, chunk), wide, column_blocks(rows.shape[0], chunk)]
-        + [column_blocks(2, chunk), row, wide, whole(weight), whole(back)],
-        out_specs=[wide, per_gene, per_gene],
-        out_shape=[jax.ShapeDtypeStruct((width, cells), f32)]
-        + [jax.ShapeDtypeStruct((size, LANES), f32)] * 2,
-        scratch_shapes=[
-            pltpu.VMEM((HOT_DEPTH, chunk), bf16),
-            pltpu.VMEM((size, chunk), f32),
-            pltpu.VMEM((size, chunk), bf16),
+        + [column_blocks(2, chunk), row, wide, whole(weights)]
+        + [whole(a) for a in (second, dropout, theta, scale)],
+        out_specs=[
+            wide,
+            pl.BlockSpec((2, size, LANES), lambda i: (0, 0, 0)),
+            pl.BlockSpec((4, size), lambda i: (0, 0)),
         ],
+        out_shape=[
+            jax.ShapeDtypeStruct((width, cells), f32),
+            jax.ShapeDtypeStruct((2, size, LANES), f32),
+            jax.ShapeDtypeStruct((4, size), f32),
+        ],
+        scratch_shapes=[pltpu.VMEM((HOT_DEPTH, chunk), bf16)]
+        + [pltpu.VMEM((ROWS * groups, chunk), f32)] * 2
+        + [pltpu.VMEM((ROWS * groups, chunk), bf16)] * 2
+        + [pltpu.VMEM((size, LANES), f32)],
         compiler_params=PARAMS,
         name="frequency",
-    )(slopes, hidden, rows, pull, share, other, weight, back)
+    )(slopes, hidden, rows, pull, share, other, weights, second, dropout, theta, scale)
 
 
 def encoder_back_kernel(counts_ref, grad_ref, weight_ref, input_ref, weight_grad_ref):
@@ -921,10 +1349,12 @@
     weight_grad_ref[...] = lax.dot_general(
         inputs, grad_ref[...], (((1,), (1,)), ((), ())), preferred_element_type=f32
     )
-    input_ref[...] = jnp.dot(weight_ref[...], grad_ref[...], preferred_element_type=f32)
-
-
-def encoder_back(counts_t, grad, weight16):
+    input_ref[...] = jnp.dot(
+        weight_ref[...].astype(bf16), grad_ref[...], preferred_element_type=f32
+    )
+
+
+def encoder_back(counts_t, grad, weight):
     genes, cells = counts_t.shape
     width = grad.shape[0]
     block = LANES
@@ -942,11 +1372,11 @@
         ],
         out_shape=[
             jax.ShapeDtypeStruct((genes, cells), f32),
-            jax.ShapeDtypeStruct((genes, width), f32),
+            jax.ShapeDtypeStruct((-(-genes // 32) * 32, width), f32),
         ],
         compiler_params=PARAMS,
         name="encoder_back",
-    )(counts_t, grad, weight16)
+    )(counts_t, grad, weight)
 
 
 def local(
@@ -984,43 +1414,13 @@
     genes_all = genes * gene_devices
     latent = head_bias.shape[0] // 2
     batches = batch_shift.shape[0]
-    size = padded(genes)
-    gap = size - genes
+
+    def by_gene(array):
+        return jnp.transpose(array, (2, 0, 1)).reshape(2 * genes, -1)
+
     counts_t = counts.T
-    weight16 = encoder_weight.astype(bf16)
-    encoder_t = jnp.pad(weight16, ((0, gap), (0, 0))).T
-
-    theta = jnp.pad(jnp.exp(gene_vectors[2]), (0, gap), constant_values=1.0)
-    log_theta = jnp.log2(theta + rate_epsilon)
-
-    def spread(column):
-        return jnp.broadcast_to(column[:, None], (size, LANES))
-
-    steps = jnp.arange(LANES // 2, dtype=f32)[None, :]
-    column = theta[:, None]
-    table = jnp.concatenate(
-        [
-            lax.lgamma(steps + column) - lax.lgamma(column) - lax.lgamma(steps + 1.0),
-            lax.digamma(steps + column) - lax.digamma(column),
-        ],
-        axis=1,
-    )
-    gene_tables = (
-        spread(theta),
-        spread(log_theta),
-        spread(log_theta + theta / (theta + rate_epsilon) / ln2),
-        table,
-    )
-    genes_first = jnp.transpose(output_weight, (2, 0, 1))
-    out16 = jnp.pad(genes_first.astype(bf16), ((0, gap), (0, 0), (0, 0)))
-    bias = jnp.pad(gene_vectors[:2].T, ((0, gap), (0, 0)))
-    off = (jnp.arange(size) >= genes)[:, None] & (jnp.arange(2) == 0)[None, :]
-    bias = jnp.where(off, -1e30, bias)
-    parts = jnp.stack(three_parts(bias), axis=2).astype(bf16)
-    ones = jnp.broadcast_to((jnp.arange(2) == 0).astype(bf16)[None, :, None], (size, 2, 3))
-    rest = jnp.zeros((size, 2, HOT_DEPTH - LANES - 6), bf16)
-    weights = jnp.transpose(jnp.concatenate([out16, parts, ones, rest], axis=2), (1, 0, 2))
-    backs = jnp.transpose(out16, (1, 2, 0))
+    output_rows = by_gene(output_weight)
+    weights, *gene_tables = prepare(output_rows, gene_vectors, genes)
 
     pad = 16
     heads_t = jnp.pad(head_weight.T.reshape(2, latent, -1), ((0, 0), (0, pad - latent), (0, 0)))
@@ -1041,32 +1441,48 @@
     )
     index, valid, noise = batch_index[None, :], valid_mask[None, :], noise_draw.T
 
-    encoded = encode(counts_t, encoder_t)
+    encoded = encode(counts_t, encoder_weight)
     hidden2, centered2, sample, share, stats, centered1, heads, rest_rows = middle(
         encoded, index, valid, noise, pack, batches, pad, genes_all
     )
-    rows = combine_tops(totals(hidden2, weights[0]), rest_rows)
+    rows = combine_tops(totals(hidden2, weights, genes), rest_rows)
     slopes, sums, grad_hidden2, grad_out1, grad_bias1, grad_theta = likelihood(
-        counts_t, hidden2, rows, share, weights, backs[1], gene_tables
+        counts_t, hidden2, rows, share, weights, gene_tables
     )
     pull = combine_sums(sums, rows, rest_rows, valid, genes_all)
     cell_loss = pull[1]
 
-    grad_hidden2, grad_out0, grad_bias0 = frequency(
-        slopes, hidden2, rows, pull, share, grad_hidden2, weights[0], backs[0]
-    )
-    grad_genes = jnp.stack(
-        [
-            jnp.sum(grad_bias0, axis=1),
-            jnp.sum(grad_bias1, axis=1),
-            jnp.sum(grad_theta, axis=1) * theta,
-        ]
-    )[:, :genes]
-    grad_pre16, small, norm_rows = middle_back(
-        grad_hidden2, centered2, sample, index, valid, noise, pack, stats, centered1, heads, batches
-    )
-    input_grad, grad_encoder = encoder_back(counts_t, grad_pre16, weight16)
-    small = lax.psum(small, ("gene", "cell"))
+    grad_hidden2, grad_out, grad_genes = frequency(
+        slopes,
+        hidden2,
+        rows,
+        pull,
+        share,
+        grad_hidden2,
+        weights,
+        grad_out1,
+        grad_bias1,
+        grad_theta,
+        gene_tables[0],
+        genes,
+    )
+    grad_pre16, small, norm_rows, grad_out, grad_genes = middle_back(
+        grad_hidden2,
+        centered2,
+        sample,
+        index,
+        valid,
+        noise,
+        pack,
+        stats,
+        centered1,
+        heads,
+        grad_out,
+        grad_genes,
+        batches,
+    )
+    input_grad, grad_encoder = encoder_back(counts_t, grad_pre16, encoder_weight)
+    grad_encoder, small = last_sums(grad_encoder, small)
     depth = pad + batches
     grad_mixing = jnp.concatenate([small[:latent], small[pad:depth]], axis=0)
     grad_heads = small[depth : depth + 2 * pad].reshape(2, pad, -1)[:, :latent]
@@ -1074,24 +1490,17 @@
     grad_head_bias = jnp.sum(small[depth + 2 * pad : depth + 4 * pad], axis=1)
     grad_head_bias = grad_head_bias.reshape(2, pad)[:, :latent].reshape(-1)
     grad_shift = small[depth + 4 * pad :]
-    grad_norms = norm_rows[:4]
-    grad_encoder, grad_out0, grad_out1, grad_genes = lax.psum(
-        (grad_encoder, grad_out0[:genes], grad_out1[:genes], grad_genes), "cell"
-    )
-    grad_output = jnp.transpose(jnp.stack([grad_out0, grad_out1], axis=1), (1, 2, 0))
-    weights_in = (
-        encoder_weight,
-        output_weight,
-        gene_vectors,
-        batch_shift,
-        layer_norm_params,
-        head_weight,
-        head_bias,
-        decoder_input,
-    )
+
+    updated = update(
+        (encoder_weight, encoder_weight_momentum, encoder_weight_average),
+        grad_encoder,
+        (output_rows, by_gene(output_weight_momentum), by_gene(output_weight_average)),
+        grad_out,
+    )
+    encoder_new = updated[:3]
+    output_new = [jnp.transpose(a.reshape(genes, 2, -1), (1, 2, 0)) for a in updated[3:]]
+    vectors = (gene_vectors, batch_shift, layer_norm_params, head_weight, head_bias, decoder_input)
     momenta = (
-        encoder_weight_momentum,
-        output_weight_momentum,
         gene_vectors_momentum,
         batch_shift_momentum,
         norm_params_momentum,
@@ -1100,8 +1509,6 @@
         decoder_input_momentum,
     )
     averages = (
-        encoder_weight_average,
-        output_weight_average,
         gene_vectors_average,
         batch_shift_average,
         norm_params_average,
@@ -1110,19 +1517,20 @@
         decoder_input_average,
     )
     grads = (
-        grad_encoder,
-        grad_output,
-        grad_genes,
+        grad_genes[:3, :genes],
         grad_shift,
-        grad_norms,
+        norm_rows[:4],
         grad_heads,
         grad_head_bias,
         grad_mixing,
     )
-    fresh, moments, means = zip(
-        *[nesterov(*group) for group in zip(weights_in, momenta, averages, grads, step_rates)]
-    )
-    return (cell_loss, input_grad.T, *fresh, *moments, *means)
+    small_new = zip(
+        *[nesterov(*group) for group in zip(vectors, momenta, averages, grads, step_rates[2:])]
+    )
+    results = []
+    for i, rest in enumerate(small_new):
+        results += [encoder_new[i], output_new[i], *rest]
+    return (cell_loss, input_grad.T, *results)
 
 
 def solution(mesh):

time: 716 us -> 486 us (0.68)
  waiting for transfers between devices: 146 us -> 0 us
  local copies, waits for them, and re-layouts: 60.5 us -> 10.3 us
  other arithmetic: 36.9 us -> 6 us
  Pallas kernels: 440 us -> 467 us
  between operations: 14.8 us -> 0.89 us
  blocking collectives: 10.9 us -> 0 us
    psum x2 -> x0, waiting for transfers between devices: 146 us -> none  [the longest x1 82.5 us: local(): lax.psum((grad_encoder, grad_out0[:genes], grad_out1[:genes], grad_genes)...]
    pallas_call x2 -> x5, Pallas kernels: 59.1 us -> 127 us  [the longest x1 41.4 us: frequency(): pl.pallas_call(functools.partial(frequency_kernel, genes=genes, chunk=chu...]
    pallas_call x1, Pallas kernels: 167 us -> 122 us  [likelihood(): pl.pallas_call(functools.partial(likelihood_kernel, genes=genes, chunk=ch...]
    unnamed x65 -> x38, local copies, waits for them, and re-layouts: 28.6 us -> 0.1 us
    sub x1 -> x0, other arithmetic: 15.1 us -> none  [local(): lax.lgamma(steps + column) - lax.lgamma(column) - lax.lgamma(steps + 1.0)]
    psum x1 -> x0, blocking collectives: 10.9 us -> none  [local(): lax.psum((grad_encoder, grad_out0[:genes], grad_out1[:genes], grad_genes)...]
  transfers between devices with their start and end apart: 2 -> 0, of which waited for: 2 -> 0; matrix products, arithmetic and copies ran while one was open for 2% -> 0% of each run, Pallas kernels for 6% -> 0%
where the time goes in v3:
time: 486 us; the launch traced here: 484 us
  Pallas kernels  467 us (96%)
  local copies, waits for them, and re-layouts  10.3 us (2%)
  other arithmetic  6 us (1%)
    pallas_call x1, Pallas kernels, likelihood(): pl.pallas_call(functools.partial(likelihood_kernel, genes=genes, chunk=ch...  122 us
    pallas_call x1, Pallas kernels, middle(): pl.pallas_call(functools.partial(middle_kernel, batches=batches, latent=n...  81.4 us
    pallas_call x1, Pallas kernels, middle_back(): pl.pallas_call(functools.partial(middle_back_kernel, batches=batches, lat...  52.5 us
    pallas_call x1, Pallas kernels, frequency(): pl.pallas_call(functools.partial(frequency_kernel, genes=genes, chunk=chu...  41.4 us
    pallas_call x1, Pallas kernels, encoder_back(): pl.pallas_call(encoder_back_kernel, grid=(pl.cdiv(genes, block),), in_spe...  39.5 us
    pallas_call x1, Pallas kernels, last_sums(): pl.pallas_call(last_sums_kernel, out_shape=[jax.ShapeDtypeStruct(grad.sha...  36.1 us
    pallas_call x1, Pallas kernels, encode(): pl.pallas_call(functools.partial(encode_kernel, genes=genes, chunk=chunk)...  20.8 us
    pallas_call x1, Pallas kernels, totals(): pl.pallas_call(functools.partial(totals_kernel, genes=genes, chunk=chunk)...  20.3 us

profile of v3, /device:TPU:0, one launch (start us, length us, event | category | flops | bytes accessed | tf_op | source)
XLA Modules:
  0.0 484.1 jit_solution(7039189960449759086)
XLA Ops:
  0.7 0.7 reshape.94
  1.4 0.1 reshape.95
  1.5 0.7 slice.36
  2.2 0.7 reshape.96
  2.9 0.7 slice.37
  3.7 5.7 %concatenate.6.pack_ref = f32[120,128]{1,0:T(8,128)} concatenate(f32[4,128]{1,0:T(4,128)} %param.36, f32[1,128]{1,0:T(1,128)S(1)} %pad.13, f32[3,128]{1,0:T(4,128)S(1)} %broadcast_in_dim.14, f32[10,128]{1,0:T(8,128)S(1)} %slice.36, f32[6,128]{1,0:T(8,128)S(1)} %broadcast_in_dim.15, f32[32,128]{1,0:T(8,128)S(1)} %slice.37, f32[32,128]{1,0:T(8,128)S(1)} %bitcast.53, f32[32,128]{1,0:T(8,128)} %param.35), dimensions={0} | concatenate | bytes 122880 | tf_op jit(solution)/shard_map/concatenate | solution.py:1429
  9.3 20.8 %encode.1.encoded_ref = f32[136,4096]{1,0:T(8,128)} custom-call(s32[2500,4096]{1,0:T(8,128)} %bitcast.38, f32[2500,128]{1,0:T(8,128)} %refs_0_.1), custom_call_target="tpu_custom_call" | custom-call | tf_op jit(solution)/shard_map/encode/pallas_call | solution.py:174
  30.2 81.4 %middle.1 = (bf16[128,4096]{1,0:T(8,128)(2,1)}, f32[128,4096]{1,0:T(8,128)}, f32[16,4096]{1,0:T(8,128)}, f32[1,4096]{1,0:T(1,128)}, f32[8,128]{1,0:T(8,128)}, /*...) custom-call(f32[136,4096]{1,0:T(8,128)} %encode.1.encoded_ref, s32[1,4096]{1,0:T(1,128)} %bitcast.50, ...), custom_call_target="tpu_custom_call" | custom-call | tf_op jit(solution)/shard_map/middle/pallas_call | solution.py:418
  111.6 16.2 %prepare.1 = (bf16[2,2512,256]{2,1,0:T(8,128)(2,1)}, f32[2512,128]{1,0:T(8,128)}, f32[2512,128]{1,0:T(8,128)}, f32[2512,128]{1,0:T(8,128)}, f32[2512,128]{1,0:T(8,128)}, /*index=5*/f32[2512,128]{1,0:T(8,128)}) custom-call(f32[5000,128]{1,0:T(8,128)} %bitcast.41, f32[3,2500]{1,0:T(4,128)} %vectors_ref.1), custom_call_target="tpu_custom_call" | custom-call | tf_op jit(solution)/shard_map/prepare/pallas_call | solution.py:122
  127.7 20.3 %totals.1.tops_ref = f32[2,4096]{1,0:T(2,128)} custom-call(bf16[128,4096]{1,0:T(8,128)(2,1)} %get-tuple-element.64.hidden_ref, bf16[2,2512,256]{2,1,0:T(8,128)(2,1)} %get-tuple-element.65.weight_ref), custom_call_target="tpu_custom_call" | custom-call | tf_op jit(solution)/shard_map/totals/pallas_call | solution.py:1019
  148.1 13.7 %combine_tops.1.rows_ref = f32[4,4096]{1,0:T(4,128)} custom-call(f32[2,4096]{1,0:T(2,128)} %totals.1.tops_ref, f32[2,512]{1,0:T(2,128)} %get-tuple-element.66.rest_ref), custom_call_target="tpu_custom_call" | custom-call | tf_op jit(solution)/shard_map/combine_tops/pallas_call | solution.py:483
  161.8 121.6 %likelihood.1 = (f32[2512,4096]{1,0:T(8,128)}, f32[2,4096]{1,0:T(2,128)}, f32[128,4096]{1,0:T(8,128)}, f32[2512,128]{1,0:T(8,128)}, f32[2512,128]{1,0:T(8,128)}, /*index=5*/f32[2512,128]{1,0:T(8,128)}) custom-call(s32[2500,4096]{1,0:T(8,128)} %bitcast.39, bf16[128,4096]{1,0:T(8,128)(2,1)} %get-tuple-element.64.hidden_ref, f32[4,4096]{1,0:T(4,128)} %combine_tops.1.rows_ref, ...), custom_call_target="tpu_custom_call" | custom-call | tf_op jit(solution)/shard_map/likelihood/pallas_call | solution.py:1196
  283.4 10.8 %combine_sums.1.pull_ref = f32[2,4096]{1,0:T(2,128)} custom-call(f32[2,4096]{1,0:T(2,128)} %get-tuple-element.73.sums_ref, f32[4,4096]{1,0:T(4,128)} %combine_tops.1.rows_ref, f32[2,512]{1,0:T(2,128)} %get-tuple-element.66.rest_ref, s32[1,4096]{1,0:T(1,128)} %bitcast.48), custom_call_target="tpu_custom_call" | custom-call | tf_op jit(solution)/shard_map/combine_sums/pallas_call | solution.py:522
  294.2 0.0 copy-start
  294.3 41.4 %frequency.1 = (f32[128,4096]{1,0:T(8,128)}, f32[2,2512,128]{2,1,0:T(8,128)}, f32[4,2512]{1,0:T(4,128)}) custom-call(f32[2512,4096]{1,0:T(8,128)} %get-tuple-element.74.slopes_ref, bf16[128,4096]{1,0:T(8,128)(2,1)} %get-tuple-element.64.hidden_ref, f32[4,4096]{1,0:T(4,128)} %combine_tops.1.rows_ref, f32[2,4096]{1,0:T(2,128)} %combine_sums.1.pull_ref, ...), custom_call_target="tpu_custom_call" | custom-call | tf_op jit(solution)/shard_map/frequency/pallas_call | solution.py:1322
  335.7 0.0 copy-done
  335.7 0.6 slice.38
  336.3 0.0 copy-start.13
  336.3 0.0 copy-start.14
  336.3 0.0 copy-start.15
  336.3 0.0 copy-start.1
  336.3 0.0 copy-start.5
  336.3 0.0 copy-start.6
  336.4 52.5 %middle_back.1 = (bf16[128,4096]{1,0:T(8,128)(2,1)}, f32[144,128]{1,0:T(8,128)}, f32[8,128]{1,0:T(8,128)}, f32[2,2512,128]{2,1,0:T(8,128)}, f32[4,2512]{1,0:T(4,128)}) custom-call(f32[128,4096]{1,0:T(8,128)} %get-tuple-element.79.grad_ref, f32[128,4096]{1,0:T(8,128)} %get-tuple-element.80.centered_ref, f32[16,4096]{1,0:T(8,128)} %get-tuple-element.81.sample_ref, ...), custom_call_target="tpu_custom_call" | custom-call | tf_op jit(solution)/shard_map/middle_back/pallas_call | solution.py:747
  388.9 0.0 copy-done.13
  388.9 0.0 copy-done.14
  388.9 0.0 copy-done.15
  388.9 1.3 multiply_add_fusion.7
  390.2 0.0 copy-done.1
  390.2 0.0 copy-done.5
  390.2 0.0 copy-done.6
  390.2 1.5 multiply_add_fusion
  391.6 0.0 copy-start.3
  391.6 0.0 copy-start.9
  391.7 0.0 copy-start.17
  391.7 0.0 copy-start.18
  391.7 0.0 copy-start.4
  391.7 0.0 copy-start.11
  391.7 0.0 copy-start.12
  391.7 0.0 copy-start.2
  391.7 0.0 copy-start.7
  391.7 0.0 copy-start.8
  391.8 39.5 %encoder_back.1 = (f32[2500,4096]{1,0:T(8,128)}, f32[2528,128]{1,0:T(8,128)}) custom-call(s32[2500,4096]{1,0:T(8,128)} %bitcast.40, bf16[128,4096]{1,0:T(8,128)(2,1)} %get-tuple-element.87.grad_ref, f32[2500,128]{1,0:T(8,128)} %refs_0_.1), custom_call_target="tpu_custom_call" | custom-call | tf_op jit(solution)/shard_map/encoder_back/pallas_call | solution.py:1361
  431.2 36.1 %last_sums.1 = (f32[2528,128]{1,0:T(8,128)}, f32[144,128]{1,0:T(8,128)}) custom-call(f32[2528,128]{1,0:T(8,128)} %get-tuple-element.89.grad_ref, f32[144,128]{1,0:T(8,128)} %get-tuple-element.90.small_ref), custom_call_target="tpu_custom_call" | custom-call | tf_op jit(solution)/shard_map/last_sums/pallas_call | solution.py:868
  467.3 0.7 slice.46
  468.0 0.0 copy-done.3
  468.0 0.0 copy-done.9
  468.0 0.0 copy-done.10
  468.0 1.5 fusion.3
  469.5 0.1 reshape.104
  469.6 0.1 reshape.105
  469.7 0.0 copy-done.16
  469.7 0.0 copy-done.17
  469.7 0.0 copy-done.18
  469.7 0.5 multiply_add_fusion.9
  470.2 0.0 copy-done.4
  470.2 0.0 copy-done.11
  470.2 0.0 copy-done.12
  470.2 0.6 multiply_add_fusion.6
  470.9 0.0 copy-done.2
  470.9 0.0 copy-done.7
  470.9 0.0 copy-done.8
  470.9 0.6 multiply_add_fusion.2
  471.5 12.6 %update.1 = (f32[2500,128]{1,0:T(8,128)}, f32[2500,128]{1,0:T(8,128)}, f32[2500,128]{1,0:T(8,128)}, f32[5000,128]{1,0:T(8,128)}, f32[5000,128]{1,0:T(8,128)}, /*index=5*/f32[5000,128]{1,0:T(8,128)}) custom-call(f32[2500,128]{1,0:T(8,128)} %refs_0_.1, f32[2500,128]{1,0:T(8,128)} %refs_1_.1, f32[2500,128]{1,0:T(8,128)} %refs_2_.1, ...), custom_call_target="tpu_custom_call" | custom-call | tf_op jit(solution)/shard_map/update/pallas_call | solution.py:909
  (8 shorter events, 0.0 us)
Async XLA Ops:
  294.2 41.4 %copy-start = (f32[2,4096]{1,0:T(2,128)S(1)}, f32[2,4096]{1,0:T(2,128)}, u32[]{:S(2)}) copy-start(f32[2,4096]{1,0:T(2,128)} %combine_sums.1.pull_ref) | copy-start | bytes 98308
  336.3 52.6 %copy-start.13 = (f32[4,128]{1,0:T(4,128)S(1)}, f32[4,128]{1,0:T(4,128)}, u32[]{:S(2)}) copy-start(f32[4,128]{1,0:T(4,128)} %param.36) | copy-start | bytes 6148
  336.3 52.6 %copy-start.14 = (f32[4,128]{1,0:T(4,128)S(1)}, f32[4,128]{1,0:T(4,128)}, u32[]{:S(2)}) copy-start(f32[4,128]{1,0:T(4,128)} %param.52) | copy-start | bytes 6148
  336.3 52.6 %copy-start.15 = (f32[4,128]{1,0:T(4,128)S(1)}, f32[4,128]{1,0:T(4,128)}, u32[]{:S(2)}) copy-start(f32[4,128]{1,0:T(4,128)} %param.44) | copy-start | bytes 6148
  336.3 53.8 %copy-start.1 = (f32[3,2500]{1,0:T(4,128)S(1)}, f32[3,2500]{1,0:T(4,128)}, u32[]{:S(2)}) copy-start(f32[3,2500]{1,0:T(4,128)} %vectors_ref.1) | copy-start | bytes 90004
  336.3 53.8 %copy-start.5 = (f32[3,2500]{1,0:T(4,128)S(1)}, f32[3,2500]{1,0:T(4,128)}, u32[]{:S(2)}) copy-start(f32[3,2500]{1,0:T(4,128)} %param.50) | copy-start | bytes 90004
  336.3 53.8 %copy-start.6 = (f32[3,2500]{1,0:T(4,128)S(1)}, f32[3,2500]{1,0:T(4,128)}, u32[]{:S(2)}) copy-start(f32[3,2500]{1,0:T(4,128)} %param.42) | copy-start | bytes 90004
  391.6 76.4 %copy-start.3 = (f32[32,128]{1,0:T(8,128)S(1)}, f32[32,128]{1,0:T(8,128)}, u32[]{:S(2)}) copy-start(f32[32,128]{1,0:T(8,128)} %param.35) | copy-start | bytes 49156
  391.6 76.4 %copy-start.9 = (f32[32,128]{1,0:T(8,128)S(1)}, f32[32,128]{1,0:T(8,128)}, u32[]{:S(2)}) copy-start(f32[32,128]{1,0:T(8,128)} %param.43) | copy-start | bytes 49156
  391.6 76.4 %copy-start.10 = (f32[32,128]{1,0:T(8,128)S(1)}, f32[32,128]{1,0:T(8,128)}, u32[]{:S(2)}) copy-start(f32[32,128]{1,0:T(8,128)} %param.51) | copy-start | bytes 49156
  391.6 78.0 %copy-start.16 = (f32[20]{0:T(128)S(1)}, f32[20]{0:T(128)}, u32[]{:S(2)}) copy-start(f32[20]{0:T(128)} %param.38) | copy-start | bytes 244
  391.7 78.0 %copy-start.17 = (f32[20]{0:T(128)S(1)}, f32[20]{0:T(128)}, u32[]{:S(2)}) copy-start(f32[20]{0:T(128)} %param.54) | copy-start | bytes 244
  391.7 78.0 %copy-start.18 = (f32[20]{0:T(128)S(1)}, f32[20]{0:T(128)}, u32[]{:S(2)}) copy-start(f32[20]{0:T(128)} %param.46) | copy-start | bytes 244
  391.7 78.5 %copy-start.4 = (f32[128,20]{0,1:T(8,128)S(1)}, f32[128,20]{0,1:T(8,128)}, u32[]{:S(2)}) copy-start(f32[128,20]{0,1:T(8,128)} %param.37) | copy-start | bytes 30724
  391.7 78.5 %copy-start.11 = (f32[128,20]{0,1:T(8,128)S(1)}, f32[128,20]{0,1:T(8,128)}, u32[]{:S(2)}) copy-start(f32[128,20]{0,1:T(8,128)} %param.53) | copy-start | bytes 30724
  391.7 78.5 %copy-start.12 = (f32[128,20]{0,1:T(8,128)S(1)}, f32[128,20]{0,1:T(8,128)}, u32[]{:S(2)}) copy-start(f32[128,20]{0,1:T(8,128)} %param.45) | copy-start | bytes 30724
  391.7 79.1 %copy-start.2 = (f32[42,128]{1,0:T(8,128)S(1)}, f32[42,128]{1,0:T(8,128)}, u32[]{:S(2)}) copy-start(f32[42,128]{1,0:T(8,128)} %param.39) | copy-start | bytes 64516
  391.7 79.1 %copy-start.7 = (f32[42,128]{1,0:T(8,128)S(1)}, f32[42,128]{1,0:T(8,128)}, u32[]{:S(2)}) copy-start(f32[42,128]{1,0:T(8,128)} %param.55) | copy-start | bytes 64516
  391.7 79.1 %copy-start.8 = (f32[42,128]{1,0:T(8,128)S(1)}, f32[42,128]{1,0:T(8,128)}, u32[]{:S(2)}) copy-start(f32[42,128]{1,0:T(8,128)} %param.47) | copy-start | bytes 64516

commit v4 on v3

--- a/solution.py
+++ b/solution.py
@@ -44,9 +44,9 @@
     return pl.BlockSpec((rows, chunk), lambda i: (0, i))
 
 
-def split_rows(genes):
+def split_rows(genes, most=13):
     full = genes // ROWS
-    groups = max(d for d in range(1, 14) if full % d == 0)
+    groups = max(d for d in range(1, most + 1) if full % d == 0)
     return full, groups, genes - full * ROWS
 
 
@@ -67,152 +67,22 @@
     return jnp.concatenate([piece, filler], axis=0)
 
 
-def prepare_kernel(
-    output_ref,
-    vectors_ref,
-    weights_ref,
-    theta_ref,
-    log_ref,
-    slope_ref,
-    gammas_ref,
-    digammas_ref,
-    *,
-    genes,
-):
-    block = theta_ref.shape[0]
-    turned = jnp.transpose(
-        jnp.concatenate([vectors_ref[...], jnp.zeros((block - 3, block), f32)], axis=0)
-    )
-    row = pl.program_id(0) * block + lax.broadcasted_iota(jnp.int32, (block, 1), 0)
-    inside = row < genes
-    lane = lax.broadcasted_iota(jnp.int32, (block, LANES), 1)
-    for k in range(2):
-        weight = jnp.where(inside, output_ref[pl.ds(k, block, stride=2), :], 0.0)
-        weights_ref[k, :, 0:LANES] = weight.astype(bf16)
-        bias = jnp.where(inside, turned[:, k : k + 1], 0.0 if k else -1e30)
-        high = bias.astype(bf16).astype(f32)
-        middle = (bias - high).astype(bf16).astype(f32)
-        low = (bias - high - middle).astype(bf16).astype(f32)
-        extra = jnp.where(lane == 0, high, jnp.where(lane == 1, middle, 0.0))
-        extra = jnp.where(lane == 2, low, extra)
-        if k == 0:
-            extra = jnp.where((lane >= 3) & (lane < 6), 1.0, extra)
-        weights_ref[k, :, LANES : 2 * LANES] = extra.astype(bf16)
-    theta = jnp.where(inside, jnp.exp(turned[:, 2:3]), 1.0) + jnp.zeros((block, LANES), f32)
-    log_theta = jnp.log2(theta + rate_epsilon)
-    theta_ref[...] = theta
-    log_ref[...] = log_theta
-    slope_ref[...] = ln2 * log_theta + theta / (theta + rate_epsilon)
-    step = lane.astype(f32)
-    climb = theta + step
-    upper = jnp.where(
-        lax.broadcasted_iota(jnp.int32, (LANES, LANES), 0)
-        < lax.broadcasted_iota(jnp.int32, (LANES, LANES), 1),
-        1.0,
-        0.0,
-    )
-    gammas_ref[...] = exact(jnp.log2(climb / (step + 1.0)), upper, 1, 0)
-    digammas_ref[...] = exact(1.0 / climb, upper, 1, 0)
-
-
-def prepare(output_rows, vectors, genes):
-    size = padded(genes)
-    block = LANES
-    table = pl.BlockSpec((block, LANES), lambda i: (i, 0))
-    return pl.pallas_call(
-        functools.partial(prepare_kernel, genes=genes),
-        grid=(pl.cdiv(size, block),),
-        in_specs=[
-            pl.BlockSpec((2 * block, LANES), lambda i: (i, 0)),
-            pl.BlockSpec((3, block), lambda i: (0, i)),
-        ],
-        out_specs=[pl.BlockSpec((2, block, HOT_DEPTH), lambda i: (0, i, 0))] + [table] * 5,
-        out_shape=[jax.ShapeDtypeStruct((2, size, HOT_DEPTH), bf16)]
-        + [jax.ShapeDtypeStruct((size, LANES), f32)] * 5,
-        compiler_params=PARAMS,
-        name="prepare",
-    )(output_rows, vectors)
-
-
-def encode_kernel(counts_ref, encoder_ref, out_ref, inputs_ref, weight_ref, *, genes, chunk):
-    full, groups, tail = split_rows(genes)
-    width = encoder_ref.shape[1]
-
-    @pl.when(pl.program_id(0) == 0)
-    def _():
-        weight_ref[0 : full * ROWS, :] = encoder_ref[0 : full * ROWS, :].astype(bf16)
-        if tail:
-            weight_ref[full * ROWS :, :] = tail_rows(
-                encoder_ref, full * ROWS, genes, slice(None), f32
-            ).astype(bf16)
-
-    def group(counted, rows, total):
-        inputs_ref[rows, :] = jnp.log(counted + 1.0).astype(bf16)
-        return total + counted[:8] + counted[8:]
-
-    def step(i, total):
-        rows = pl.ds(pl.multiple_of(i * ROWS, ROWS), ROWS)
-        return group(counts_ref[rows, :].astype(f32), rows, total)
-
-    total = lax.fori_loop(0, full, step, jnp.zeros((8, chunk), f32), unroll=4)
-    if tail:
-        rows = pl.ds(full * ROWS, ROWS)
-        counted = tail_rows(counts_ref, full * ROWS, genes, slice(None), jnp.int32).astype(f32)
-        total = group(counted, rows, total)
-    out_ref[0:width, :] = lax.dot_general(
-        weight_ref[...], inputs_ref[...], (((0,), (0,)), ((), ())), preferred_element_type=f32
-    )
-    row = lax.broadcasted_iota(jnp.int32, (8, chunk), 0)
-    library = jnp.sum(total, axis=0, keepdims=True)
-    out_ref[width : width + 8, :] = jnp.where(row == 0, library, 0.0)
-
-
-def encode(counts_t, weight):
-    genes, cells = counts_t.shape
-    chunk = pick_chunk(cells, 512)
-    width = weight.shape[1]
-    return pl.pallas_call(
-        functools.partial(encode_kernel, genes=genes, chunk=chunk),
-        grid=(cells // chunk,),
-        in_specs=[column_blocks(genes, chunk), whole(weight)],
-        out_specs=column_blocks(width + 8, chunk),
-        out_shape=jax.ShapeDtypeStruct((width + 8, cells), f32),
-        scratch_shapes=[
-            pltpu.VMEM((padded(genes), chunk), bf16),
-            pltpu.VMEM((padded(genes), width), bf16),
-        ],
-        compiler_params=PARAMS,
-        name="encode",
-    )(counts_t, weight)
-
-
 class Team:
-    def __init__(self, gene_only):
-        self.genes, self.cells = lax.axis_size("gene"), lax.axis_size("cell")
+    def __init__(self, axis):
+        self.size, self.me = lax.axis_size(axis), lax.axis_index(axis)
         self.gene, self.cell = lax.axis_index("gene"), lax.axis_index("cell")
-        self.gene_only = gene_only
-        self.size = self.genes if gene_only else self.genes * self.cells
-        self.me = self.gene if gene_only else self.gene * self.cells + self.cell
+        self.axis = axis
+
+    def place(self, other):
+        return (other, self.cell) if self.axis == "gene" else (self.gene, other)
 
     def others(self, act):
         def one(step, carry):
             other = lax.rem(self.me + step, self.size)
-            if self.gene_only:
-                act(other, (other, self.cell))
-            else:
-                act(other, (other // self.cells, lax.rem(other, self.cells)))
+            act(other, self.place(other))
             return carry
 
         lax.fori_loop(1, self.size, one, 0)
-
-    def greet(self):
-        barrier = pltpu.get_barrier_semaphore()
-
-        def act(other, place):
-            pl.semaphore_signal(barrier, inc=1, device_id=place, device_id_type=MESH)
-
-        self.others(act)
-        pl.semaphore_wait(barrier, self.size - 1)
 
     def send(self, source, target, sems):
         def act(other, place):
@@ -228,6 +98,17 @@
         self.others(act)
 
 
+def greet(*teams):
+    barrier = pltpu.get_barrier_semaphore()
+
+    def act(other, place):
+        pl.semaphore_signal(barrier, inc=1, device_id=place, device_id_type=MESH)
+
+    for team in teams:
+        team.others(act)
+    pl.semaphore_wait(barrier, sum(team.size - 1 for team in teams))
+
+
 def await_bytes(ref, sem):
     pltpu.make_async_copy(ref, ref, sem).wait()
 
@@ -245,6 +126,24 @@
         return total + box[i]
 
     return lax.fori_loop(1, box.shape[0], add, box[0])
+
+
+def spread_box(team, box, value, sems):
+    box[team.me] = value
+    team.send(lambda other: box.at[team.me], box.at[team.me], sems)
+    others = box.at[pl.ds(0, team.size - 1)]
+
+    def finish():
+        await_bytes(others, sems.at[0])
+        await_bytes(others, sems.at[1])
+        return box_sum(box)
+
+    return finish
+
+
+def row_boxes():
+    shapes = [(lax.axis_size(axis), 8, LANES) for axis in ("cell", "gene")]
+    return [pltpu.VMEM(shape, f32) for shape in shapes * 2]
 
 
 def eight_rows(rows):
@@ -287,12 +186,236 @@
     return mixing, heads, slice(heads.stop, heads.stop + batches)
 
 
+def prepare_tables(number, genes, output_ref, vectors_ref, weights_ref, tables):
+    theta_ref, log_ref, slope_ref, gammas_ref, digammas_ref = tables
+    lane = lax.broadcasted_iota(jnp.int32, (LANES, LANES), 1)
+    below = lax.broadcasted_iota(jnp.int32, (LANES, LANES), 0)
+    upper = jnp.where(below < lane, 1.0, 0.0)
+    step = lane.astype(f32)
+    block = theta_ref.shape[0]
+    for at in range(0, block, LANES):
+        here = slice(at, at + LANES)
+        turned = jnp.transpose(
+            jnp.concatenate([vectors_ref[:, here], jnp.zeros((LANES - 3, LANES), f32)], axis=0)
+        )
+        inside = number * block + at + below[:, 0:1] < genes
+        for k in range(2):
+            weight = output_ref[pl.ds(2 * at + k, LANES, stride=2), :]
+            weights_ref[k, here, 0:LANES] = jnp.where(inside, weight, 0.0).astype(bf16)
+            bias = jnp.where(inside, turned[:, k : k + 1], 0.0 if k else -1e30)
+            high = bias.astype(bf16).astype(f32)
+            middle = (bias - high).astype(bf16).astype(f32)
+            low = (bias - high - middle).astype(bf16).astype(f32)
+            extra = jnp.where(lane == 0, high, jnp.where(lane == 1, middle, 0.0))
+            extra = jnp.where(lane == 2, low, extra)
+            if k == 0:
+                extra = jnp.where((lane >= 3) & (lane < 6), 1.0, extra)
+            weights_ref[k, here, LANES : 2 * LANES] = extra.astype(bf16)
+        theta = jnp.where(inside, jnp.exp(turned[:, 2:3]), 1.0) + jnp.zeros((LANES, LANES), f32)
+        log_theta = jnp.log2(theta + rate_epsilon)
+        theta_ref[here, :] = theta
+        log_ref[here, :] = log_theta
+        slope_ref[here, :] = ln2 * log_theta + theta / (theta + rate_epsilon)
+        climb = theta + step
+        gammas_ref[here, :] = exact(jnp.log2(climb / (step + 1.0)), upper, 1, 0)
+        digammas_ref[here, :] = exact(1.0 / climb, upper, 1, 0)
+
+
+def encode_kernel(
+    counts_ref,
+    encoder_ref,
+    output_ref,
+    vectors_ref,
+    out_ref,
+    weights_ref,
+    theta_ref,
+    log_ref,
+    slope_ref,
+    gammas_ref,
+    digammas_ref,
+    inputs_ref,
+    weight_ref,
+    near_give,
+    near_box,
+    far_give,
+    far_box,
+    near_sems,
+    far_sems,
+    *,
+    genes,
+    table_blocks,
+):
+    slab = counts_ref.shape[1]
+    full, _, tail = split_rows(genes)
+    width = encoder_ref.shape[1]
+    group = Team("gene")
+    pairs = group.size // 2
+    high, low = group.me // 2, lax.rem(group.me, 2)
+    step = pl.program_id(0)
+    turn = step // 2
+
+    def place(high, low):
+        return (2 * high + low, group.cell)
+
+    def copy(source, target, sems, where):
+        return pltpu.make_async_remote_copy(
+            src_ref=source,
+            dst_ref=target,
+            send_sem=sems.at[0],
+            recv_sem=sems.at[1],
+            device_id=where,
+            device_id_type=MESH,
+        )
+
+    @pl.when(step == 0)
+    def _():
+        barrier = pltpu.get_barrier_semaphore()
+        pl.semaphore_signal(barrier, inc=1, device_id=place(high, 1 - low), device_id_type=MESH)
+        for d in range(1, pairs):
+            where = place(lax.rem(high + d, pairs), low)
+            pl.semaphore_signal(barrier, inc=1, device_id=where, device_id_type=MESH)
+        weight_ref[0 : full * ROWS, :] = encoder_ref[0 : full * ROWS, :].astype(bf16)
+        if tail:
+            weight_ref[full * ROWS :, :] = tail_rows(
+                encoder_ref, full * ROWS, genes, slice(None), f32
+            ).astype(bf16)
+        pl.semaphore_wait(barrier, pairs)
+
+    def part(ref):
+        def rows16(counted, rows, total):
+            inputs_ref[rows, :] = jnp.log(counted + 1.0).astype(bf16)
+            return total + counted[:8] + counted[8:]
+
+        def one(i, total):
+            rows = pl.ds(pl.multiple_of(i * ROWS, ROWS), ROWS)
+            return rows16(counts_ref[rows, :].astype(f32), rows, total)
+
+        total = lax.fori_loop(0, full, one, jnp.zeros((8, slab), f32), unroll=4)
+        if tail:
+            rows = pl.ds(full * ROWS, ROWS)
+            counted = tail_rows(counts_ref, full * ROWS, genes, slice(None), jnp.int32)
+            total = rows16(counted.astype(f32), rows, total)
+        ref[0:width, :] = lax.dot_general(
+            weight_ref[...], inputs_ref[...], (((0,), (0,)), ((), ())), preferred_element_type=f32
+        )
+        row = lax.broadcasted_iota(jnp.int32, (8, slab), 0)
+        ref[width : width + 8, :] = jnp.where(row == 0, jnp.sum(total, axis=0, keepdims=True), 0.0)
+
+    def near_copy(i):
+        return copy(near_give.at[i], near_box.at[i], near_sems.at[i], place(high, 1 - low))
+
+    def far_copy(i):
+        target = lax.rem(high + 1 + i, pairs)
+        return copy(far_give.at[i], far_box.at[i], far_sems.at[i], place(target, low))
+
+    tables = (theta_ref, log_ref, slope_ref, gammas_ref, digammas_ref)
+
+    @pl.when(step < table_blocks)
+    def _():
+        prepare_tables(step, genes, output_ref, vectors_ref, weights_ref, tables)
+
+    @pl.when(lax.rem(step, 2) == 0)
+    def _():
+        part(near_give.at[turn])
+        near_copy(turn).start()
+
+    @pl.when(lax.rem(step, 2) == 1)
+    def _():
+        part(out_ref)
+        near_copy(turn).wait_recv()
+        total = out_ref[...] + near_box[turn]
+
+        @pl.when(turn < pairs - 1)
+        def _():
+            far_give[turn] = total
+            far_copy(turn).start()
+
+        @pl.when(turn == pairs - 1)
+        def _():
+            def gather(i, total):
+                far_copy(i).wait_recv()
+                return total + far_box[i]
+
+            out_ref[...] = lax.fori_loop(0, pairs - 1, gather, total)
+
+            def drain(i, carry):
+                far_copy(i).wait_send()
+                return carry
+
+            lax.fori_loop(0, pairs - 1, drain, 0)
+
+            def drain_near(i, carry):
+                near_copy(i).wait_send()
+                return carry
+
+            lax.fori_loop(0, pairs, drain_near, 0)
+
+
+def encode(counts_t, weight, output_rows, vectors):
+    genes, cells = counts_t.shape
+    devices = lax.axis_size("gene")
+    pairs = devices // 2
+    slab = cells // devices
+    width = weight.shape[1]
+
+    def slab_of(i):
+        me = lax.axis_index("gene")
+        low = lax.rem(me + 1 + i, 2)
+        return (0, 2 * lax.rem(me // 2 + 1 + i // 2, pairs) + low)
+
+    box = pltpu.VMEM((pairs, width + 8, slab), f32)
+    size = padded(genes)
+    block = LANES * pl.cdiv(pl.cdiv(size, LANES), devices)
+    table_blocks = pl.cdiv(size, block)
+
+    def table_of(i):
+        return jnp.minimum(i, table_blocks - 1)
+
+    table = pl.BlockSpec((block, LANES), lambda i: (table_of(i), 0))
+    return pl.pallas_call(
+        functools.partial(encode_kernel, genes=genes, table_blocks=table_blocks),
+        grid=(devices,),
+        in_specs=[
+            pl.BlockSpec((genes, slab), slab_of),
+            whole(weight),
+            pl.BlockSpec((2 * block, LANES), lambda i: (table_of(i), 0)),
+            pl.BlockSpec((3, block), lambda i: (0, table_of(i))),
+        ],
+        out_specs=[
+            pl.BlockSpec((width + 8, slab), lambda i: (0, 0)),
+            pl.BlockSpec((2, block, HOT_DEPTH), lambda i: (0, table_of(i), 0)),
+        ]
+        + [table] * 5,
+        out_shape=[
+            jax.ShapeDtypeStruct((width + 8, slab), f32),
+            jax.ShapeDtypeStruct((2, size, HOT_DEPTH), bf16),
+        ]
+        + [jax.ShapeDtypeStruct((size, LANES), f32)] * 5,
+        scratch_shapes=[
+            pltpu.VMEM((padded(genes), slab), bf16),
+            pltpu.VMEM((padded(genes), width), bf16),
+            box,
+            box,
+            box,
+            box,
+            pltpu.SemaphoreType.DMA((pairs, 2)),
+            pltpu.SemaphoreType.DMA((pairs, 2)),
+        ],
+        compiler_params=talking(6),
+        name="encode",
+    )(counts_t, weight, output_rows, vectors)
+
+
 def middle_kernel(
     encoded_ref,
     index_ref,
     valid_ref,
     noise_ref,
-    pack_ref,
+    norms_ref,
+    bias_ref,
+    mixing_ref,
+    head_ref,
+    shift_ref,
     hidden_ref,
     centered_ref,
     sample_ref,
@@ -301,65 +424,60 @@
     first_ref,
     heads_ref,
     rest_ref,
-    slab_box,
+    pack_ref,
     box1,
     box2,
-    slab_sems,
+    box3,
+    box4,
     sems1,
     sems2,
+    sems3,
+    sems4,
     sample_sems,
     *,
     batches,
     latent,
     genes_all,
 ):
-    group, everyone = Team(True), Team(False)
+    group, team = Team("gene"), Team("cell")
     width, slab = first_ref.shape
     cells = hidden_ref.shape[1]
     pad = sample_ref.shape[0]
     mixing_rows, heads_rows, shift_rows = pack_layout(pad, batches)
+    pack_ref[...] = jnp.zeros_like(pack_ref)
+    pack_ref[0:4, :] = norms_ref[...]
+    pack_ref[4:5, 0:latent] = bias_ref[:, 0:latent]
+    pack_ref[4:5, pad : pad + latent] = bias_ref[:, latent : 2 * latent]
+    at = mixing_rows.start
+    pack_ref[at : at + latent, :] = mixing_ref[0:latent, :]
+    pack_ref[at + pad : at + pad + batches, :] = mixing_ref[latent:, :]
+    at = heads_rows.start
+    pack_ref[at : at + latent, :] = head_ref[0:latent, :]
+    pack_ref[at + pad : at + pad + latent, :] = head_ref[latent:, :]
+    pack_ref[shift_rows, :] = shift_ref[...]
     mixing = pack_ref[mixing_rows, :]
 
     def part(other):
         return pl.ds(pl.multiple_of(other * slab, LANES), slab)
 
     mine = part(group.me)
-    everyone.greet()
-    group.send(lambda other: encoded_ref.at[:, part(other)], slab_box.at[group.me], slab_sems)
-    slab_box[group.me] = encoded_ref[:, mine]
+    greet(group, team)
     hot = hot_rows(index_ref[:, mine], batches)
     valid = valid_ref[:, mine].astype(f32)
     shift = exact(pack_ref[shift_rows, :], hot, 0, 0)
     gain1, bias1, gain2, bias2, head_bias = columns_of([pack_ref[i : i + 1, :] for i in range(5)])
-    others = slab_box.at[pl.ds(0, group.size - 1)]
-    await_bytes(others, slab_sems.at[0])
-    await_bytes(others, slab_sems.at[1])
-    total = box_sum(slab_box)
+    total = encoded_ref[...]
     rest_ref[0:1, :] = total[width : width + 1, :]
     pre1 = total[0:width, :] + shift
 
-    def reduced(rows, box, sems):
-        box[everyone.me] = eight_rows(rows)
-        everyone.send(lambda other: box.at[everyone.me], box.at[everyone.me], sems)
-        others = box.at[pl.ds(0, everyone.size - 1)]
-
-        def finish():
-            await_bytes(others, sems.at[0])
-            await_bytes(others, sems.at[1])
-            return box_sum(box)
-
-        return finish
-
     weighed = valid * pre1
-    sums = reduced(
-        [
-            row_sums(fold_lanes(weighed)),
-            row_sums(fold_lanes(weighed * pre1)),
-            jnp.broadcast_to(jnp.sum(valid, axis=1, keepdims=True), (1, LANES)),
-        ],
-        box1,
-        sems1,
-    )()
+    rows = [
+        row_sums(fold_lanes(weighed)),
+        row_sums(fold_lanes(weighed * pre1)),
+        jnp.broadcast_to(jnp.sum(valid, axis=1, keepdims=True), (1, LANES)),
+    ]
+    sums = spread_box(team, box1, eight_rows(rows), sems1)()
+    sums = spread_box(group, box2, sums, sems2)()
     count = jnp.maximum(sums[2:3], 1.0)
     mean1 = sums[0:1] / count
     inverse1 = lax.rsqrt(sums[1:2] / count - mean1 * mean1 + norm_epsilon)
@@ -380,9 +498,9 @@
     group.send(lambda other: sample_ref.at[:, mine], sample_ref.at[:, mine], sample_sems)
     pre2 = exact(mixing, jnp.concatenate([sample, hot], axis=0), 0, 0)
     weighed = valid * pre2
-    finish = reduced(
-        [row_sums(fold_lanes(weighed)), row_sums(fold_lanes(weighed * pre2))], box2, sems2
-    )
+    rows = [row_sums(fold_lanes(weighed)), row_sums(fold_lanes(weighed * pre2))]
+    sums = spread_box(team, box3, eight_rows(rows), sems3)()
+    finish = spread_box(group, box4, sums, sems4)
     scale = 1.0 / (count * genes_all)
     share_ref[...] = valid_ref[...].astype(f32) * scale[:, 0:1]
     sums = finish()
@@ -409,11 +527,10 @@
     lax.fori_loop(0, cells // piece, decode, 0)
 
 
-def middle(encoded, index, valid, noise, pack, batches, pad, genes_all):
+def middle(encoded, index, valid, noise, small_weights, batches, pad, genes_all):
     cells = index.shape[1]
     width = LANES
     genes_axis = lax.axis_size("gene")
-    devices = genes_axis * lax.axis_size("cell")
     slab = cells // genes_axis
     return pl.pallas_call(
         functools.partial(
@@ -428,29 +545,25 @@
             jax.ShapeDtypeStruct((width, slab), f32),
             jax.ShapeDtypeStruct((2 * pad, slab), f32),
             jax.ShapeDtypeStruct((2, slab), f32),
+            jax.ShapeDtypeStruct((8 + 3 * pad + 2 * batches, LANES), f32),
         ],
-        in_specs=[IN_VMEM] * 5,
-        out_specs=[IN_VMEM] * 8,
-        scratch_shapes=[
-            pltpu.VMEM((genes_axis, width + 8, slab), f32),
-            pltpu.VMEM((devices, 8, LANES), f32),
-            pltpu.VMEM((devices, 8, LANES), f32),
-        ]
-        + [pltpu.SemaphoreType.DMA((2,))] * 4,
+        in_specs=[IN_VMEM] * 9,
+        out_specs=[IN_VMEM] * 9,
+        scratch_shapes=row_boxes() + [pltpu.SemaphoreType.DMA((2,))] * 5,
         compiler_params=talking(1),
         name="middle",
-    )(encoded, index, valid, noise, pack)
+    )(encoded, index, valid, noise, *small_weights)
 
 
 def tops_kernel(tops_ref, rest_ref, out_ref, box, sems, back_sems):
-    group = Team(True)
+    group = Team("gene")
     slab = rest_ref.shape[1]
 
     def part(other):
         return pl.ds(pl.multiple_of(other * slab, LANES), slab)
 
     mine = part(group.me)
-    group.greet()
+    greet(group)
     group.send(lambda other: tops_ref.at[:, part(other)], box.at[group.me], sems)
     box[group.me] = tops_ref[:, mine]
     others = box.at[pl.ds(0, group.size - 1)]
@@ -492,14 +605,14 @@
 
 
 def sums_kernel(sums_ref, rows_ref, rest_ref, valid_ref, out_ref, box, sems, back_sems, *, genes_all):
-    group = Team(True)
+    group = Team("gene")
     slab = rest_ref.shape[1]
 
     def part(other):
         return pl.ds(pl.multiple_of(other * slab, LANES), slab)
 
     mine = part(group.me)
-    group.greet()
+    greet(group)
     group.send(lambda other: sums_ref.at[:, part(other)], box.at[group.me], sems)
     box[group.me] = sums_ref[:, mine]
     others = box.at[pl.ds(0, group.size - 1)]
@@ -552,6 +665,8 @@
     slab_box,
     box1,
     box2,
+    box3,
+    box4,
     output_box,
     half_box,
     half_give,
@@ -559,6 +674,8 @@
     slab_sems,
     sems1,
     sems2,
+    sems3,
+    sems4,
     grad_sems,
     output_sems,
     genes_sems,
@@ -566,7 +683,7 @@
     batches,
     latent,
 ):
-    group, everyone = Team(True), Team(False)
+    group, team = Team("gene"), Team("cell")
     cell = lax.axis_index("cell")
     bit, near, far = lax.rem(cell, 2), cell + 1 - 2 * lax.rem(cell, 2), lax.rem(cell + 2, 4)
     half = output_ref.shape[1] // 2
@@ -595,12 +712,12 @@
         return pl.ds(pl.multiple_of(other * slab, LANES), slab)
 
     mine = part(group.me)
-    everyone.greet()
+    greet(group, team)
     swap1 = swap(output_ref.at[1 - bit], output_box, near, 0)
     genes_box[cell] = genes_ref[...]
 
     def tell(step, carry):
-        other = lax.rem(cell + step, group.cells)
+        other = lax.rem(cell + step, team.size)
         pltpu.make_async_remote_copy(
             src_ref=genes_ref,
             dst_ref=genes_box.at[cell],
@@ -611,7 +728,7 @@
         ).start()
         return carry
 
-    lax.fori_loop(1, group.cells, tell, 0)
+    lax.fori_loop(1, team.size, tell, 0)
     inverse1, inverse2 = stats_ref[0:1, :], stats_ref[1:2, :]
     count, scale = stats_ref[2:3, 0:1], stats_ref[3:4, 0:1]
     factor2 = inverse2 * pack_ref[2:3, :]
@@ -641,21 +758,10 @@
         0, cells // piece, gather, (zeros, zeros, jnp.zeros((depth, width), f32))
     )
 
-    def reduced(rows, box, sems):
-        box[everyone.me] = eight_rows(rows)
-        everyone.send(lambda other: box.at[everyone.me], box.at[everyone.me], sems)
-        others = box.at[pl.ds(0, everyone.size - 1)]
-
-        def finish():
-            await_bytes(others, sems.at[0])
-            await_bytes(others, sems.at[1])
-            return box_sum(box)
-
-        return finish
-
-    finish = reduced([row_sums(gains), row_sums(shifts)], box1, sems1)
+    finish = spread_box(team, box1, eight_rows([row_sums(gains), row_sums(shifts)]), sems1)
     group.send(lambda other: part_ref.at[:, part(other)], slab_box.at[group.me], slab_sems)
     slab_box[group.me] = part_ref[:, mine]
+    finish = spread_box(group, box2, finish(), sems2)
     swap1.wait()
     own, given = rows_of(far // 2), rows_of(cell // 2)
     half_give[...] = output_ref[bit, own] + output_box[own]
@@ -694,11 +800,8 @@
         [grad_sample + scaled * mean_z, grad_sample * log_factor + grad_log_own], axis=0
     )
     grad_normed1 = exact(pack_ref[heads_rows, :], grad_heads, 0, 0) * slope1
-    finish = reduced(
-        [row_sums(fold_lanes(grad_normed1 * centered1)), row_sums(fold_lanes(grad_normed1))],
-        box2,
-        sems2,
-    )
+    rows = [row_sums(fold_lanes(grad_normed1 * centered1)), row_sums(fold_lanes(grad_normed1))]
+    finish = spread_box(group, box4, spread_box(team, box3, eight_rows(rows), sems3)(), sems4)
     swap2.wait()
     output_sum_ref[bit, given] = output_sum_ref[bit, given] + half_box[...]
     swap3 = swap(output_sum_ref.at[bit, given], output_sum_ref.at[bit, given], far, 2)
@@ -712,7 +815,7 @@
     grad16_ref[:, mine] = grad_pre1.astype(bf16)
     group.send(lambda other: grad16_ref.at[:, mine], grad16_ref.at[:, mine], grad_sems)
     small_ref[depth + 4 * pad :, :] = exact(hot, grad_pre1, 1, 1)
-    others = genes_box.at[pl.ds(0, group.cells - 1)]
+    others = genes_box.at[pl.ds(0, team.size - 1)]
     await_bytes(others, genes_sems.at[0])
     await_bytes(others, genes_sems.at[1])
     genes_sum_ref[...] = box_sum(genes_box)
@@ -743,7 +846,6 @@
     width, slab = first.shape
     pad = sample.shape[0]
     genes_axis = lax.axis_size("gene")
-    devices = genes_axis * lax.axis_size("cell")
     return pl.pallas_call(
         functools.partial(middle_back_kernel, batches=batches, latent=noise.shape[0]),
         out_shape=[
@@ -758,14 +860,13 @@
         scratch_shapes=[
             pltpu.VMEM((pad, cells), f32),
             pltpu.VMEM((genes_axis, pad, slab), f32),
-            pltpu.VMEM((devices, 8, LANES), f32),
-            pltpu.VMEM((devices, 8, LANES), f32),
+            *row_boxes(),
             pltpu.VMEM(output_grad.shape[1:], f32),
             pltpu.VMEM((output_grad.shape[1] // 2, LANES), f32),
             pltpu.VMEM((output_grad.shape[1] // 2, LANES), f32),
-            pltpu.VMEM((devices // genes_axis, *genes_grad.shape), f32),
+            pltpu.VMEM((lax.axis_size("cell"), *genes_grad.shape), f32),
         ]
-        + [pltpu.SemaphoreType.DMA((2,))] * 4
+        + [pltpu.SemaphoreType.DMA((2,))] * 6
         + [pltpu.SemaphoreType.DMA((4, 2)), pltpu.SemaphoreType.DMA((2,))],
         compiler_params=talking(4),
         name="middle_back",
@@ -785,105 +886,176 @@
     )
 
 
-def last_sums_kernel(
-    grad_ref, small_ref, sum_ref, total_ref, box, half_box, half_give, small_box, sems, small_sems
+def encoder_grad_kernel(
+    counts_ref,
+    grad_ref,
+    small_ref,
+    sum_ref,
+    total_ref,
+    near_give,
+    near_box,
+    far_give,
+    far_box,
+    whole_box,
+    small_box,
+    near_sems,
+    far_sems,
+    last_sems,
+    small_sems,
 ):
-    group, everyone = Team(True), Team(False)
-    cell = lax.axis_index("cell")
-    bit, near, far = lax.rem(cell, 2), cell + 1 - 2 * lax.rem(cell, 2), lax.rem(cell + 2, 4)
-    high = cell // 2
-    size = grad_ref.shape[0]
-    half, quarter = size // 2, size // 4
-    everyone.greet()
-
-    def swap(source, target, other, sems):
-        copy = pltpu.make_async_remote_copy(
+    gene, cell = lax.axis_index("gene"), lax.axis_index("cell")
+    bit, high = lax.rem(cell, 2), cell // 2
+    near, far = cell + 1 - 2 * bit, lax.rem(cell + 2, 4)
+    quarter, cells = counts_ref.shape
+    step = pl.program_id(0)
+
+    def copy(source, target, sems, where):
+        return pltpu.make_async_remote_copy(
             src_ref=source,
             dst_ref=target,
             send_sem=sems.at[0],
             recv_sem=sems.at[1],
-            device_id=other,
+            device_id=where,
             device_id_type=MESH,
         )
-        copy.start()
-        return copy
-
-    total_ref[...] = small_ref[...]
-    rounds = []
-    for step in (1, 2):
-        other = near if step == 1 else far
-        rounds.append((group.gene, other))
-    step = 1
-    while step < group.genes:
-        flip = group.gene + step - 2 * step * lax.rem(group.gene // step, 2)
-        rounds.append((flip, cell))
-        step *= 2
-
-    def small_round(number):
+
+    rounds = [(gene, near), (gene, far)]
+    size = 1
+    while size < lax.axis_size("gene"):
+        rounds.append((gene + size - 2 * size * lax.rem(gene // size, 2), cell))
+        size *= 2
+
+    def small_copy(number):
         source = small_ref if number == 0 else small_box.at[1, number - 1]
-        return swap(source, small_box.at[0, number], rounds[number], small_sems.at[number])
-
-    def small_end(copy, number):
-        copy.wait()
+        return copy(source, small_box.at[0, number], small_sems.at[number], rounds[number])
+
+    def small_end(number):
+        small_copy(number).wait()
         source = small_ref[...] if number == 0 else small_box[1, number - 1]
         small_box[1, number] = source + small_box[0, number]
 
-    def half_of(number):
-        return pl.ds(pl.multiple_of(number * half, 8), half)
-
-    def quarter_of(number):
-        return pl.ds(pl.multiple_of(bit * half + number * quarter, 8), quarter)
-
-    copy = swap(grad_ref.at[half_of(1 - bit)], box, (group.gene, near), sems.at[0])
-    small = small_round(0)
-    copy.wait()
-
-    def inside(number):
-        return pl.ds(pl.multiple_of(number * quarter, 8), quarter)
-
-    half_give[...] = grad_ref[quarter_of(1 - high), :] + box[inside(1 - high), :]
-    copy = swap(half_give, half_box, (group.gene, far), sems.at[1])
-    small_end(small, 0)
-    small = small_round(1)
-    small_end(small, 1)
-    small = small_round(2)
-    copy.wait()
-    mine = quarter_of(high)
-    sum_ref[mine, :] = grad_ref[mine, :] + box[inside(high), :] + half_box[...]
-    copy = swap(sum_ref.at[mine], sum_ref.at[mine], (group.gene, far), sems.at[2])
-    small_end(small, 2)
-    for number in range(3, len(rounds)):
-        small_end(small_round(number), number)
-    total_ref[...] = small_box[1, len(rounds) - 1]
-    copy.wait()
-    copy = swap(sum_ref.at[half_of(bit)], sum_ref.at[half_of(bit)], (group.gene, near), sems.at[3])
-    copy.wait()
-
-
-def last_sums(grad, small):
+    def rows_of(bit, high):
+        return pl.ds(pl.multiple_of((2 * bit + high) * quarter, ROWS), quarter)
+
+    def near_copy(number):
+        return copy(near_give.at[number], near_box.at[number], near_sems.at[number], (gene, near))
+
+    far_copy = copy(far_give, far_box, far_sems, (gene, far))
+
+    def last_copy(number, high, other):
+        rows = rows_of(bit, high)
+        return copy(whole_box.at[rows], whole_box.at[rows], last_sems.at[number], (gene, other))
+
+    @pl.when(step == 0)
+    def _():
+        barrier = pltpu.get_barrier_semaphore()
+        for where in rounds:
+            pl.semaphore_signal(barrier, inc=1, device_id=where, device_id_type=MESH)
+        pl.semaphore_wait(barrier, len(rounds))
+        small_copy(0).start()
+
+    piece = pick_chunk(cells, 512)
+
+    def part():
+        total = jnp.zeros((quarter, LANES), f32)
+        for at in range(0, cells, piece):
+            columns = slice(at, at + piece)
+            inputs = jnp.log(counts_ref[:, columns].astype(f32) + 1.0).astype(bf16)
+            total = total + lax.dot_general(
+                inputs,
+                grad_ref[:, columns],
+                (((1,), (1,)), ((), ())),
+                preferred_element_type=f32,
+            )
+        return total
+
+    value = part()
+
+    @pl.when(step < 2)
+    def _():
+        near_give[step] = value
+        near_copy(step).start()
+
+    @pl.when(step == 1)
+    def _():
+        small_end(0)
+        small_copy(1).start()
+
+    @pl.when(step == 2)
+    def _():
+        near_copy(0).wait()
+        far_give[...] = value + near_box[0]
+        far_copy.start()
+        small_end(1)
+        small_copy(2).start()
+
+    @pl.when(step == 3)
+    def _():
+        near_copy(1).wait()
+        total = value + near_box[1]
+        small_end(2)
+        if len(rounds) > 3:
+            small_copy(3).start()
+        far_copy.wait()
+        whole_box[rows_of(bit, high), :] = total + far_box[...]
+        own_far, own_near = last_copy(0, high, far), last_copy(1, high, near)
+        own_far.start()
+        own_near.start()
+        for number in range(3, len(rounds)):
+            small_end(number)
+            if number + 1 < len(rounds):
+                small_copy(number + 1).start()
+        total_ref[...] = small_box[1, len(rounds) - 1]
+        own_far.wait()
+        passed = last_copy(2, 1 - high, near)
+        passed.start()
+        own_near.wait()
+        passed.wait()
+        sum_ref[...] = whole_box[...]
+
+
+def encoder_grad(counts_t, grad, small):
+    genes, cells = counts_t.shape
+    quarter = ROWS * pl.cdiv(genes, 4 * ROWS)
     rounds = 2
     while 2 ** (rounds - 2) < lax.axis_size("gene"):
         rounds += 1
-    size = grad.shape[0]
+
+    def quarter_of(i):
+        cell = lax.axis_index("cell")
+        bit, high = lax.rem(cell, 2), cell // 2
+        half = lax.rem(bit + 1 + i // 2, 2)
+        return (2 * half + lax.rem(high + 1 + i, 2), 0)
+
+    box = pltpu.VMEM((2, quarter, LANES), f32)
+    one = pltpu.VMEM((quarter, LANES), f32)
     return pl.pallas_call(
-        last_sums_kernel,
+        encoder_grad_kernel,
+        grid=(4,),
+        in_specs=[pl.BlockSpec((quarter, cells), quarter_of), whole(grad), whole(small)],
+        out_specs=[
+            pl.BlockSpec((4 * quarter, LANES), lambda i: (0, 0)),
+            pl.BlockSpec(small.shape, lambda i: (0, 0)),
+        ],
         out_shape=[
-            jax.ShapeDtypeStruct(grad.shape, f32),
+            jax.ShapeDtypeStruct((4 * quarter, LANES), f32),
             jax.ShapeDtypeStruct(small.shape, f32),
         ],
-        in_specs=[IN_VMEM] * 2,
-        out_specs=[IN_VMEM] * 2,
         scratch_shapes=[
-            pltpu.VMEM((size // 2, LANES), f32),
-            pltpu.VMEM((size // 4, LANES), f32),
-            pltpu.VMEM((size // 4, LANES), f32),
+            box,
+            box,
+            one,
+            one,
+            pltpu.VMEM((4 * quarter, LANES), f32),
             pltpu.VMEM((2, rounds, *small.shape), f32),
-            pltpu.SemaphoreType.DMA((4, 2)),
+            pltpu.SemaphoreType.DMA((2, 2)),
+            pltpu.SemaphoreType.DMA((2,)),
+            pltpu.SemaphoreType.DMA((3, 2)),
             pltpu.SemaphoreType.DMA((rounds, 2)),
         ],
         compiler_params=talking(5),
-        name="last_sums",
-    )(grad, small)
+        name="encoder_grad",
+    )(counts_t, grad, small)
 
 
 def update_kernel(*refs):
@@ -972,7 +1144,7 @@
 
 
 def totals_kernel(hidden_ref, weight_ref, out_ref, long_ref, even_ref, odd_ref, *, genes, chunk):
-    full, groups, tail = split_rows(genes)
+    full, groups, tail = split_rows(genes, 26)
     block = ROWS * groups
     blocks = full // groups
     values = (even_ref, odd_ref)
@@ -1014,8 +1186,8 @@
 
 def totals(hidden, weights, genes):
     width, cells = hidden.shape
-    chunk = pick_chunk(cells, 512)
-    groups = split_rows(genes)[1]
+    chunk = pick_chunk(cells, 2048)
+    groups = split_rows(genes, 26)[1]
     return pl.pallas_call(
         functools.partial(totals_kernel, genes=genes, chunk=chunk),
         grid=(cells // chunk,),
@@ -1244,7 +1416,7 @@
     genes,
     chunk,
 ):
-    full, groups, tail = split_rows(genes)
+    full, groups, tail = split_rows(genes, 26)
     block = ROWS * groups
     blocks = full // groups
     size = weight_ref.shape[1]
@@ -1315,8 +1487,8 @@
 def frequency(slopes, hidden, rows, pull, share, other, weights, second, dropout, theta, scale, genes):
     size, cells = slopes.shape
     width = hidden.shape[0]
-    chunk = pick_chunk(cells, 512)
-    groups = split_rows(genes)[1]
+    chunk = pick_chunk(cells, 1024)
+    groups = split_rows(genes, 26)[1]
     row = column_blocks(1, chunk)
     wide = column_blocks(width, chunk)
     return pl.pallas_call(
@@ -1344,39 +1516,25 @@
     )(slopes, hidden, rows, pull, share, other, weights, second, dropout, theta, scale)
 
 
-def encoder_back_kernel(counts_ref, grad_ref, weight_ref, input_ref, weight_grad_ref):
-    inputs = jnp.log(counts_ref[...].astype(f32) + 1.0).astype(bf16)
-    weight_grad_ref[...] = lax.dot_general(
-        inputs, grad_ref[...], (((1,), (1,)), ((), ())), preferred_element_type=f32
-    )
+def input_grad_kernel(grad_ref, weight_ref, input_ref):
     input_ref[...] = jnp.dot(
         weight_ref[...].astype(bf16), grad_ref[...], preferred_element_type=f32
     )
 
 
-def encoder_back(counts_t, grad, weight):
-    genes, cells = counts_t.shape
-    width = grad.shape[0]
-    block = LANES
+def encoder_input_grad(grad, weight):
+    width, cells = grad.shape
+    genes = weight.shape[0]
+    block = 2 * LANES
     return pl.pallas_call(
-        encoder_back_kernel,
+        input_grad_kernel,
         grid=(pl.cdiv(genes, block),),
-        in_specs=[
-            pl.BlockSpec((block, cells), lambda i: (i, 0)),
-            whole(grad),
-            pl.BlockSpec((block, width), lambda i: (i, 0)),
-        ],
-        out_specs=[
-            pl.BlockSpec((block, cells), lambda i: (i, 0)),
-            pl.BlockSpec((block, width), lambda i: (i, 0)),
-        ],
-        out_shape=[
-            jax.ShapeDtypeStruct((genes, cells), f32),
-            jax.ShapeDtypeStruct((-(-genes // 32) * 32, width), f32),
-        ],
+        in_specs=[whole(grad), pl.BlockSpec((block, width), lambda i: (i, 0))],
+        out_specs=pl.BlockSpec((block, cells), lambda i: (i, 0)),
+        out_shape=jax.ShapeDtypeStruct((genes, cells), f32),
         compiler_params=PARAMS,
-        name="encoder_back",
-    )(counts_t, grad, weight)
+        name="input_grad",
+    )(grad, weight)
 
 
 def local(
@@ -1420,30 +1578,20 @@
 
     counts_t = counts.T
     output_rows = by_gene(output_weight)
-    weights, *gene_tables = prepare(output_rows, gene_vectors, genes)
 
     pad = 16
-    heads_t = jnp.pad(head_weight.T.reshape(2, latent, -1), ((0, 0), (0, pad - latent), (0, 0)))
-    bias_row = jnp.pad(head_bias.reshape(2, latent), ((0, 0), (0, pad - latent))).reshape(1, -1)
-    bias_row = jnp.pad(bias_row, ((0, 0), (0, LANES - 2 * pad)))
-    pack = jnp.concatenate(
-        [
-            layer_norm_params,
-            bias_row,
-            jnp.zeros((3, LANES), f32),
-            decoder_input[:latent],
-            jnp.zeros((pad - latent, LANES), f32),
-            decoder_input[latent:],
-            heads_t.reshape(2 * pad, -1),
-            batch_shift,
-        ],
-        axis=0,
+    small_weights = (
+        layer_norm_params,
+        head_bias[None, :],
+        decoder_input,
+        head_weight.T,
+        batch_shift,
     )
     index, valid, noise = batch_index[None, :], valid_mask[None, :], noise_draw.T
 
-    encoded = encode(counts_t, encoder_weight)
-    hidden2, centered2, sample, share, stats, centered1, heads, rest_rows = middle(
-        encoded, index, valid, noise, pack, batches, pad, genes_all
+    encoded, weights, *gene_tables = encode(counts_t, encoder_weight, output_rows, gene_vectors)
+    hidden2, centered2, sample, share, stats, centered1, heads, rest_rows, pack = middle(
+        encoded, index, valid, noise, small_weights, batches, pad, genes_all
     )
     rows = combine_tops(totals(hidden2, weights, genes), rest_rows)
     slopes, sums, grad_hidden2, grad_out1, grad_bias1, grad_theta = likelihood(
@@ -1481,8 +1629,8 @@
         grad_genes,
         batches,
     )
-    input_grad, grad_encoder = encoder_back(counts_t, grad_pre16, encoder_weight)
-    grad_encoder, small = last_sums(grad_encoder, small)
+    grad_encoder, small = encoder_grad(counts_t, grad_pre16, small)
+    input_grad = encoder_input_grad(grad_pre16, encoder_weight)
     depth = pad + batches
     grad_mixing = jnp.concatenate([small[:latent], small[pad:depth]], axis=0)
     grad_heads = small[depth : depth + 2 * pad].reshape(2, pad, -1)[:, :latent]

time: 486 us -> 397 us (0.82)
  Pallas kernels: 467 us -> 387 us
  local copies, waits for them, and re-layouts: 10.3 us -> 1.59 us
    pallas_call x1, Pallas kernels: 81.4 us -> 25.9 us  [middle(): pl.pallas_call(functools.partial(middle_kernel, batches=batches, latent=n...]
    pallas_call x4 -> x3, Pallas kernels: 113 us -> 99.2 us  [the longest x1 46.8 us: encode(): pl.pallas_call(functools.partial(encode_kernel, genes=genes, table_blocks...]
    pallas_call x1, Pallas kernels: 20.3 us -> 13.9 us  [totals(): pl.pallas_call(functools.partial(totals_kernel, genes=genes, chunk=chunk)...]
    concatenate x1 -> x0, local copies, waits for them, and re-layouts: 5.69 us -> none  [local(): jnp.concatenate([layer_norm_params, bias_row, jnp.zeros((3, LANES), f32),...]
    pallas_call x1, Pallas kernels: 41.4 us -> 36.5 us  [frequency(): pl.pallas_call(functools.partial(frequency_kernel, genes=genes, chunk=chu...]
where the time goes in v4:
time: 397 us; the launch traced here: 396 us
  Pallas kernels  387 us (97%)
  other arithmetic  6 us (2%)
    pallas_call x1, Pallas kernels, likelihood(): pl.pallas_call(functools.partial(likelihood_kernel, genes=genes, chunk=ch...  122 us
    pallas_call x1, Pallas kernels, middle_back(): pl.pallas_call(functools.partial(middle_back_kernel, batches=batches, lat...  53.2 us
    pallas_call x1, Pallas kernels, encode(): pl.pallas_call(functools.partial(encode_kernel, genes=genes, table_blocks...  46.8 us
    pallas_call x1, Pallas kernels, frequency(): pl.pallas_call(functools.partial(frequency_kernel, genes=genes, chunk=chu...  36.5 us
    pallas_call x1, Pallas kernels, encoder_grad(): pl.pallas_call(encoder_grad_kernel, grid=(4,), in_specs=[pl.BlockSpec((qu...  36.5 us
    pallas_call x1, Pallas kernels, middle(): pl.pallas_call(functools.partial(middle_kernel, batches=batches, latent=n...  25.9 us
    pallas_call x1, Pallas kernels, encoder_input_grad(): pl.pallas_call(input_grad_kernel, grid=(pl.cdiv(genes, block),), in_specs...  15.9 us
    pallas_call x1, Pallas kernels, totals(): pl.pallas_call(functools.partial(totals_kernel, genes=genes, chunk=chunk)...  13.9 us

profile of v4, /device:TPU:0, one launch (start us, length us, event | category | flops | bytes accessed | tf_op | source)
XLA Modules:
  0.0 395.7 jit_solution(16814936163697737784)
XLA Ops:
  0.7 46.8 %encode.1 = (f32[136,512]{1,0:T(8,128)}, bf16[2,2512,256]{2,1,0:T(8,128)(2,1)}, f32[2512,128]{1,0:T(8,128)}, f32[2512,128]{1,0:T(8,128)}, f32[2512,128]{1,0:T(8,...) custom-call(s32[2500,4096]{1,0:T(8,128)} %bitcast.38, f32[2500,128]{1,0:T(8,128)} %refs_0_.1, f32[5000,128]{1,0:T(8,128)} %bitcast.42, ...), custom_call_target="tpu_custom_call" | custom-call | tf_op jit(solution)/shard_map/encode/pallas_call | solution.py:375
  47.5 25.9 %middle.1 = (bf16[128,4096]{1,0:T(8,128)(2,1)}, f32[128,4096]{1,0:T(8,128)}, f32[16,4096]{1,0:T(8,128)}, f32[1,4096]{1,0:T(1,128)}, f32[8,128]{1,0:T(8,128)}, /*...) custom-call(f32[136,512]{1,0:T(8,128)} %get-tuple-element.64.encoded_ref, ...), custom_call_target="tpu_custom_call" | custom-call | tf_op jit(solution)/shard_map/middle/pallas_call | solution.py:535
  73.4 13.9 %totals.1.tops_ref = f32[2,4096]{1,0:T(2,128)} custom-call(bf16[128,4096]{1,0:T(8,128)(2,1)} %get-tuple-element.65.hidden_ref, bf16[2,2512,256]{2,1,0:T(8,128)(2,1)} %get-tuple-element.66.weight_ref), custom_call_target="tpu_custom_call" | custom-call | tf_op jit(solution)/shard_map/totals/pallas_call | solution.py:1191
  87.3 11.4 %combine_tops.1.rows_ref = f32[4,4096]{1,0:T(4,128)} custom-call(f32[2,4096]{1,0:T(2,128)} %totals.1.tops_ref, f32[2,512]{1,0:T(2,128)} %get-tuple-element.67.rest_ref), custom_call_target="tpu_custom_call" | custom-call | tf_op jit(solution)/shard_map/combine_tops/pallas_call | solution.py:596
  98.7 121.6 %likelihood.1 = (f32[2512,4096]{1,0:T(8,128)}, f32[2,4096]{1,0:T(2,128)}, f32[128,4096]{1,0:T(8,128)}, f32[2512,128]{1,0:T(8,128)}, f32[2512,128]{1,0:T(8,128)}, /*index=5*/f32[2512,128]{1,0:T(8,128)}) custom-call(s32[2500,4096]{1,0:T(8,128)} %bitcast.39, bf16[128,4096]{1,0:T(8,128)(2,1)} %get-tuple-element.65.hidden_ref, f32[4,4096]{1,0:T(4,128)} %combine_tops.1.rows_ref, ...), custom_call_target="tpu_custom_call" | custom-call | tf_op jit(solution)/shard_map/likelihood/pallas_call | solution.py:1368
  220.3 12.8 %combine_sums.1.pull_ref = f32[2,4096]{1,0:T(2,128)} custom-call(f32[2,4096]{1,0:T(2,128)} %get-tuple-element.74.sums_ref, f32[4,4096]{1,0:T(4,128)} %combine_tops.1.rows_ref, f32[2,512]{1,0:T(2,128)} %get-tuple-element.67.rest_ref, s32[1,4096]{1,0:T(1,128)} %bitcast.49), custom_call_target="tpu_custom_call" | custom-call | tf_op jit(solution)/shard_map/combine_sums/pallas_call | solution.py:635
  233.1 0.0 copy-start
  233.1 36.5 %frequency.1 = (f32[128,4096]{1,0:T(8,128)}, f32[2,2512,128]{2,1,0:T(8,128)}, f32[4,2512]{1,0:T(4,128)}) custom-call(f32[2512,4096]{1,0:T(8,128)} %get-tuple-element.75.slopes_ref, bf16[128,4096]{1,0:T(8,128)(2,1)} %get-tuple-element.65.hidden_ref, f32[4,4096]{1,0:T(4,128)} %combine_tops.1.rows_ref, f32[2,4096]{1,0:T(2,128)} %combine_sums.1.pull_ref, ...), custom_call_target="tpu_custom_call" | custom-call | tf_op jit(solution)/shard_map/frequency/pallas_call | solution.py:1494
  269.6 0.0 copy-done
  269.6 0.6 slice.30
  270.3 0.0 copy-start.13
  270.3 0.0 copy-start.14
  270.3 0.0 copy-start.15
  270.3 0.0 copy-start.1
  270.3 0.0 copy-start.5
  270.3 0.0 copy-start.6
  270.3 53.2 %middle_back.1 = (bf16[128,4096]{1,0:T(8,128)(2,1)}, f32[144,128]{1,0:T(8,128)}, f32[8,128]{1,0:T(8,128)}, f32[2,2512,128]{2,1,0:T(8,128)}, f32[4,2512]{1,0:T(4,128)}) custom-call(f32[128,4096]{1,0:T(8,128)} %get-tuple-element.80.grad_ref, f32[128,4096]{1,0:T(8,128)} %get-tuple-element.81.centered_ref, f32[16,4096]{1,0:T(8,128)} %get-tuple-element.82.sample_ref, ...), custom_call_target="tpu_custom_call" | custom-call | tf_op jit(solution)/shard_map/middle_back/pallas_call | solution.py:849
  323.5 0.0 copy-done.13
  323.6 0.0 copy-done.14
  323.6 0.0 copy-done.15
  323.6 1.3 multiply_add_fusion.7
  324.8 0.0 copy-done.1
  324.8 0.0 copy-done.5
  324.8 0.0 copy-done.6
  324.9 1.5 multiply_add_fusion
  326.3 0.0 copy-start.3
  326.3 0.0 copy-start.9
  326.3 0.0 copy-start.10
  326.3 0.0 copy-start.16
  326.3 0.0 copy-start.17
  326.3 0.0 copy-start.18
  326.4 0.0 copy-start.4
  326.4 0.0 copy-start.11
  326.4 0.0 copy-start.12
  326.4 0.0 copy-start.2
  326.4 0.0 copy-start.7
  326.4 0.0 copy-start.8
  326.4 36.5 %encoder_grad.1 = (f32[2560,128]{1,0:T(8,128)}, f32[144,128]{1,0:T(8,128)}) custom-call(s32[2500,4096]{1,0:T(8,128)} %bitcast.40, bf16[128,4096]{1,0:T(8,128)(2,1)} %get-tuple-element.89.grad_ref, f32[144,128]{1,0:T(8,128)} %get-tuple-element.90.small_ref), custom_call_target="tpu_custom_call" | custom-call | tf_op jit(solution)/shard_map/encoder_grad/pallas_call | solution.py:1032
  362.9 0.7 slice.38
  363.6 0.0 copy-done.3
  363.6 0.0 copy-done.9
  363.7 0.0 copy-done.10
  363.7 1.5 fusion.3
  365.2 0.1 reshape.88
  365.2 0.1 reshape.89
  365.3 0.0 copy-done.16
  365.3 0.0 copy-done.17
  365.3 0.0 copy-done.18
  365.3 0.5 multiply_add_fusion.9
  365.9 0.0 copy-done.4
  365.9 0.0 copy-done.11
  365.9 0.0 copy-done.12
  365.9 0.6 multiply_add_fusion.6
  366.5 0.0 copy-done.2
  366.5 0.0 copy-done.7
  366.5 0.0 copy-done.8
  366.5 0.6 multiply_add_fusion.2
  367.1 12.6 %update.1 = (f32[2500,128]{1,0:T(8,128)}, f32[2500,128]{1,0:T(8,128)}, f32[2500,128]{1,0:T(8,128)}, f32[5000,128]{1,0:T(8,128)}, f32[5000,128]{1,0:T(8,128)}, /*index=5*/f32[5000,128]{1,0:T(8,128)}) custom-call(f32[2500,128]{1,0:T(8,128)} %refs_0_.1, f32[2500,128]{1,0:T(8,128)} %refs_1_.1, f32[2500,128]{1,0:T(8,128)} %refs_2_.1, ...), custom_call_target="tpu_custom_call" | custom-call | tf_op jit(solution)/shard_map/update/pallas_call | solution.py:1081
  379.8 15.9 %input_grad.1 = f32[2500,4096]{1,0:T(8,128)} custom-call(bf16[128,4096]{1,0:T(8,128)(2,1)} %get-tuple-element.89.grad_ref, f32[2500,128]{1,0:T(8,128)} %refs_0_.1), custom_call_target="tpu_custom_call" | custom-call | tf_op jit(solution)/shard_map/input_grad/pallas_call | solution.py:1529
  (1 shorter events, 0.0 us)
Async XLA Ops:
  233.1 36.5 %copy-start = (f32[2,4096]{1,0:T(2,128)S(1)}, f32[2,4096]{1,0:T(2,128)}, u32[]{:S(2)}) copy-start(f32[2,4096]{1,0:T(2,128)} %combine_sums.1.pull_ref) | copy-start | bytes 98308
  270.3 53.3 %copy-start.13 = (f32[4,128]{1,0:T(4,128)S(1)}, f32[4,128]{1,0:T(4,128)}, u32[]{:S(2)}) copy-start(f32[4,128]{1,0:T(4,128)} %norms_ref.1) | copy-start | bytes 6148
  270.3 53.3 %copy-start.14 = (f32[4,128]{1,0:T(4,128)S(1)}, f32[4,128]{1,0:T(4,128)}, u32[]{:S(2)}) copy-start(f32[4,128]{1,0:T(4,128)} %param.52) | copy-start | bytes 6148
  270.3 53.3 %copy-start.15 = (f32[4,128]{1,0:T(4,128)S(1)}, f32[4,128]{1,0:T(4,128)}, u32[]{:S(2)}) copy-start(f32[4,128]{1,0:T(4,128)} %param.44) | copy-start | bytes 6148
  270.3 54.6 %copy-start.1 = (f32[3,2500]{1,0:T(4,128)S(1)}, f32[3,2500]{1,0:T(4,128)}, u32[]{:S(2)}) copy-start(f32[3,2500]{1,0:T(4,128)} %vectors_ref.1) | copy-start | bytes 90004
  270.3 54.6 %copy-start.5 = (f32[3,2500]{1,0:T(4,128)S(1)}, f32[3,2500]{1,0:T(4,128)}, u32[]{:S(2)}) copy-start(f32[3,2500]{1,0:T(4,128)} %param.50) | copy-start | bytes 90004
  270.3 54.6 %copy-start.6 = (f32[3,2500]{1,0:T(4,128)S(1)}, f32[3,2500]{1,0:T(4,128)}, u32[]{:S(2)}) copy-start(f32[3,2500]{1,0:T(4,128)} %param.42) | copy-start | bytes 90004
  326.3 37.3 %copy-start.3 = (f32[32,128]{1,0:T(8,128)S(1)}, f32[32,128]{1,0:T(8,128)}, u32[]{:S(2)}) copy-start(f32[32,128]{1,0:T(8,128)} %shift_ref.1) | copy-start | bytes 49156
  326.3 37.3 %copy-start.9 = (f32[32,128]{1,0:T(8,128)S(1)}, f32[32,128]{1,0:T(8,128)}, u32[]{:S(2)}) copy-start(f32[32,128]{1,0:T(8,128)} %param.43) | copy-start | bytes 49156
  326.3 37.3 %copy-start.10 = (f32[32,128]{1,0:T(8,128)S(1)}, f32[32,128]{1,0:T(8,128)}, u32[]{:S(2)}) copy-start(f32[32,128]{1,0:T(8,128)} %param.51) | copy-start | bytes 49156
  326.3 39.0 %copy-start.16 = (f32[20]{0:T(128)S(1)}, f32[20]{0:T(128)}, u32[]{:S(2)}) copy-start(f32[20]{0:T(128)} %param.38) | copy-start | bytes 244
  326.3 39.0 %copy-start.17 = (f32[20]{0:T(128)S(1)}, f32[20]{0:T(128)}, u32[]{:S(2)}) copy-start(f32[20]{0:T(128)} %param.54) | copy-start | bytes 244
  326.3 39.0 %copy-start.18 = (f32[20]{0:T(128)S(1)}, f32[20]{0:T(128)}, u32[]{:S(2)}) copy-start(f32[20]{0:T(128)} %param.46) | copy-start | bytes 244
  326.4 39.5 %copy-start.4 = (f32[128,20]{0,1:T(8,128)S(1)}, f32[128,20]{0,1:T(8,128)}, u32[]{:S(2)}) copy-start(f32[128,20]{0,1:T(8,128)} %param.37) | copy-start | bytes 30724
  326.4 39.5 %copy-start.11 = (f32[128,20]{0,1:T(8,128)S(1)}, f32[128,20]{0,1:T(8,128)}, u32[]{:S(2)}) copy-start(f32[128,20]{0,1:T(8,128)} %param.53) | copy-start | bytes 30724
  326.4 39.5 %copy-start.12 = (f32[128,20]{0,1:T(8,128)S(1)}, f32[128,20]{0,1:T(8,128)}, u32[]{:S(2)}) copy-start(f32[128,20]{0,1:T(8,128)} %param.45) | copy-start | bytes 30724
  326.4 40.1 %copy-start.2 = (f32[42,128]{1,0:T(8,128)S(1)}, f32[42,128]{1,0:T(8,128)}, u32[]{:S(2)}) copy-start(f32[42,128]{1,0:T(8,128)} %mixing_ref.1) | copy-start | bytes 64516
  326.4 40.1 %copy-start.7 = (f32[42,128]{1,0:T(8,128)S(1)}, f32[42,128]{1,0:T(8,128)}, u32[]{:S(2)}) copy-start(f32[42,128]{1,0:T(8,128)} %param.55) | copy-start | bytes 64516
  326.4 40.1 %copy-start.8 = (f32[42,128]{1,0:T(8,128)S(1)}, f32[42,128]{1,0:T(8,128)}, u32[]{:S(2)}) copy-start(f32[42,128]{1,0:T(8,128)} %param.47) | copy-start | bytes 64516

commit v5 on v4

--- a/solution.py
+++ b/solution.py
@@ -146,6 +146,89 @@
     return [pltpu.VMEM(shape, f32) for shape in shapes * 2]
 
 
+class Gather:
+    def __init__(self, ref, slab, far_sems, near_sems):
+        self.ref, self.slab = ref, slab
+        self.gene, self.cell = lax.axis_index("gene"), lax.axis_index("cell")
+        self.pairs = lax.axis_size("gene") // 2
+        self.high, self.low = self.gene // 2, lax.rem(self.gene, 2)
+        self.far_sems, self.near_sems = far_sems, near_sems
+
+    def copy(self, source_high, target, sems):
+        columns = pl.ds(
+            pl.multiple_of((2 * source_high + self.low) * self.slab, LANES), self.slab
+        )
+        return pltpu.make_async_remote_copy(
+            src_ref=self.ref.at[:, columns],
+            dst_ref=self.ref.at[:, columns],
+            send_sem=sems.at[0],
+            recv_sem=sems.at[1],
+            device_id=(target, self.cell),
+            device_id_type=MESH,
+        )
+
+    def far(self, d):
+        target = 2 * lax.rem(self.high + d, self.pairs) + self.low
+        return self.copy(self.high, target, self.far_sems.at[d - 1])
+
+    def near(self, d):
+        source = lax.rem(self.high - d + self.pairs, self.pairs)
+        return self.copy(source, 2 * self.high + 1 - self.low, self.near_sems.at[d])
+
+    def start(self):
+        self.near(0).start()
+
+        def one(d, carry):
+            self.far(d).start()
+            return carry
+
+        lax.fori_loop(1, self.pairs, one, 0)
+
+    def finish(self):
+        def one(d, carry):
+            self.far(d).wait_recv()
+            self.near(d).start()
+            return carry
+
+        lax.fori_loop(1, self.pairs, one, 0)
+
+        def drain(d, carry):
+            self.near(d).wait()
+            return carry
+
+        lax.fori_loop(0, self.pairs, drain, 0)
+
+        def drain_far(d, carry):
+            self.far(d).wait_send()
+            return carry
+
+        lax.fori_loop(1, self.pairs, drain_far, 0)
+
+
+def gather_sems():
+    pairs = lax.axis_size("gene") // 2
+    return [pltpu.SemaphoreType.DMA((pairs, 2))] * 2
+
+
+class Shared:
+    def __init__(self, box, sems, chunk):
+        self.box, self.sems, self.team = box, sems, Team("gene")
+        start = pl.multiple_of(pl.program_id(0) * chunk, LANES)
+        self.here = pl.ds(start, chunk)
+
+    def send(self, first, second):
+        me = self.team.me
+        self.box[me, 0:1, self.here] = first
+        self.box[me, 1:2, self.here] = second
+        place = self.box.at[me, :, self.here]
+        self.team.send(lambda other: place, place, self.sems)
+
+    def finish(self):
+        others = self.box.at[pl.ds(0, self.team.size - 1)]
+        await_bytes(others, self.sems.at[0])
+        await_bytes(others, self.sems.at[1])
+
+
 def eight_rows(rows):
     filler = jnp.zeros((8 - len(rows), LANES), f32)
     return jnp.concatenate([*rows, filler], axis=0) if len(rows) < 8 else jnp.concatenate(rows, 0)
@@ -190,7 +273,7 @@
     theta_ref, log_ref, slope_ref, gammas_ref, digammas_ref = tables
     lane = lax.broadcasted_iota(jnp.int32, (LANES, LANES), 1)
     below = lax.broadcasted_iota(jnp.int32, (LANES, LANES), 0)
-    upper = jnp.where(below < lane, 1.0, 0.0)
+    upper = jnp.where(below < lane, 1.0, 0.0).astype(bf16)
     step = lane.astype(f32)
     block = theta_ref.shape[0]
     for at in range(0, block, LANES):
@@ -217,8 +300,22 @@
         log_ref[here, :] = log_theta
         slope_ref[here, :] = ln2 * log_theta + theta / (theta + rate_epsilon)
         climb = theta + step
-        gammas_ref[here, :] = exact(jnp.log2(climb / (step + 1.0)), upper, 1, 0)
-        digammas_ref[here, :] = exact(1.0 / climb, upper, 1, 0)
+        terms = jnp.concatenate([jnp.log2(climb / (step + 1.0)), 1.0 / climb], axis=0)
+        high = terms.astype(bf16)
+        rest = terms - high.astype(f32)
+        middle = rest.astype(bf16)
+        low = (rest - middle.astype(f32)).astype(bf16)
+        total = jnp.zeros((2 * LANES, LANES), f32)
+        for piece in (low, middle, high):
+            total = total + jnp.dot(piece, upper, preferred_element_type=f32)
+        gammas_ref[here, :] = total[0:LANES]
+        digammas_ref[here, :] = total[LANES:]
+
+
+def encode_order(step, steps):
+    last = step // (steps - 1)
+    given = 1 - (step + steps - 1) // steps + lax.rem(step, 2) * (1 - last)
+    return given, given * ((step + 1) // 2) + (1 - given) * (step // 2 - 1 + last)
 
 
 def encode_kernel(
@@ -246,13 +343,12 @@
     table_blocks,
 ):
     slab = counts_ref.shape[1]
-    full, _, tail = split_rows(genes)
     width = encoder_ref.shape[1]
     group = Team("gene")
     pairs = group.size // 2
     high, low = group.me // 2, lax.rem(group.me, 2)
     step = pl.program_id(0)
-    turn = step // 2
+    given, turn = encode_order(step, group.size)
 
     def place(high, low):
         return (2 * high + low, group.cell)
@@ -274,30 +370,36 @@
         for d in range(1, pairs):
             where = place(lax.rem(high + d, pairs), low)
             pl.semaphore_signal(barrier, inc=1, device_id=where, device_id_type=MESH)
-        weight_ref[0 : full * ROWS, :] = encoder_ref[0 : full * ROWS, :].astype(bf16)
-        if tail:
-            weight_ref[full * ROWS :, :] = tail_rows(
-                encoder_ref, full * ROWS, genes, slice(None), f32
-            ).astype(bf16)
+        for at in range(0, weight_ref.shape[1], LANES):
+            stop = min(at + LANES, genes)
+            piece = encoder_ref[at:stop, :]
+            if stop < at + LANES:
+                filler = jnp.zeros((at + LANES - stop, width), f32)
+                piece = jnp.concatenate([piece, filler], axis=0)
+            weight_ref[:, at : at + LANES] = jnp.transpose(piece).astype(bf16)
         pl.semaphore_wait(barrier, pairs)
 
     def part(ref):
-        def rows16(counted, rows, total):
-            inputs_ref[rows, :] = jnp.log(counted + 1.0).astype(bf16)
-            return total + counted[:8] + counted[8:]
-
-        def one(i, total):
-            rows = pl.ds(pl.multiple_of(i * ROWS, ROWS), ROWS)
-            return rows16(counts_ref[rows, :].astype(f32), rows, total)
-
-        total = lax.fori_loop(0, full, one, jnp.zeros((8, slab), f32), unroll=4)
-        if tail:
-            rows = pl.ds(full * ROWS, ROWS)
-            counted = tail_rows(counts_ref, full * ROWS, genes, slice(None), jnp.int32)
-            total = rows16(counted.astype(f32), rows, total)
-        ref[0:width, :] = lax.dot_general(
-            weight_ref[...], inputs_ref[...], (((0,), (0,)), ((), ())), preferred_element_type=f32
-        )
+        depth = 3 * LANES
+        total = jnp.zeros((8, slab), f32)
+        for number, at in enumerate(range(0, genes, depth)):
+            held = inputs_ref.at[number % 2]
+            stop = min(at + depth, genes)
+            for row in range(at, stop, ROWS):
+                if row + ROWS <= genes:
+                    counted = counts_ref[row : row + ROWS, :].astype(f32)
+                else:
+                    counted = tail_rows(counts_ref, row, genes, slice(None), jnp.int32).astype(f32)
+                held[row - at : row - at + ROWS, :] = jnp.log(counted + 1.0).astype(bf16)
+                total = total + counted[:8] + counted[8:]
+            here = padded(stop - at)
+            product = jnp.dot(
+                weight_ref[:, at : at + here], held[0:here, :], preferred_element_type=f32
+            )
+            if at == 0:
+                ref[0:width, :] = product
+            else:
+                ref[0:width, :] += product
         row = lax.broadcasted_iota(jnp.int32, (8, slab), 0)
         ref[width : width + 8, :] = jnp.where(row == 0, jnp.sum(total, axis=0, keepdims=True), 0.0)
 
@@ -314,12 +416,12 @@
     def _():
         prepare_tables(step, genes, output_ref, vectors_ref, weights_ref, tables)
 
-    @pl.when(lax.rem(step, 2) == 0)
+    @pl.when(given == 1)
     def _():
         part(near_give.at[turn])
         near_copy(turn).start()
 
-    @pl.when(lax.rem(step, 2) == 1)
+    @pl.when(given == 0)
     def _():
         part(out_ref)
         near_copy(turn).wait_recv()
@@ -360,11 +462,11 @@
 
     def slab_of(i):
         me = lax.axis_index("gene")
-        low = lax.rem(me + 1 + i, 2)
-        return (0, 2 * lax.rem(me // 2 + 1 + i // 2, pairs) + low)
+        given, turn = encode_order(i, devices)
+        return (0, 2 * lax.rem(me // 2 + 1 + turn, pairs) + lax.rem(me + given, 2))
 
     box = pltpu.VMEM((pairs, width + 8, slab), f32)
-    size = padded(genes)
+    size = 2 * ROWS * pl.cdiv(genes, 2 * ROWS)
     block = LANES * pl.cdiv(pl.cdiv(size, LANES), devices)
     table_blocks = pl.cdiv(size, block)
 
@@ -392,8 +494,8 @@
         ]
         + [jax.ShapeDtypeStruct((size, LANES), f32)] * 5,
         scratch_shapes=[
-            pltpu.VMEM((padded(genes), slab), bf16),
-            pltpu.VMEM((padded(genes), width), bf16),
+            pltpu.VMEM((2, 3 * LANES, slab), bf16),
+            pltpu.VMEM((width, LANES * pl.cdiv(genes, LANES)), bf16),
             box,
             box,
             box,
@@ -423,7 +525,6 @@
     stats_ref,
     first_ref,
     heads_ref,
-    rest_ref,
     pack_ref,
     box1,
     box2,
@@ -433,7 +534,8 @@
     sems2,
     sems3,
     sems4,
-    sample_sems,
+    sample_far,
+    sample_near,
     *,
     batches,
     latent,
@@ -467,7 +569,7 @@
     shift = exact(pack_ref[shift_rows, :], hot, 0, 0)
     gain1, bias1, gain2, bias2, head_bias = columns_of([pack_ref[i : i + 1, :] for i in range(5)])
     total = encoded_ref[...]
-    rest_ref[0:1, :] = total[width : width + 1, :]
+    library = total[width : width + 1, :]
     pre1 = total[0:width, :] + shift
 
     weighed = valid * pre1
@@ -491,11 +593,13 @@
     mean_z, log_var = heads[0:pad], heads[pad : 2 * pad]
     noise = jnp.concatenate([noise_ref[:, mine], jnp.zeros((pad - latent, slab), f32)], axis=0)
     sample = mean_z + jnp.exp(0.5 * log_var) * noise
-    rest_ref[1:2, :] = 0.5 * jnp.sum(
+    sample_ref[:, mine] = sample
+    sample_ref[pad - 2 : pad - 1, mine] = 0.5 * jnp.sum(
         mean_z * mean_z + jnp.exp(log_var) - log_var - 1.0, axis=0, keepdims=True
     )
-    sample_ref[:, mine] = sample
-    group.send(lambda other: sample_ref.at[:, mine], sample_ref.at[:, mine], sample_sems)
+    sample_ref[pad - 1 : pad, mine] = library
+    gathering = Gather(sample_ref, slab, sample_far, sample_near)
+    gathering.start()
     pre2 = exact(mixing, jnp.concatenate([sample, hot], axis=0), 0, 0)
     weighed = valid * pre2
     rows = [row_sums(fold_lanes(weighed)), row_sums(fold_lanes(weighed * pre2))]
@@ -508,9 +612,7 @@
     inverse2 = lax.rsqrt(sums[1:2] / count - mean2 * mean2 + norm_epsilon)
     stats_ref[...] = eight_rows([inverse1, inverse2, count, scale])
     mean_col, inverse_col = columns_of([mean2, inverse2])
-    others = sample_ref.at[:, pl.ds(0, (group.size - 1) * slab)]
-    await_bytes(others, sample_sems.at[0])
-    await_bytes(others, sample_sems.at[1])
+    gathering.finish()
     piece = pick_chunk(cells, 512)
 
     def decode(i, carry):
@@ -544,103 +646,14 @@
             jax.ShapeDtypeStruct((8, LANES), f32),
             jax.ShapeDtypeStruct((width, slab), f32),
             jax.ShapeDtypeStruct((2 * pad, slab), f32),
-            jax.ShapeDtypeStruct((2, slab), f32),
             jax.ShapeDtypeStruct((8 + 3 * pad + 2 * batches, LANES), f32),
         ],
         in_specs=[IN_VMEM] * 9,
-        out_specs=[IN_VMEM] * 9,
-        scratch_shapes=row_boxes() + [pltpu.SemaphoreType.DMA((2,))] * 5,
+        out_specs=[IN_VMEM] * 8,
+        scratch_shapes=row_boxes() + [pltpu.SemaphoreType.DMA((2,))] * 4 + gather_sems(),
         compiler_params=talking(1),
         name="middle",
     )(encoded, index, valid, noise, *small_weights)
-
-
-def tops_kernel(tops_ref, rest_ref, out_ref, box, sems, back_sems):
-    group = Team("gene")
-    slab = rest_ref.shape[1]
-
-    def part(other):
-        return pl.ds(pl.multiple_of(other * slab, LANES), slab)
-
-    mine = part(group.me)
-    greet(group)
-    group.send(lambda other: tops_ref.at[:, part(other)], box.at[group.me], sems)
-    box[group.me] = tops_ref[:, mine]
-    others = box.at[pl.ds(0, group.size - 1)]
-    await_bytes(others, sems.at[0])
-    await_bytes(others, sems.at[1])
-
-    def highest(i, best):
-        return jnp.maximum(best, box[i, 0:1, :])
-
-    top = lax.fori_loop(1, group.size, highest, box[0, 0:1, :])
-
-    def add(i, total):
-        return total + box[i, 1:2, :] * jnp.exp(box[i, 0:1, :] - top)
-
-    total = lax.fori_loop(0, group.size, add, jnp.zeros_like(top))
-    inverse = 1.0 / total
-    out_ref[0:1, mine] = top
-    out_ref[1:2, mine] = rest_ref[0:1, :] * inverse
-    out_ref[2:3, mine] = inverse
-    out_ref[3:4, mine] = inverse
-    group.send(lambda other: out_ref.at[:, mine], out_ref.at[:, mine], back_sems)
-    others = out_ref.at[:, pl.ds(0, (group.size - 1) * slab)]
-    await_bytes(others, back_sems.at[0])
-    await_bytes(others, back_sems.at[1])
-
-
-def combine_tops(tops, rest):
-    group = lax.axis_size("gene")
-    slab = rest.shape[1]
-    return pl.pallas_call(
-        tops_kernel,
-        out_shape=jax.ShapeDtypeStruct((4, tops.shape[1]), f32),
-        in_specs=[IN_VMEM] * 2,
-        out_specs=IN_VMEM,
-        scratch_shapes=[pltpu.VMEM((group, 2, slab), f32)] + [pltpu.SemaphoreType.DMA((2,))] * 2,
-        compiler_params=talking(2),
-        name="combine_tops",
-    )(tops, rest)
-
-
-def sums_kernel(sums_ref, rows_ref, rest_ref, valid_ref, out_ref, box, sems, back_sems, *, genes_all):
-    group = Team("gene")
-    slab = rest_ref.shape[1]
-
-    def part(other):
-        return pl.ds(pl.multiple_of(other * slab, LANES), slab)
-
-    mine = part(group.me)
-    greet(group)
-    group.send(lambda other: sums_ref.at[:, part(other)], box.at[group.me], sems)
-    box[group.me] = sums_ref[:, mine]
-    others = box.at[pl.ds(0, group.size - 1)]
-    await_bytes(others, sems.at[0])
-    await_bytes(others, sems.at[1])
-    total = box_sum(box)
-    out_ref[0:1, mine] = total[0:1] * rows_ref[2:3, mine]
-    out_ref[1:2, mine] = (
-        valid_ref[:, mine].astype(f32) * (total[1:2] + rest_ref[1:2, :]) / genes_all
-    )
-    group.send(lambda other: out_ref.at[:, mine], out_ref.at[:, mine], back_sems)
-    others = out_ref.at[:, pl.ds(0, (group.size - 1) * slab)]
-    await_bytes(others, back_sems.at[0])
-    await_bytes(others, back_sems.at[1])
-
-
-def combine_sums(sums, rows, rest, valid, genes_all):
-    group = lax.axis_size("gene")
-    slab = rest.shape[1]
-    return pl.pallas_call(
-        functools.partial(sums_kernel, genes_all=genes_all),
-        out_shape=jax.ShapeDtypeStruct((2, sums.shape[1]), f32),
-        in_specs=[IN_VMEM] * 4,
-        out_specs=IN_VMEM,
-        scratch_shapes=[pltpu.VMEM((group, 2, slab), f32)] + [pltpu.SemaphoreType.DMA((2,))] * 2,
-        compiler_params=talking(3),
-        name="combine_sums",
-    )(sums, rows, rest, valid)
 
 
 def middle_back_kernel(
@@ -676,7 +689,8 @@
     sems2,
     sems3,
     sems4,
-    grad_sems,
+    grad_far,
+    grad_near,
     output_sems,
     genes_sems,
     *,
@@ -766,7 +780,7 @@
     own, given = rows_of(far // 2), rows_of(cell // 2)
     half_give[...] = output_ref[bit, own] + output_box[own]
     swap2 = swap(half_give, half_box, far, 1)
-    output_sum_ref[bit, given] = output_ref[bit, given] + output_box[given]
+    output_sum_ref[given] = output_ref[bit, given] + output_box[given]
     hot = hot_rows(index_ref[:, mine], batches)
     valid = valid_ref[:, mine].astype(f32)
     mixed = valid * jnp.concatenate([sample_ref[:, mine], hot], axis=0)
@@ -803,8 +817,8 @@
     rows = [row_sums(fold_lanes(grad_normed1 * centered1)), row_sums(fold_lanes(grad_normed1))]
     finish = spread_box(group, box4, spread_box(team, box3, eight_rows(rows), sems3)(), sems4)
     swap2.wait()
-    output_sum_ref[bit, given] = output_sum_ref[bit, given] + half_box[...]
-    swap3 = swap(output_sum_ref.at[bit, given], output_sum_ref.at[bit, given], far, 2)
+    output_sum_ref[given] = output_sum_ref[given] + half_box[...]
+    swap3 = swap(output_sum_ref.at[given], output_sum_ref.at[given], far, 2)
     small_ref[depth : depth + 2 * pad, :] = exact(grad_heads, hidden1, 1, 1)
     small_ref[depth + 2 * pad : depth + 4 * pad, :] = fold_lanes(grad_heads)
     sums = finish()
@@ -813,18 +827,15 @@
     gain_col, shift_col = columns_of([gain1_grad, shift1_grad])
     grad_pre1 = factor1 * (grad_normed1 - share * (shift_col + centered1 * gain_col))
     grad16_ref[:, mine] = grad_pre1.astype(bf16)
-    group.send(lambda other: grad16_ref.at[:, mine], grad16_ref.at[:, mine], grad_sems)
+    gathering = Gather(grad16_ref, slab, grad_far, grad_near)
+    gathering.start()
     small_ref[depth + 4 * pad :, :] = exact(hot, grad_pre1, 1, 1)
+    gathering.finish()
     others = genes_box.at[pl.ds(0, team.size - 1)]
     await_bytes(others, genes_sems.at[0])
     await_bytes(others, genes_sems.at[1])
     genes_sum_ref[...] = box_sum(genes_box)
     swap3.wait()
-    swap4 = swap(output_sum_ref.at[bit], output_sum_ref.at[bit], near, 3)
-    swap4.wait()
-    others = grad16_ref.at[:, pl.ds(0, (group.size - 1) * slab)]
-    await_bytes(others, grad_sems.at[0])
-    await_bytes(others, grad_sems.at[1])
 
 
 def middle_back(
@@ -852,7 +863,7 @@
             jax.ShapeDtypeStruct((width, cells), bf16),
             jax.ShapeDtypeStruct((5 * pad + 2 * batches, LANES), f32),
             jax.ShapeDtypeStruct((8, LANES), f32),
-            jax.ShapeDtypeStruct(output_grad.shape, f32),
+            jax.ShapeDtypeStruct(output_grad.shape[1:], f32),
             jax.ShapeDtypeStruct(genes_grad.shape, f32),
         ],
         in_specs=[IN_VMEM] * 12,
@@ -866,8 +877,9 @@
             pltpu.VMEM((output_grad.shape[1] // 2, LANES), f32),
             pltpu.VMEM((lax.axis_size("cell"), *genes_grad.shape), f32),
         ]
-        + [pltpu.SemaphoreType.DMA((2,))] * 6
-        + [pltpu.SemaphoreType.DMA((4, 2)), pltpu.SemaphoreType.DMA((2,))],
+        + [pltpu.SemaphoreType.DMA((2,))] * 5
+        + gather_sems()
+        + [pltpu.SemaphoreType.DMA((3, 2)), pltpu.SemaphoreType.DMA((2,))],
         compiler_params=talking(4),
         name="middle_back",
     )(
@@ -890,8 +902,10 @@
     counts_ref,
     grad_ref,
     small_ref,
+    output_ref,
     sum_ref,
     total_ref,
+    output_sum_ref,
     near_give,
     near_box,
     far_give,
@@ -902,6 +916,8 @@
     far_sems,
     last_sems,
     small_sems,
+    output_box,
+    output_sems,
 ):
     gene, cell = lax.axis_index("gene"), lax.axis_index("cell")
     bit, high = lax.rem(cell, 2), cell // 2
@@ -946,13 +962,17 @@
         rows = rows_of(bit, high)
         return copy(whole_box.at[rows], whole_box.at[rows], last_sems.at[number], (gene, other))
 
+    output_copy = copy(output_box.at[bit], output_box.at[bit], output_sems, (gene, near))
+
     @pl.when(step == 0)
     def _():
+        output_box[bit] = output_ref[...]
         barrier = pltpu.get_barrier_semaphore()
         for where in rounds:
             pl.semaphore_signal(barrier, inc=1, device_id=where, device_id_type=MESH)
         pl.semaphore_wait(barrier, len(rounds))
         small_copy(0).start()
+        output_copy.start()
 
     piece = pick_chunk(cells, 512)
 
@@ -1012,9 +1032,11 @@
         own_near.wait()
         passed.wait()
         sum_ref[...] = whole_box[...]
-
-
-def encoder_grad(counts_t, grad, small):
+        output_copy.wait()
+        output_sum_ref[...] = output_box[...]
+
+
+def encoder_grad(counts_t, grad, small, output):
     genes, cells = counts_t.shape
     quarter = ROWS * pl.cdiv(genes, 4 * ROWS)
     rounds = 2
@@ -1032,14 +1054,17 @@
     return pl.pallas_call(
         encoder_grad_kernel,
         grid=(4,),
-        in_specs=[pl.BlockSpec((quarter, cells), quarter_of), whole(grad), whole(small)],
+        in_specs=[pl.BlockSpec((quarter, cells), quarter_of)]
+        + [whole(array) for array in (grad, small, output)],
         out_specs=[
             pl.BlockSpec((4 * quarter, LANES), lambda i: (0, 0)),
             pl.BlockSpec(small.shape, lambda i: (0, 0)),
+            pl.BlockSpec((2, *output.shape), lambda i: (0, 0, 0)),
         ],
         out_shape=[
             jax.ShapeDtypeStruct((4 * quarter, LANES), f32),
             jax.ShapeDtypeStruct(small.shape, f32),
+            jax.ShapeDtypeStruct((2, *output.shape), f32),
         ],
         scratch_shapes=[
             box,
@@ -1052,42 +1077,78 @@
             pltpu.SemaphoreType.DMA((2,)),
             pltpu.SemaphoreType.DMA((3, 2)),
             pltpu.SemaphoreType.DMA((rounds, 2)),
+            pltpu.VMEM((2, *output.shape), f32),
+            pltpu.SemaphoreType.DMA((2,)),
         ],
         compiler_params=talking(5),
         name="encoder_grad",
-    )(counts_t, grad, small)
-
-
-def update_kernel(*refs):
-    groups, outs = refs[:8], refs[8:]
-    encoder, output = groups[:4], groups[4:]
-    fresh, moment, mean = nesterov(*[ref[...] for ref in encoder], step_rates[0])
-    for ref, value in zip(outs[:3], (fresh, moment, mean)):
-        ref[...] = value
-    rows = output[3].shape[1]
+    )(counts_t, grad, small, output)
+
+
+def finish_kernel(*refs, pad, latent, batches):
+    grad16_ref, encoder_grad_ref, output_grad_ref, genes_grad_ref, small_ref, norms_ref = refs[:6]
+    ins, input_ref, outs = refs[6:30], refs[30], refs[31:]
+
+    def group(number):
+        return [part[8 * i + number] for part in (ins, outs) for i in range(3)]
+
+    def step(number, here, grad):
+        weight, momentum, average, *results = group(number)
+        old = [ref[here] for ref in (weight, momentum, average)]
+        for ref, value in zip(results, nesterov(*old, grad, step_rates[number])):
+            ref[here] = value
+
+    input_ref[...] = jnp.dot(
+        ins[0][...].astype(bf16), grad16_ref[...], preferred_element_type=f32
+    )
+    step(0, (slice(None), slice(None)), encoder_grad_ref[...])
     for k in range(2):
-        here = pl.ds(k, rows, stride=2)
-        old = [ref[here, :] for ref in output[:3]]
-        for ref, value in zip(outs[3:], nesterov(*old, output[3][k], step_rates[1])):
-            ref[here, :] = value
-
-
-def update(encoder, encoder_grad, output, output_grad):
-    genes = encoder[0].shape[0]
+        rows = pl.ds(k, output_grad_ref.shape[1], stride=2)
+        step(1, (rows, slice(None)), output_grad_ref[k])
+    step(2, (slice(None), slice(None)), genes_grad_ref[0:3, :])
+
+    @pl.when(pl.program_id(0) == 0)
+    def _():
+        depth = pad + batches
+        columns = slice(None)
+        step(3, (columns, columns), small_ref[depth + 4 * pad :, :])
+        step(4, (columns, columns), norms_ref[0:4, :])
+        step(7, (slice(0, latent), columns), small_ref[0:latent, :])
+        step(7, (slice(latent, None), columns), small_ref[pad:depth, :])
+        bias = exact(
+            jnp.ones((8, LANES), f32), small_ref[depth + 2 * pad : depth + 4 * pad, :], 1, 1
+        )
+        for half in range(2):
+            rows = slice(half * latent, (half + 1) * latent)
+            at = half * pad
+            step(5, (rows, columns), small_ref[depth + at : depth + at + latent, :])
+            step(6, (slice(None), rows), bias[0:1, at : at + latent])
+
+
+def finish(grad16, encoder_grad, output_grad, genes_grad, small, norms, states, pad, latent, batches):
+    width, cells = grad16.shape
+    genes = states[0][0].shape[0]
     block = 2 * LANES
     one = pl.BlockSpec((block, LANES), lambda i: (i, 0))
     two = pl.BlockSpec((2 * block, LANES), lambda i: (i, 0))
     both = pl.BlockSpec((2, block, LANES), lambda i: (0, i, 0))
-    return pl.pallas_call(
-        update_kernel,
+
+    def rows(count):
+        return pl.BlockSpec((count, block), lambda i: (0, i))
+
+    specs = [spec for state in states for spec in [one, two, rows(3), *map(whole, state[3:])]]
+    flat = [array for state in states for array in state]
+    results = pl.pallas_call(
+        functools.partial(finish_kernel, pad=pad, latent=latent, batches=batches),
         grid=(pl.cdiv(genes, block),),
-        in_specs=[one] * 4 + [two] * 3 + [both],
-        out_specs=[one] * 3 + [two] * 3,
-        out_shape=[jax.ShapeDtypeStruct(encoder[0].shape, f32)] * 3
-        + [jax.ShapeDtypeStruct(output[0].shape, f32)] * 3,
+        in_specs=[whole(grad16), one, both, rows(4), whole(small), whole(norms)] + specs,
+        out_specs=[pl.BlockSpec((block, cells), lambda i: (i, 0))] + specs,
+        out_shape=[jax.ShapeDtypeStruct((genes, cells), f32)]
+        + [jax.ShapeDtypeStruct(array.shape, f32) for array in flat],
         compiler_params=PARAMS,
-        name="update",
-    )(*encoder, encoder_grad, *output, output_grad)
+        name="finish",
+    )(grad16, encoder_grad, output_grad, genes_grad, small, norms, *flat)
+    return results[0], [results[1 + 8 * i : 9 + 8 * i] for i in range(3)]
 
 
 def fill_hidden(long_ref, hidden_ref, top):
@@ -1143,13 +1204,19 @@
     return [(k, slice(j, j + width)) for k in range(ks) for j in range(0, chunk, width)]
 
 
-def totals_kernel(hidden_ref, weight_ref, out_ref, long_ref, even_ref, odd_ref, *, genes, chunk):
+def totals_kernel(
+    hidden_ref, weight_ref, sample_ref, out_ref, long_ref, even_ref, odd_ref, box, sems, *, genes, chunk
+):
     full, groups, tail = split_rows(genes, 26)
     block = ROWS * groups
     blocks = full // groups
     values = (even_ref, odd_ref)
     fill_hidden(long_ref, hidden_ref, None)
     pieces = logit_pieces(1, chunk)
+
+    @pl.when(pl.program_id(0) == 0)
+    def _():
+        greet(Team("gene"))
 
     def logits(i, rows, size, which):
         for _, columns in which:
@@ -1180,25 +1247,41 @@
     best, total = carry
     top = jnp.max(best, axis=0, keepdims=True)
     total = total * jnp.exp2((best - top) * (1.0 / ln2))
-    out_ref[0:1, :] = top
-    out_ref[1:2, :] = jnp.sum(total, axis=0, keepdims=True)
-
-
-def totals(hidden, weights, genes):
+    shared = Shared(box, sems, chunk)
+    shared.send(top, jnp.sum(total, axis=0, keepdims=True))
+
+    @pl.when(pl.program_id(0) == pl.num_programs(0) - 1)
+    def _():
+        shared.finish()
+        top = box[0, 0:1, :]
+        for i in range(1, box.shape[0]):
+            top = jnp.maximum(top, box[i, 0:1, :])
+        total = jnp.zeros_like(top)
+        for i in range(box.shape[0]):
+            total = total + box[i, 1:2, :] * jnp.exp(box[i, 0:1, :] - top)
+        inverse = 1.0 / total
+        out_ref[0:1, :] = top
+        out_ref[1:2, :] = sample_ref[sample_ref.shape[0] - 1 :, :] * inverse
+        out_ref[2:3, :] = inverse
+        out_ref[3:4, :] = inverse
+
+
+def totals(hidden, weights, sample, genes):
     width, cells = hidden.shape
     chunk = pick_chunk(cells, 2048)
     groups = split_rows(genes, 26)[1]
     return pl.pallas_call(
         functools.partial(totals_kernel, genes=genes, chunk=chunk),
         grid=(cells // chunk,),
-        in_specs=[column_blocks(width, chunk), whole(weights)],
-        out_specs=column_blocks(2, chunk),
-        out_shape=jax.ShapeDtypeStruct((2, cells), f32),
+        in_specs=[column_blocks(width, chunk), whole(weights), whole(sample)],
+        out_specs=pl.BlockSpec((4, cells), lambda i: (0, 0)),
+        out_shape=jax.ShapeDtypeStruct((4, cells), f32),
         scratch_shapes=[pltpu.VMEM((HOT_DEPTH, chunk), bf16)]
-        + [pltpu.VMEM((ROWS * groups, chunk), f32)] * 2,
-        compiler_params=PARAMS,
+        + [pltpu.VMEM((ROWS * groups, chunk), f32)] * 2
+        + [pltpu.VMEM((lax.axis_size("gene"), 2, cells), f32), pltpu.SemaphoreType.DMA((2,))],
+        compiler_params=talking(2),
         name="totals",
-    )(hidden, weights)
+    )(hidden, weights, sample)
 
 
 def likelihood_kernel(
@@ -1206,6 +1289,9 @@
     hidden_ref,
     rows_ref,
     share_ref,
+    all_rows_ref,
+    sample_ref,
+    valid_ref,
     weight_ref,
     theta_ref,
     log_ref,
@@ -1223,11 +1309,14 @@
     odd_ref,
     even_grad_ref,
     odd_grad_ref,
+    box,
+    sems,
     *,
     genes,
     chunk,
+    genes_all,
 ):
-    full, groups, tail = split_rows(genes)
+    full, groups, tail = split_rows(genes, 12)
     block = ROWS * groups
     blocks = full // groups
     width = hidden_ref.shape[0]
@@ -1236,6 +1325,7 @@
     def _():
         for ref in (grad_weight_ref, grad_bias_ref, grad_theta_ref):
             ref[...] = jnp.zeros_like(ref)
+        greet(Team("gene"))
 
     fill_hidden(long_ref, hidden_ref, rows_ref[0:1, :])
     wide = min(WIDE, chunk)
@@ -1352,28 +1442,42 @@
             carry,
         )
         back(1, rows, ROWS)
-    for j, columns in enumerate(tiles):
-        sums_ref[0:1, columns] = jnp.sum(carry[1][j], axis=0, keepdims=True)
-        sums_ref[1:2, columns] = jnp.sum(carry[0][j], axis=0, keepdims=True) * ln2
-
-
-def likelihood(counts_t, hidden, rows, share, weights, gene_tables):
+    shared = Shared(box, sems, chunk)
+    rows = [
+        jnp.concatenate([jnp.sum(part, axis=0, keepdims=True) for part in carry[i]], axis=1)
+        for i in (1, 0)
+    ]
+    shared.send(rows[0], rows[1] * ln2)
+
+    @pl.when(pl.program_id(0) == pl.num_programs(0) - 1)
+    def _():
+        shared.finish()
+        total = box_sum(box)
+        at = sample_ref.shape[0] - 2
+        sums_ref[0:1, :] = total[0:1] * all_rows_ref[2:3, :]
+        sums_ref[1:2, :] = (
+            valid_ref[...].astype(f32) * (total[1:2] + sample_ref[at : at + 1, :]) / genes_all
+        )
+
+
+def likelihood(counts_t, hidden, rows, share, sample, valid, weights, gene_tables, genes_all):
     genes, cells = counts_t.shape
     size = weights.shape[1]
     width = hidden.shape[0]
     chunk = pick_chunk(cells, 512)
-    groups = split_rows(genes)[1]
+    groups = split_rows(genes, 12)[1]
     row = column_blocks(1, chunk)
     per_gene = pl.BlockSpec((size, LANES), lambda i: (0, 0))
     return pl.pallas_call(
-        functools.partial(likelihood_kernel, genes=genes, chunk=chunk),
+        functools.partial(likelihood_kernel, genes=genes, chunk=chunk, genes_all=genes_all),
         grid=(cells // chunk,),
         in_specs=[column_blocks(genes, chunk), column_blocks(width, chunk)]
-        + [column_blocks(rows.shape[0], chunk), row, whole(weights)]
+        + [column_blocks(rows.shape[0], chunk), row]
+        + [whole(a) for a in (rows, sample, valid, weights)]
         + [whole(a) for a in gene_tables],
         out_specs=[
             column_blocks(size, chunk),
-            column_blocks(2, chunk),
+            pl.BlockSpec((2, cells), lambda i: (0, 0)),
             column_blocks(width, chunk),
         ]
         + [per_gene] * 3,
@@ -1385,10 +1489,11 @@
         + [jax.ShapeDtypeStruct((size, LANES), f32)] * 3,
         scratch_shapes=[pltpu.VMEM((HOT_DEPTH, chunk), bf16)]
         + [pltpu.VMEM((2, ROWS * groups, chunk), f32)] * 2
-        + [pltpu.VMEM((ROWS * groups, chunk), bf16)] * 2,
-        compiler_params=PARAMS,
+        + [pltpu.VMEM((ROWS * groups, chunk), bf16)] * 2
+        + [pltpu.VMEM((lax.axis_size("gene"), 2, cells), f32), pltpu.SemaphoreType.DMA((2,))],
+        compiler_params=talking(3),
         name="likelihood",
-    )(counts_t, hidden, rows, share, weights, *gene_tables)
+    )(counts_t, hidden, rows, share, rows, sample, valid, weights, *gene_tables)
 
 
 def frequency_kernel(
@@ -1514,27 +1619,6 @@
         compiler_params=PARAMS,
         name="frequency",
     )(slopes, hidden, rows, pull, share, other, weights, second, dropout, theta, scale)
-
-
-def input_grad_kernel(grad_ref, weight_ref, input_ref):
-    input_ref[...] = jnp.dot(
-        weight_ref[...].astype(bf16), grad_ref[...], preferred_element_type=f32
-    )
-
-
-def encoder_input_grad(grad, weight):
-    width, cells = grad.shape
-    genes = weight.shape[0]
-    block = 2 * LANES
-    return pl.pallas_call(
-        input_grad_kernel,
-        grid=(pl.cdiv(genes, block),),
-        in_specs=[whole(grad), pl.BlockSpec((block, width), lambda i: (i, 0))],
-        out_specs=pl.BlockSpec((block, cells), lambda i: (i, 0)),
-        out_shape=jax.ShapeDtypeStruct((genes, cells), f32),
-        compiler_params=PARAMS,
-        name="input_grad",
-    )(grad, weight)
 
 
 def local(
@@ -1590,14 +1674,13 @@
     index, valid, noise = batch_index[None, :], valid_mask[None, :], noise_draw.T
 
     encoded, weights, *gene_tables = encode(counts_t, encoder_weight, output_rows, gene_vectors)
-    hidden2, centered2, sample, share, stats, centered1, heads, rest_rows, pack = middle(
+    hidden2, centered2, sample, share, stats, centered1, heads, pack = middle(
         encoded, index, valid, noise, small_weights, batches, pad, genes_all
     )
-    rows = combine_tops(totals(hidden2, weights, genes), rest_rows)
-    slopes, sums, grad_hidden2, grad_out1, grad_bias1, grad_theta = likelihood(
-        counts_t, hidden2, rows, share, weights, gene_tables
+    rows = totals(hidden2, weights, sample, genes)
+    slopes, pull, grad_hidden2, grad_out1, grad_bias1, grad_theta = likelihood(
+        counts_t, hidden2, rows, share, sample, valid, weights, gene_tables, genes_all
     )
-    pull = combine_sums(sums, rows, rest_rows, valid, genes_all)
     cell_loss = pull[1]
 
     grad_hidden2, grad_out, grad_genes = frequency(
@@ -1629,55 +1712,58 @@
         grad_genes,
         batches,
     )
-    grad_encoder, small = encoder_grad(counts_t, grad_pre16, small)
-    input_grad = encoder_input_grad(grad_pre16, encoder_weight)
-    depth = pad + batches
-    grad_mixing = jnp.concatenate([small[:latent], small[pad:depth]], axis=0)
-    grad_heads = small[depth : depth + 2 * pad].reshape(2, pad, -1)[:, :latent]
-    grad_heads = grad_heads.reshape(2 * latent, -1).T
-    grad_head_bias = jnp.sum(small[depth + 2 * pad : depth + 4 * pad], axis=1)
-    grad_head_bias = grad_head_bias.reshape(2, pad)[:, :latent].reshape(-1)
-    grad_shift = small[depth + 4 * pad :]
-
-    updated = update(
-        (encoder_weight, encoder_weight_momentum, encoder_weight_average),
+    grad_encoder, small, grad_out = encoder_grad(counts_t, grad_pre16, small, grad_out)
+    states = [
+        (encoder, by_gene(output), vectors, shift, norms, head.T, bias[None, :], mixing)
+        for encoder, output, vectors, shift, norms, head, bias, mixing in (
+            (
+                encoder_weight,
+                output_weight,
+                gene_vectors,
+                batch_shift,
+                layer_norm_params,
+                head_weight,
+                head_bias,
+                decoder_input,
+            ),
+            (
+                encoder_weight_momentum,
+                output_weight_momentum,
+                gene_vectors_momentum,
+                batch_shift_momentum,
+                norm_params_momentum,
+                head_weight_momentum,
+                head_bias_momentum,
+                decoder_input_momentum,
+            ),
+            (
+                encoder_weight_average,
+                output_weight_average,
+                gene_vectors_average,
+                batch_shift_average,
+                norm_params_average,
+                head_weight_average,
+                head_bias_average,
+                decoder_input_average,
+            ),
+        )
+    ]
+    input_grad, fresh = finish(
+        grad_pre16,
         grad_encoder,
-        (output_rows, by_gene(output_weight_momentum), by_gene(output_weight_average)),
         grad_out,
-    )
-    encoder_new = updated[:3]
-    output_new = [jnp.transpose(a.reshape(genes, 2, -1), (1, 2, 0)) for a in updated[3:]]
-    vectors = (gene_vectors, batch_shift, layer_norm_params, head_weight, head_bias, decoder_input)
-    momenta = (
-        gene_vectors_momentum,
-        batch_shift_momentum,
-        norm_params_momentum,
-        head_weight_momentum,
-        head_bias_momentum,
-        decoder_input_momentum,
-    )
-    averages = (
-        gene_vectors_average,
-        batch_shift_average,
-        norm_params_average,
-        head_weight_average,
-        head_bias_average,
-        decoder_input_average,
-    )
-    grads = (
-        grad_genes[:3, :genes],
-        grad_shift,
-        norm_rows[:4],
-        grad_heads,
-        grad_head_bias,
-        grad_mixing,
-    )
-    small_new = zip(
-        *[nesterov(*group) for group in zip(vectors, momenta, averages, grads, step_rates[2:])]
+        grad_genes,
+        small,
+        norm_rows,
+        states,
+        pad,
+        latent,
+        batches,
     )
     results = []
-    for i, rest in enumerate(small_new):
-        results += [encoder_new[i], output_new[i], *rest]
+    for encoder, output, vectors, shift, norms, head, bias, mixing in fresh:
+        output = jnp.transpose(output.reshape(genes, 2, -1), (1, 2, 0))
+        results += [encoder, output, vectors, shift, norms, head.T, bias[0], mixing]
     return (cell_loss, input_grad.T, *results)
 
 

time: 397 us -> 369 us (0.929)
  Pallas kernels: 387 us -> 367 us
  other arithmetic: 6 us -> 0 us
    pallas_call x4 -> x1, Pallas kernels: 52.8 us -> 24.5 us  [finish(): pl.pallas_call(functools.partial(finish_kernel, pad=pad, latent=latent, b...]
    pallas_call x1, Pallas kernels: 13.9 us -> 20.8 us  [totals(): pl.pallas_call(functools.partial(totals_kernel, genes=genes, chunk=chunk)...]
    pallas_call x1, Pallas kernels: 122 us -> 128 us  [likelihood(): pl.pallas_call(functools.partial(likelihood_kernel, genes=genes, chunk=ch...]
    add x5 -> x0, other arithmetic: 4.5 us -> none  [nesterov(): average_decay * average + (1.0 - average_decay) * fresh]
where the time goes in v5:
time: 369 us
  Pallas kernels  367 us (99%)
    pallas_call x1, Pallas kernels, likelihood(): pl.pallas_call(functools.partial(likelihood_kernel, genes=genes, chunk=ch...  128 us
    pallas_call x1, Pallas kernels, middle_back(): pl.pallas_call(functools.partial(middle_back_kernel, batches=batches, lat...  52.8 us
    pallas_call x1, Pallas kernels, encode(): pl.pallas_call(functools.partial(encode_kernel, genes=genes, table_blocks...  43.8 us
    pallas_call x1, Pallas kernels, frequency(): pl.pallas_call(functools.partial(frequency_kernel, genes=genes, chunk=chu...  36.4 us
    pallas_call x1, Pallas kernels, encoder_grad(): pl.pallas_call(encoder_grad_kernel, grid=(4,), in_specs=[pl.BlockSpec((qu...  32.8 us
    pallas_call x1, Pallas kernels, middle(): pl.pallas_call(functools.partial(middle_kernel, batches=batches, latent=n...  28.1 us
    pallas_call x1, Pallas kernels, finish(): pl.pallas_call(functools.partial(finish_kernel, pad=pad, latent=latent, b...  24.5 us
    pallas_call x1, Pallas kernels, totals(): pl.pallas_call(functools.partial(totals_kernel, genes=genes, chunk=chunk)...  20.8 us

profile of v5, /device:TPU:0, one launch (start us, length us, event | category | flops | bytes accessed | tf_op | source)
XLA Modules:
  0.0 368.7 jit_solution(1076237222296810629)
XLA Ops:
  0.7 43.8 %encode.1 = (f32[136,512]{1,0:T(8,128)}, bf16[2,2528,256]{2,1,0:T(8,128)(2,1)}, f32[2528,128]{1,0:T(8,128)}, f32[2528,128]{1,0:T(8,128)}, f32[2528,128]{1,0:T(8,...) custom-call(s32[2500,4096]{1,0:T(8,128)} %bitcast.36, f32[2500,128]{1,0:T(8,128)} %refs_6_.1, f32[5000,128]{1,0:T(8,128)} %bitcast.39, ...), custom_call_target="tpu_custom_call" | custom-call | tf_op jit(solution)/shard_map/encode/pallas_call | solution.py:477
  44.4 28.1 %middle.1 = (bf16[128,4096]{1,0:T(8,128)(2,1)}, f32[128,4096]{1,0:T(8,128)}, f32[16,4096]{1,0:T(8,128)}, f32[1,4096]{1,0:T(1,128)}, f32[8,128]{1,0:T(8,128)}, /*...) custom-call(f32[136,512]{1,0:T(8,128)} %get-tuple-element.83.encoded_ref, s32[1,4096]{1,0:T(1,128)} %bitcast.48, ...), custom_call_target="tpu_custom_call" | custom-call | tf_op jit(solution)/shard_map/middle/pallas_call | solution.py:637
  72.6 20.8 %totals.1.rows_ref.all_rows_ref = f32[4,4096]{1,0:T(4,128)} custom-call(bf16[128,4096]{1,0:T(8,128)(2,1)} %get-tuple-element.84.hidden_ref, bf16[2,2528,256]{2,1,0:T(8,128)(2,1)} %get-tuple-element.85.weight_ref, f32[16,4096]{1,0:T(8,128)} %get-tuple-element.86.sample_ref), custom_call_target="tpu_custom_call" | custom-call | tf_op jit(solution)/shard_map/totals/pallas_call | solution.py:1273
  93.4 128.0 %likelihood.1 = (f32[2528,4096]{1,0:T(8,128)}, f32[2,4096]{1,0:T(2,128)}, f32[128,4096]{1,0:T(8,128)}, f32[2528,128]{1,0:T(8,128)}, f32[2528,128]{1,0:T(8,128)}, /*index=5*/f32[2528,128]{1,0:T(8,128)}) custom-call(s32[2500,4096]{1,0:T(8,128)} %bitcast.37, bf16[128,4096]{1,0:T(8,128)(2,1)} %get-tuple-element.84.hidden_ref, ...), custom_call_target="tpu_custom_call" | custom-call | tf_op jit(solution)/shard_map/likelihood/pallas_call | solution.py:1471
  221.4 0.0 copy-start
  221.4 36.4 %frequency.1 = (f32[128,4096]{1,0:T(8,128)}, f32[2,2528,128]{2,1,0:T(8,128)}, f32[4,2528]{1,0:T(4,128)}) custom-call(f32[2528,4096]{1,0:T(8,128)} %get-tuple-element.94.slopes_ref, bf16[128,4096]{1,0:T(8,128)(2,1)} %get-tuple-element.84.hidden_ref, f32[4,4096]{1,0:T(4,128)} %totals.1.rows_ref.all_rows_ref, f32[2,4096]{1,0:T(2,128)} %get-tuple-element.93.pull_ref, ...), custom_call_target="tpu_custom_call" | custom-call | tf_op jit(solution)/shard_map/frequency/pallas_call | solution.py:1599
  257.8 0.0 copy-done
  257.9 0.6 slice.3
  258.5 52.8 %middle_back.1 = (bf16[128,4096]{1,0:T(8,128)(2,1)}, f32[144,128]{1,0:T(8,128)}, f32[8,128]{1,0:T(8,128)}, f32[2528,128]{1,0:T(8,128)}, f32[4,2528]{1,0:T(4,128)}) custom-call(f32[128,4096]{1,0:T(8,128)} %get-tuple-element.99.grad_ref, f32[128,4096]{1,0:T(8,128)} %get-tuple-element.100.centered_ref, f32[16,4096]{1,0:T(8,128)} %get-tuple-element.86.sample_ref, ...), custom_call_target="tpu_custom_call" | custom-call | tf_op jit(solution)/shard_map/middle_back/pallas_call | solution.py:860
  311.2 32.8 %encoder_grad.1 = (f32[2560,128]{1,0:T(8,128)}, f32[144,128]{1,0:T(8,128)}, f32[2,2528,128]{2,1,0:T(8,128)}) custom-call(s32[2500,4096]{1,0:T(8,128)} %bitcast.38, bf16[128,4096]{1,0:T(8,128)(2,1)} %get-tuple-element.107.grad_ref.refs_0_, f32[144,128]{1,0:T(8,128)} %get-tuple-element.108.small_ref, f32[2528,128]{1,0:T(8,128)} %get-tuple-element.109.output_ref), custom_call_target="tpu_custom_call" | custom-call | tf_op jit(solution)/shard_map/encoder_grad/pallas_call | solution.py:1054
  344.0 24.5 %finish.1 = (f32[2500,4096]{1,0:T(8,128)}, f32[2500,128]{1,0:T(8,128)}, f32[5000,128]{1,0:T(8,128)}, f32[3,2500]{1,0:T(4,128)}, f32[32,128]{1,0:T(8,128)}, /*ind...) custom-call(bf16[128,4096]{1,0:T(8,128)(2,1)} %get-tuple-element.107, ...), custom_call_target="tpu_custom_call" | custom-call | tf_op jit(solution)/shard_map/finish/pallas_call | solution.py:1141
Async XLA Ops:
  221.4 36.5 %copy-start = (f32[2,4096]{1,0:T(2,128)S(1)}, f32[2,4096]{1,0:T(2,128)}, u32[]{:S(2)}) copy-start(f32[2,4096]{1,0:T(2,128)} %get-tuple-element.93.pull_ref) | copy-start | bytes 98308

commit v6 on v5

--- a/solution.py
+++ b/solution.py
@@ -106,7 +106,7 @@
 
     for team in teams:
         team.others(act)
-    pl.semaphore_wait(barrier, sum(team.size - 1 for team in teams))
+    return lambda: pl.semaphore_wait(barrier, sum(team.size - 1 for team in teams))
 
 
 def await_bytes(ref, sem):
@@ -377,7 +377,6 @@
                 filler = jnp.zeros((at + LANES - stop, width), f32)
                 piece = jnp.concatenate([piece, filler], axis=0)
             weight_ref[:, at : at + LANES] = jnp.transpose(piece).astype(bf16)
-        pl.semaphore_wait(barrier, pairs)
 
     def part(ref):
         depth = 3 * LANES
@@ -419,6 +418,11 @@
     @pl.when(given == 1)
     def _():
         part(near_give.at[turn])
+
+        @pl.when(step == 0)
+        def _():
+            pl.semaphore_wait(pltpu.get_barrier_semaphore(), pairs)
+
         near_copy(turn).start()
 
     @pl.when(given == 0)
@@ -563,7 +567,7 @@
         return pl.ds(pl.multiple_of(other * slab, LANES), slab)
 
     mine = part(group.me)
-    greet(group, team)
+    greet(group, team)()
     hot = hot_rows(index_ref[:, mine], batches)
     valid = valid_ref[:, mine].astype(f32)
     shift = exact(pack_ref[shift_rows, :], hot, 0, 0)
@@ -726,7 +730,7 @@
         return pl.ds(pl.multiple_of(other * slab, LANES), slab)
 
     mine = part(group.me)
-    greet(group, team)
+    greet(group, team)()
     swap1 = swap(output_ref.at[1 - bit], output_box, near, 0)
     genes_box[cell] = genes_ref[...]
 
@@ -970,9 +974,6 @@
         barrier = pltpu.get_barrier_semaphore()
         for where in rounds:
             pl.semaphore_signal(barrier, inc=1, device_id=where, device_id_type=MESH)
-        pl.semaphore_wait(barrier, len(rounds))
-        small_copy(0).start()
-        output_copy.start()
 
     piece = pick_chunk(cells, 512)
 
@@ -990,6 +991,12 @@
         return total
 
     value = part()
+
+    @pl.when(step == 0)
+    def _():
+        pl.semaphore_wait(pltpu.get_barrier_semaphore(), len(rounds))
+        small_copy(0).start()
+        output_copy.start()
 
     @pl.when(step < 2)
     def _():
@@ -1128,7 +1135,7 @@
 def finish(grad16, encoder_grad, output_grad, genes_grad, small, norms, states, pad, latent, batches):
     width, cells = grad16.shape
     genes = states[0][0].shape[0]
-    block = 2 * LANES
+    block = 4 * LANES
     one = pl.BlockSpec((block, LANES), lambda i: (i, 0))
     two = pl.BlockSpec((2 * block, LANES), lambda i: (i, 0))
     both = pl.BlockSpec((2, block, LANES), lambda i: (0, i, 0))
@@ -1248,6 +1255,11 @@
     top = jnp.max(best, axis=0, keepdims=True)
     total = total * jnp.exp2((best - top) * (1.0 / ln2))
     shared = Shared(box, sems, chunk)
+
+    @pl.when(pl.program_id(0) == 0)
+    def _():
+        pl.semaphore_wait(pltpu.get_barrier_semaphore(), box.shape[0] - 1)
+
     shared.send(top, jnp.sum(total, axis=0, keepdims=True))
 
     @pl.when(pl.program_id(0) == pl.num_programs(0) - 1)
@@ -1268,7 +1280,7 @@
 
 def totals(hidden, weights, sample, genes):
     width, cells = hidden.shape
-    chunk = pick_chunk(cells, 2048)
+    chunk = pick_chunk(cells, 4096)
     groups = split_rows(genes, 26)[1]
     return pl.pallas_call(
         functools.partial(totals_kernel, genes=genes, chunk=chunk),
@@ -1443,6 +1455,11 @@
         )
         back(1, rows, ROWS)
     shared = Shared(box, sems, chunk)
+
+    @pl.when(pl.program_id(0) == 0)
+    def _():
+        pl.semaphore_wait(pltpu.get_barrier_semaphore(), box.shape[0] - 1)
+
     rows = [
         jnp.concatenate([jnp.sum(part, axis=0, keepdims=True) for part in carry[i]], axis=1)
         for i in (1, 0)
@@ -1582,10 +1599,17 @@
 
     @pl.when(pl.program_id(0) == pl.num_programs(0) - 1)
     def _():
-        ones = jnp.ones((8, LANES), f32)
+        ones = jnp.ones((ROWS, LANES), bf16)
         parts = (grad_bias_ref[...], dropout_ref[...], theta_ref[...] * scale_ref[...])
         for i, values in enumerate(parts):
-            genes_ref[i : i + 1, :] = exact(ones, values, 1, 1)[0:1]
+            total = jnp.zeros((1, size), f32)
+            for _ in range(3):
+                piece = values.astype(bf16)
+                values = values - piece.astype(f32)
+                total = total + lax.dot_general(
+                    ones, piece, (((1,), (1,)), ((), ())), preferred_element_type=f32
+                )[0:1]
+            genes_ref[i : i + 1, :] = total
         genes_ref[3:4, :] = jnp.zeros((1, size), f32)
 
 

time: 369 us -> 361 us (0.978)
  Pallas kernels: 367 us -> 359 us
where the time goes in v6:
time: 361 us
  Pallas kernels  359 us (99%)
    pallas_call x1, Pallas kernels, likelihood(): pl.pallas_call(functools.partial(likelihood_kernel, genes=genes, chunk=ch...  128 us
    pallas_call x1, Pallas kernels, middle_back(): pl.pallas_call(functools.partial(middle_back_kernel, batches=batches, lat...  52 us
    pallas_call x1, Pallas kernels, encode(): pl.pallas_call(functools.partial(encode_kernel, genes=genes, table_blocks...  42 us
    pallas_call x1, Pallas kernels, frequency(): pl.pallas_call(functools.partial(frequency_kernel, genes=genes, chunk=chu...  34.6 us
    pallas_call x1, Pallas kernels, encoder_grad(): pl.pallas_call(encoder_grad_kernel, grid=(4,), in_specs=[pl.BlockSpec((qu...  31.6 us
    pallas_call x1, Pallas kernels, middle(): pl.pallas_call(functools.partial(middle_kernel, batches=batches, latent=n...  28.5 us
    pallas_call x1, Pallas kernels, finish(): pl.pallas_call(functools.partial(finish_kernel, pad=pad, latent=latent, b...  24.4 us
    pallas_call x1, Pallas kernels, totals(): pl.pallas_call(functools.partial(totals_kernel, genes=genes, chunk=chunk)...  18.2 us

profile of v6, /device:TPU:0, one launch (start us, length us, event | category | flops | bytes accessed | tf_op | source)
XLA Modules:
  0.0 360.5 jit_solution(11271007573106722277)
XLA Ops:
  0.7 42.0 %encode.1 = (f32[136,512]{1,0:T(8,128)}, bf16[2,2528,256]{2,1,0:T(8,128)(2,1)}, f32[2528,128]{1,0:T(8,128)}, f32[2528,128]{1,0:T(8,128)}, f32[2528,128]{1,0:T(8,...) custom-call(s32[2500,4096]{1,0:T(8,128)} %bitcast.36, f32[2500,128]{1,0:T(8,128)} %refs_6_.1, f32[5000,128]{1,0:T(8,128)} %bitcast.39, ...), custom_call_target="tpu_custom_call" | custom-call | tf_op jit(solution)/shard_map/encode/pallas_call | solution.py:481
  42.7 28.5 %middle.1 = (bf16[128,4096]{1,0:T(8,128)(2,1)}, f32[128,4096]{1,0:T(8,128)}, f32[16,4096]{1,0:T(8,128)}, f32[1,4096]{1,0:T(1,128)}, f32[8,128]{1,0:T(8,128)}, /*...) custom-call(f32[136,512]{1,0:T(8,128)} %get-tuple-element.83.encoded_ref, s32[1,4096]{1,0:T(1,128)} %bitcast.48, ...), custom_call_target="tpu_custom_call" | custom-call | tf_op jit(solution)/shard_map/middle/pallas_call | solution.py:641
  71.1 18.2 %totals.1.rows_ref.all_rows_ref = f32[4,4096]{1,0:T(4,128)} custom-call(bf16[128,4096]{1,0:T(8,128)(2,1)} %get-tuple-element.84.hidden_ref, bf16[2,2528,256]{2,1,0:T(8,128)(2,1)} %get-tuple-element.85.weight_ref, f32[16,4096]{1,0:T(8,128)} %get-tuple-element.86.sample_ref), custom_call_target="tpu_custom_call" | custom-call | tf_op jit(solution)/shard_map/totals/pallas_call | solution.py:1285
  89.3 127.7 %likelihood.1 = (f32[2528,4096]{1,0:T(8,128)}, f32[2,4096]{1,0:T(2,128)}, f32[128,4096]{1,0:T(8,128)}, f32[2528,128]{1,0:T(8,128)}, f32[2528,128]{1,0:T(8,128)}, /*index=5*/f32[2528,128]{1,0:T(8,128)}) custom-call(s32[2500,4096]{1,0:T(8,128)} %bitcast.37, bf16[128,4096]{1,0:T(8,128)(2,1)} %get-tuple-element.84.hidden_ref, ...), custom_call_target="tpu_custom_call" | custom-call | tf_op jit(solution)/shard_map/likelihood/pallas_call | solution.py:1488
  217.0 0.0 copy-start
  217.0 34.6 %frequency.1 = (f32[128,4096]{1,0:T(8,128)}, f32[2,2528,128]{2,1,0:T(8,128)}, f32[4,2528]{1,0:T(4,128)}) custom-call(f32[2528,4096]{1,0:T(8,128)} %get-tuple-element.94.slopes_ref, bf16[128,4096]{1,0:T(8,128)(2,1)} %get-tuple-element.84.hidden_ref, f32[4,4096]{1,0:T(4,128)} %totals.1.rows_ref.all_rows_ref, f32[2,4096]{1,0:T(2,128)} %get-tuple-element.93.pull_ref, ...), custom_call_target="tpu_custom_call" | custom-call | tf_op jit(solution)/shard_map/frequency/pallas_call | solution.py:1623
  251.7 0.0 copy-done
  251.7 0.6 slice.3
  252.3 52.0 %middle_back.1 = (bf16[128,4096]{1,0:T(8,128)(2,1)}, f32[144,128]{1,0:T(8,128)}, f32[8,128]{1,0:T(8,128)}, f32[2528,128]{1,0:T(8,128)}, f32[4,2528]{1,0:T(4,128)}) custom-call(f32[128,4096]{1,0:T(8,128)} %get-tuple-element.99.grad_ref, f32[128,4096]{1,0:T(8,128)} %get-tuple-element.100.centered_ref, f32[16,4096]{1,0:T(8,128)} %get-tuple-element.86.sample_ref, ...), custom_call_target="tpu_custom_call" | custom-call | tf_op jit(solution)/shard_map/middle_back/pallas_call | solution.py:864
  304.4 31.6 %encoder_grad.1 = (f32[2560,128]{1,0:T(8,128)}, f32[144,128]{1,0:T(8,128)}, f32[2,2528,128]{2,1,0:T(8,128)}) custom-call(s32[2500,4096]{1,0:T(8,128)} %bitcast.38, bf16[128,4096]{1,0:T(8,128)(2,1)} %get-tuple-element.107.grad_ref.refs_0_, f32[144,128]{1,0:T(8,128)} %get-tuple-element.108.small_ref, f32[2528,128]{1,0:T(8,128)} %get-tuple-element.109.output_ref), custom_call_target="tpu_custom_call" | custom-call | tf_op jit(solution)/shard_map/encoder_grad/pallas_call | solution.py:1061
  335.9 24.4 %finish.1 = (f32[2500,4096]{1,0:T(8,128)}, f32[2500,128]{1,0:T(8,128)}, f32[5000,128]{1,0:T(8,128)}, f32[3,2500]{1,0:T(4,128)}, f32[32,128]{1,0:T(8,128)}, /*ind...) custom-call(bf16[128,4096]{1,0:T(8,128)(2,1)} %get-tuple-element.107, ...), custom_call_target="tpu_custom_call" | custom-call | tf_op jit(solution)/shard_map/finish/pallas_call | solution.py:1148
Async XLA Ops:
  217.0 34.6 %copy-start = (f32[2,4096]{1,0:T(2,128)S(1)}, f32[2,4096]{1,0:T(2,128)}, u32[]{:S(2)}) copy-start(f32[2,4096]{1,0:T(2,128)} %get-tuple-element.93.pull_ref) | copy-start | bytes 98308

commit v7 on v6

--- a/solution.py
+++ b/solution.py
@@ -567,7 +567,7 @@
         return pl.ds(pl.multiple_of(other * slab, LANES), slab)
 
     mine = part(group.me)
-    greet(group, team)()
+    entered = greet(group, team)
     hot = hot_rows(index_ref[:, mine], batches)
     valid = valid_ref[:, mine].astype(f32)
     shift = exact(pack_ref[shift_rows, :], hot, 0, 0)
@@ -582,6 +582,7 @@
         row_sums(fold_lanes(weighed * pre1)),
         jnp.broadcast_to(jnp.sum(valid, axis=1, keepdims=True), (1, LANES)),
     ]
+    entered()
     sums = spread_box(team, box1, eight_rows(rows), sems1)()
     sums = spread_box(group, box2, sums, sems2)()
     count = jnp.maximum(sums[2:3], 1.0)

time: 361 us -> 360 us (level)
  no operation moved by 1% of the time
where the time goes in v7:
time: 360 us
  Pallas kernels  359 us (100%)
    pallas_call x1, Pallas kernels, likelihood(): pl.pallas_call(functools.partial(likelihood_kernel, genes=genes, chunk=ch...  128 us
    pallas_call x1, Pallas kernels, middle_back(): pl.pallas_call(functools.partial(middle_back_kernel, batches=batches, lat...  52 us
    pallas_call x1, Pallas kernels, encode(): pl.pallas_call(functools.partial(encode_kernel, genes=genes, table_blocks...  42 us
    pallas_call x1, Pallas kernels, frequency(): pl.pallas_call(functools.partial(frequency_kernel, genes=genes, chunk=chu...  34.6 us
    pallas_call x1, Pallas kernels, encoder_grad(): pl.pallas_call(encoder_grad_kernel, grid=(4,), in_specs=[pl.BlockSpec((qu...  31.6 us
    pallas_call x1, Pallas kernels, middle(): pl.pallas_call(functools.partial(middle_kernel, batches=batches, latent=n...  28 us
    pallas_call x1, Pallas kernels, finish(): pl.pallas_call(functools.partial(finish_kernel, pad=pad, latent=latent, b...  24.4 us
    pallas_call x1, Pallas kernels, totals(): pl.pallas_call(functools.partial(totals_kernel, genes=genes, chunk=chunk)...  18.2 us

profile of v7, /device:TPU:0, one launch (start us, length us, event | category | flops | bytes accessed | tf_op | source)
XLA Modules:
  0.0 360.1 jit_solution(1293372048366502055)
XLA Ops:
  0.7 42.0 %encode.1 = (f32[136,512]{1,0:T(8,128)}, bf16[2,2528,256]{2,1,0:T(8,128)(2,1)}, f32[2528,128]{1,0:T(8,128)}, f32[2528,128]{1,0:T(8,128)}, f32[2528,128]{1,0:T(8,...) custom-call(s32[2500,4096]{1,0:T(8,128)} %bitcast.36, f32[2500,128]{1,0:T(8,128)} %refs_6_.1, f32[5000,128]{1,0:T(8,128)} %bitcast.39, ...), custom_call_target="tpu_custom_call" | custom-call | tf_op jit(solution)/shard_map/encode/pallas_call | solution.py:481
  42.7 28.0 %middle.1 = (bf16[128,4096]{1,0:T(8,128)(2,1)}, f32[128,4096]{1,0:T(8,128)}, f32[16,4096]{1,0:T(8,128)}, f32[1,4096]{1,0:T(1,128)}, f32[8,128]{1,0:T(8,128)}, /*...) custom-call(f32[136,512]{1,0:T(8,128)} %get-tuple-element.83.encoded_ref, s32[1,4096]{1,0:T(1,128)} %bitcast.48, ...), custom_call_target="tpu_custom_call" | custom-call | tf_op jit(solution)/shard_map/middle/pallas_call | solution.py:642
  70.6 18.2 %totals.1.rows_ref.all_rows_ref = f32[4,4096]{1,0:T(4,128)} custom-call(bf16[128,4096]{1,0:T(8,128)(2,1)} %get-tuple-element.84.hidden_ref, bf16[2,2528,256]{2,1,0:T(8,128)(2,1)} %get-tuple-element.85.weight_ref, f32[16,4096]{1,0:T(8,128)} %get-tuple-element.86.sample_ref), custom_call_target="tpu_custom_call" | custom-call | tf_op jit(solution)/shard_map/totals/pallas_call | solution.py:1286
  88.8 127.7 %likelihood.1 = (f32[2528,4096]{1,0:T(8,128)}, f32[2,4096]{1,0:T(2,128)}, f32[128,4096]{1,0:T(8,128)}, f32[2528,128]{1,0:T(8,128)}, f32[2528,128]{1,0:T(8,128)}, /*index=5*/f32[2528,128]{1,0:T(8,128)}) custom-call(s32[2500,4096]{1,0:T(8,128)} %bitcast.37, bf16[128,4096]{1,0:T(8,128)(2,1)} %get-tuple-element.84.hidden_ref, ...), custom_call_target="tpu_custom_call" | custom-call | tf_op jit(solution)/shard_map/likelihood/pallas_call | solution.py:1489
  216.5 0.0 copy-start
  216.5 34.6 %frequency.1 = (f32[128,4096]{1,0:T(8,128)}, f32[2,2528,128]{2,1,0:T(8,128)}, f32[4,2528]{1,0:T(4,128)}) custom-call(f32[2528,4096]{1,0:T(8,128)} %get-tuple-element.94.slopes_ref, bf16[128,4096]{1,0:T(8,128)(2,1)} %get-tuple-element.84.hidden_ref, f32[4,4096]{1,0:T(4,128)} %totals.1.rows_ref.all_rows_ref, f32[2,4096]{1,0:T(2,128)} %get-tuple-element.93.pull_ref, ...), custom_call_target="tpu_custom_call" | custom-call | tf_op jit(solution)/shard_map/frequency/pallas_call | solution.py:1624
  251.2 0.0 copy-done
  251.2 0.6 slice.3
  251.8 52.0 %middle_back.1 = (bf16[128,4096]{1,0:T(8,128)(2,1)}, f32[144,128]{1,0:T(8,128)}, f32[8,128]{1,0:T(8,128)}, f32[2528,128]{1,0:T(8,128)}, f32[4,2528]{1,0:T(4,128)}) custom-call(f32[128,4096]{1,0:T(8,128)} %get-tuple-element.99.grad_ref, f32[128,4096]{1,0:T(8,128)} %get-tuple-element.100.centered_ref, f32[16,4096]{1,0:T(8,128)} %get-tuple-element.86.sample_ref, ...), custom_call_target="tpu_custom_call" | custom-call | tf_op jit(solution)/shard_map/middle_back/pallas_call | solution.py:865
  303.8 31.6 %encoder_grad.1 = (f32[2560,128]{1,0:T(8,128)}, f32[144,128]{1,0:T(8,128)}, f32[2,2528,128]{2,1,0:T(8,128)}) custom-call(s32[2500,4096]{1,0:T(8,128)} %bitcast.38, bf16[128,4096]{1,0:T(8,128)(2,1)} %get-tuple-element.107.grad_ref.refs_0_, f32[144,128]{1,0:T(8,128)} %get-tuple-element.108.small_ref, f32[2528,128]{1,0:T(8,128)} %get-tuple-element.109.output_ref), custom_call_target="tpu_custom_call" | custom-call | tf_op jit(solution)/shard_map/encoder_grad/pallas_call | solution.py:1062
  335.4 24.4 %finish.1 = (f32[2500,4096]{1,0:T(8,128)}, f32[2500,128]{1,0:T(8,128)}, f32[5000,128]{1,0:T(8,128)}, f32[3,2500]{1,0:T(4,128)}, f32[32,128]{1,0:T(8,128)}, /*ind...) custom-call(bf16[128,4096]{1,0:T(8,128)(2,1)} %get-tuple-element.107, ...), custom_call_target="tpu_custom_call" | custom-call | tf_op jit(solution)/shard_map/finish/pallas_call | solution.py:1149
Async XLA Ops:
  216.5 34.6 %copy-start = (f32[2,4096]{1,0:T(2,128)S(1)}, f32[2,4096]{1,0:T(2,128)}, u32[]{:S(2)}) copy-start(f32[2,4096]{1,0:T(2,128)} %get-tuple-element.93.pull_ref) | copy-start | bytes 98308
